TPU v7x, 32 devices: a whole 2x2x4 slice. The times are simulated.
32 devices in a mesh: dp: 4 (over x, core), ctx: 8 (over z, y).
Axes of the slice: x: 2, y: 2, z: 4, core: 2. Of those that a mesh axis runs over, the one named last changes fastest.
Arguments:
- residual: bfloat16 [512, 4, 1024], P('ctx', 'dp'), may hold values from -10 to 10
- projections: bfloat16 [512, 4, 3072], P('ctx', 'dp'), may hold values from -8 to 8
- out_weight: bfloat16 [1024, 1024], replicated, may hold values from -0.1875 to 0.1875
- gain_one: float32 [1024], replicated, may hold values from 0.1 to 1.9
- up_weight: bfloat16 [1024, 2048], replicated, may hold values from -0.1875 to 0.1875
- conv_kernel: float32 [31, 1024], replicated, may hold values from -1 to 1
- gain_two: float32 [1024], replicated, may hold values from 0.1 to 1.9
- down_weight: bfloat16 [1024, 1024], replicated, may hold values from -0.1875 to 0.1875
- lengths: int32 [4], P('dp'), may hold values from 128 to 512, as said below
- out_grad: bfloat16 [512, 4, 1024], P('ctx', 'dp'), may hold values from -0.13183594 to 0.13183594
Outputs:
- block_out: bfloat16 [512, 4, 1024], P('ctx', 'dp')
- up_grad: float32 [2048, 1024], P(('dp', 'ctx'))
- down_grad: float32 [1024, 1024], P(('dp', 'ctx'))
- kernel_grad: float32 [1024, 31], P(('dp', 'ctx'))
- gain_one_grad: float32 [1024], P(('dp', 'ctx'))
- gain_two_grad: float32 [1024], P(('dp', 'ctx'))
Inputs may be any that keep to these rules, and one draw needn't show every extreme that they name: `lengths`: utterance 0 has all 512 frames valid.
All inputs are finite; a program needn't handle non-finite values.
Results may differ from a plain program's by a relative error of at most 0.02.
Values may be sent and summed in bfloat16 or wider, within the bound.
No kernel may reach another device: no remote copies, remote signals or barrier semaphores. Data moves between devices by JAX's collectives and lax.ppermute only.
A program may use at most 128 MiB of HBM per device.

v0:
```python
import math

import jax
import jax.numpy as jnp
from jax import lax
from jax.sharding import PartitionSpec as P

HEADS = 16


EPSILON = 1e-05


def extended(x, sides, width):
    for axis, dim in sides:
        size, length = (lax.axis_size(axis), x.shape[dim])
        up = [(i, (i + 1) % size) for i in range(size - 1)]
        down = [(j, i) for i, j in up]
        last = lax.slice_in_dim(x, length - width, length, axis=dim)
        leading = lax.slice_in_dim(x, 0, width, axis=dim)
        before = lax.ppermute(last, axis, up)
        after = lax.ppermute(leading, axis, down)
        x = jnp.concatenate([before, x, after], axis=dim)
    return x


def normalize(values):
    center = values - jnp.mean(values, axis=-1, keepdims=True)
    inverse = lax.rsqrt(jnp.mean(center * center, axis=-1, keepdims=True) + EPSILON)
    return (center * inverse, inverse)


def attend(pieces):
    packed_four, marks_three = pieces
    length = packed_four.shape[0]
    count = packed_four.shape[2]
    triple = packed_four.shape[3]
    packed = packed_four.reshape(length, count, triple)
    key_marks = marks_three.reshape(length, count)
    head_size = triple // 3
    query_rows = packed[:, :, :head_size]
    key_rows = packed[:, :, head_size : 2 * head_size]
    value_rows = packed[:, :, 2 * head_size :]
    allowed = jnp.transpose(key_marks > 0)
    block_span = math.gcd(length, 512)
    blocks = query_rows.reshape(length // block_span, block_span, count, head_size)
    score_scale = head_size ** (-0.5)

    def one_block(query_block):
        scores = (
            jnp.einsum("qmd,kmd->mqk", query_block, key_rows, preferred_element_type=jnp.float32)
            * score_scale
        )
        scores = jnp.where(allowed[:, None, :], scores, -jnp.inf)
        highest = jnp.max(scores, axis=-1, keepdims=True)
        raised = jnp.exp(scores - highest)
        weights_bf = (raised / jnp.sum(raised, axis=-1, keepdims=True)).astype(jnp.bfloat16)
        return jnp.einsum(
            "mqk,kmd->qmd", weights_bf, value_rows, preferred_element_type=jnp.float32
        ).astype(jnp.bfloat16)

    return lax.map(one_block, blocks).reshape(length, 1, count, head_size)


def on_device(
    residual,
    projections,
    out_weight,
    gain_one,
    up_weight,
    conv_kernel,
    gain_two,
    down_weight,
    lengths,
    out_grad,
):
    frames, utter_count, model_width = residual.shape
    head_count = HEADS
    head_size = model_width // head_count
    kernel_len = conv_kernel.shape[0]
    half_width = (kernel_len - 1) // 2
    row_count = frames * utter_count
    ctx_count = lax.axis_size("ctx")
    per_device = utter_count * head_count // ctx_count
    first_frame = lax.axis_index("ctx") * frames
    positions = first_frame + jnp.arange(frames, dtype=jnp.int32)
    valid = (positions[:, None] < lengths[None, :]).astype(jnp.bfloat16)
    key_marks = jnp.broadcast_to(valid[:, :, None], (frames, utter_count, head_count)).reshape(
        frames, ctx_count, per_device
    )
    packed = projections.reshape(frames, ctx_count, per_device, 3 * head_size)
    by_head = attend(
        (
            lax.all_to_all(packed, "ctx", split_axis=1, concat_axis=0, tiled=True),
            lax.all_to_all(key_marks, "ctx", split_axis=1, concat_axis=0, tiled=True),
        )
    )
    by_frame = lax.all_to_all(by_head, "ctx", split_axis=0, concat_axis=1, tiled=True)
    context = by_frame.reshape(row_count, model_width)
    hidden = residual.reshape(row_count, model_width).astype(jnp.float32) + jnp.dot(
        context, out_weight, preferred_element_type=jnp.float32
    )
    normed_one, inverse_one = normalize(hidden)
    scaled_one = (normed_one * gain_one).astype(jnp.bfloat16)
    lifted = jnp.dot(scaled_one, up_weight, preferred_element_type=jnp.float32)
    linear_part = lifted[:, :model_width]
    gate_part = jax.nn.sigmoid(lifted[:, model_width:])
    row_mask = valid.reshape(row_count, 1).astype(jnp.float32)
    glu_out = (linear_part * gate_part * row_mask).astype(jnp.bfloat16)
    glu_rimmed = extended(
        glu_out.reshape(frames, utter_count, model_width), (("ctx", 0),), half_width
    )
    glu_wide = glu_rimmed.astype(jnp.float32)
    conv_out = jnp.zeros((frames, utter_count, model_width), jnp.float32)
    for offset in range(kernel_len):
        conv_out = conv_out + conv_kernel[offset] * glu_wide[offset : offset + frames]
    normed_two, inverse_two = normalize(conv_out.reshape(row_count, model_width))
    pre_act = normed_two * gain_two
    gate_two = jax.nn.sigmoid(pre_act)
    activated = (pre_act * gate_two).astype(jnp.bfloat16)
    block_out = (
        hidden + jnp.dot(activated, down_weight, preferred_element_type=jnp.float32)
    ).astype(jnp.bfloat16)
    block_out = block_out.reshape(frames, utter_count, model_width)
    cotangent = (out_grad * valid[:, :, None]).reshape(row_count, model_width)
    down_grad = jnp.einsum("ro,ri->oi", cotangent, activated, preferred_element_type=jnp.float32)
    act_grad = lax.dot_general(
        cotangent, down_weight, (((1,), (1,)), ((), ())), preferred_element_type=jnp.float32
    )
    pre_grad = act_grad * gate_two * (1.0 + pre_act * (1.0 - gate_two))
    gain_two_grad = jnp.sum(pre_grad * normed_two, axis=0)
    scaled_grad = pre_grad * gain_two
    conv_grad = inverse_two * (
        scaled_grad
        - jnp.mean(scaled_grad, axis=-1, keepdims=True)
        - normed_two * jnp.mean(scaled_grad * normed_two, axis=-1, keepdims=True)
    )
    conv_grad = conv_grad.astype(jnp.bfloat16).reshape(frames, utter_count, model_width)
    conv_rimmed = extended(conv_grad, (("ctx", 0),), half_width)
    conv_wide = conv_rimmed.astype(jnp.float32)
    conv_local = conv_wide[half_width : half_width + frames]
    kernel_cols = []
    glu_grad = jnp.zeros((frames, utter_count, model_width), jnp.float32)
    for offset in range(kernel_len):
        kernel_cols.append(jnp.sum(conv_local * glu_wide[offset : offset + frames], axis=(0, 1)))
        start_row = 2 * half_width - offset
        glu_grad = glu_grad + conv_kernel[offset] * conv_wide[start_row : start_row + frames]
    kernel_grad = jnp.stack(kernel_cols, axis=1)
    glu_grad = glu_grad.reshape(row_count, model_width) * row_mask
    linear_grad = glu_grad * gate_part
    gate_grad = glu_grad * linear_part * gate_part * (1.0 - gate_part)
    lifted_grad = jnp.concatenate([linear_grad, gate_grad], axis=1).astype(jnp.bfloat16)
    up_grad = jnp.einsum("rj,ri->ji", lifted_grad, scaled_one, preferred_element_type=jnp.float32)
    input_grad = lax.dot_general(
        lifted_grad, up_weight, (((1,), (1,)), ((), ())), preferred_element_type=jnp.float32
    )
    gain_one_grad = jnp.sum(input_grad * normed_one, axis=0)
    summed = (
        lax.psum_scatter(up_grad, ("dp", "ctx"), scatter_dimension=0, tiled=True),
        lax.psum_scatter(down_grad, ("dp", "ctx"), scatter_dimension=0, tiled=True),
        lax.psum_scatter(kernel_grad, ("dp", "ctx"), scatter_dimension=0, tiled=True),
        lax.psum_scatter(gain_one_grad, ("dp", "ctx"), scatter_dimension=0, tiled=True),
        lax.psum_scatter(gain_two_grad, ("dp", "ctx"), scatter_dimension=0, tiled=True),
    )
    return (block_out, summed[0], summed[1], summed[2], summed[3], summed[4])


def solution(mesh):
    in_specs = (
        P("ctx", "dp", None),
        P("ctx", "dp", None),
        P(),
        P(),
        P(),
        P(),
        P(),
        P(),
        P("dp"),
        P("ctx", "dp", None),
    )
    out_specs = (
        P("ctx", "dp", None),
        P(("dp", "ctx"), None),
        P(("dp", "ctx"), None),
        P(("dp", "ctx"), None),
        P(("dp", "ctx")),
        P(("dp", "ctx")),
    )
    return jax.shard_map(
        on_device, mesh=mesh, in_specs=in_specs, out_specs=out_specs, check_vma=False
    )
```

profile of v0, /device:TPU:0, one launch (start us, length us, event | category | flops | bytes accessed | tf_op | source)
XLA Modules:
  0.0 558.3 jit_solution(371304480372175075)
XLA Ops:
  7.2 0.0 copy-start
  8.0 0.6 reshape.319
  8.6 7.3 %all-to-all-start = ((bf16[64,8,2]{0,2,1:T(2,128)(2,1)}), bf16[64,8,2]{0,2,1:T(2,128)(2,1)S(1)}, u32[]{:S(2)}, u32[]{:S(2)}) async-start(bf16[64,8,2]{0,2,1:T(2,128)(2,1)} %reshape.319), calls=%async_computation | async-start | bytes 8192 | tf_op jit(solution)/shard_map/all_to_all | solution.py:95
  15.9 1.6 reshape.320
  17.5 0.9 copy.34
  18.4 3.8 all-to-all-done
  22.3 3.5 all-to-all-start.1
  25.8 0.1 gt.19
  25.9 13.1 %all-to-all-done.1 = bf16[64,8,2,192]{3,0,2,1:T(8,128)(2,1)S(1)} async-done(((bf16[64,8,2,192]{3,0,2,1:T(8,128)(2,1)}), bf16[64,8,2,192]{3,0,2,1:T(8,128)(2,1)S(1)}, u32[]{:S(2)}, u32[]{:S(2)}) %all-to-all-start.1) | async-done | bytes 393248 | tf_op jit(solution)/shard_map/all_to_all | solution.py:94
  39.1 0.8 fusion.102
  39.9 1.1 fusion.6
  41.0 0.0 copy-start.3
  41.0 0.2 copy.40
  41.2 0.9 reshape.331
  42.1 3.7 all-to-all-start.2
  45.8 0.0 reduce-scatter.10.cloned.1.call-start
  45.9 0.0 copy-start.12
  45.9 0.0 copy-start.13
  45.9 0.1 fusion.100
  46.2 6.9 %all-to-all-done.2 = bf16[8,2,4096]{2,1,0:T(2,128)(2,1)S(1)} async-done(((bf16[8,2,4096]{2,1,0:T(2,128)(2,1)}), bf16[8,2,4096]{2,1,0:T(2,128)(2,1)S(1)}, u32[]{:S(2)}, u32[]{:S(2)}) %all-to-all-start.2) | async-done | bytes 131104 | tf_op jit(solution)/shard_map/all_to_all | solution.py:98
  53.1 0.2 reshape.332
  53.3 0.2 copy.50
  53.5 0.2 reshape.323
  53.7 2.2 fusion.107
  55.9 0.2 multiply_reduce_fusion.34
  56.1 3.1 fusion.96
  59.3 0.1 multiply_convert_fusion.5
  59.4 2.1 collective-permute-start
  61.5 1.3 collective-permute-start.1
  62.8 0.1 fusion.114
  62.9 0.2 collective-permute-done
  63.1 4.2 collective-permute-done.1
  67.7 0.8 fusion.98
  68.5 0.2 multiply_reduce_fusion.33
  68.8 1.4 multiply_reduce_fusion
  70.2 0.1 multiply_convert_fusion.3
  70.3 3.9 collective-permute-start.2
  74.3 1.3 collective-permute-start.3
  75.6 0.3 collective-permute-done.2
  75.8 4.2 collective-permute-done.3
  80.1 0.9 multiply_reduce_fusion.19
  81.1 0.9 multiply_reduce_fusion.10
  82.0 1.1 multiply_reduce_fusion.1
  83.1 5.5 stack.127
  88.6 1.9 copy.44
  90.5 0.0 reduce-scatter.10.cloned.1.call-update
  90.6 0.0 reduce-scatter.8.cloned.1.call-start
  90.6 3.7 fusion.59
  94.3 0.0 reduce-scatter.8.cloned.1.call-update
  94.4 0.2 reduce-scatter.6.cloned.1.call-start
  94.6 1.7 multiply_convert_fusion.2
  96.4 0.1 multiply_convert_fusion.1
  96.5 0.5 copy-done.1
  97.0 4.5 fusion.58
  101.6 0.0 reduce-scatter.6.cloned.1.call-update
  101.6 0.6 copy-done.36
  102.2 1.2 fusion.5
  103.5 3.6 fusion.4
  107.1 39.3 %all-reduce.2 = (f32[1024]{0:T(1024)S(1)}, f32[1024]{0:T(1024)S(1)}) all-reduce(f32[1024]{0:T(1024)S(1)} %fusion.4, f32[1024]{0:T(1024)S(1)} %copy-done.47), channel_id=5, replica_groups=mesh['dp'=4,'ctx'=8] {'dp','ctx'}, use_global_device_ids=true, to_apply=%region_43.44.clone | all-reduce | flops 2048 | bytes 16384
  146.4 0.6 dynamic-slice.1
  147.0 0.6 dynamic-slice.2
  147.6 75.9 %reduce-scatter.10.cloned.1.call-done = f32[32,31]{1,0:T(8,128)} async-done(((f32[1024,31]{1,0:T(8,128)}), f32[32,31]{1,0:T(8,128)}) %reduce-scatter.10.cloned.1.call-update) | async-done | bytes 3984
  223.5 143.5 %reduce-scatter.8.cloned.1.call-done = f32[32,1024]{1,0:T(8,128)} async-done(((f32[1024,1024]{1,0:T(8,128)}), f32[32,1024]{1,0:T(8,128)}) %reduce-scatter.8.cloned.1.call-update) | async-done | bytes 131088 | tf_op jit(solution)/shard_map/reduce_scatter | solution.py:160
  367.0 184.7 %reduce-scatter.6.cloned.1.call-done = f32[64,1024]{1,0:T(8,128)} async-done(((f32[2048,1024]{1,0:T(8,128)}), f32[64,1024]{1,0:T(8,128)}) %reduce-scatter.6.cloned.1.call-update) | async-done | bytes 262160 | tf_op jit(solution)/shard_map/reduce_scatter | solution.py:159
  (108 shorter events, 0.5 us)
Async XLA Ops:
  7.2 61.5 %copy-start = (bf16[1024,1024]{1,0:T(8,128)(2,1)S(1)}, bf16[1024,1024]{1,0:T(8,128)(2,1)}, u32[]{:S(2)}) copy-start(bf16[1024,1024]{1,0:T(8,128)(2,1)} %param.17) | copy-start | bytes 6291460
  8.0 54.8 %copy-start.40 = (f32[64]{0:T(128)}, f32[64]{0:T(128)S(1)}, u32[]{:S(2)}) copy-start(f32[64]{0:T(128)S(1)} %get-tuple-element.82) | copy-start | bytes 772
  8.0 60.7 %copy-start.46 = (bf16[64]{0:T(256)(128)(2,1)}, bf16[64]{0:T(256)(128)(2,1)S(1)}, u32[]{:S(2)}) copy-start(bf16[64]{0:T(256)(128)(2,1)S(1)} %get-tuple-element.83) | copy-start | bytes 388
  8.6 13.7 %all-to-all-start = ((bf16[64,8,2]{0,2,1:T(2,128)(2,1)}), bf16[64,8,2]{0,2,1:T(2,128)(2,1)S(1)}, u32[]{:S(2)}, u32[]{:S(2)}) async-start(bf16[64,8,2]{0,2,1:T(2,128)(2,1)} %reshape.319), calls=%async_computation | async-start | bytes 8192 | tf_op jit(solution)/shard_map/all_to_all | solution.py:95
  22.3 16.8 %all-to-all-start.1 = ((bf16[64,8,2,192]{3,0,2,1:T(8,128)(2,1)}), bf16[64,8,2,192]{3,0,2,1:T(8,128)(2,1)S(1)}, u32[]{:S(2)}, u32[]{:S(2)}) async-start(bf16[64,8,2,192]{3,0,2,1:T(8,128)(2,1)} %copy.34), calls=%async_computation.1 | async-start | bytes 1048576 | tf_op jit(solution)/shard_map/all_to_all | solution.py:94
  39.9 5.9 %copy-start.5 = (f32[31,1024]{1,0:T(8,128)S(1)}, f32[31,1024]{1,0:T(8,128)}, u32[]{:S(2)}) copy-start(f32[31,1024]{1,0:T(8,128)} %param.15) | copy-start | bytes 380932
  41.0 12.7 %copy-start.3 = (bf16[64,1,1024]{2,0,1:T(8,128)(2,1)S(1)}, bf16[64,1,1024]{2,0,1:T(8,128)(2,1)}, u32[]{:S(2)}) copy-start(bf16[64,1,1024]{2,0,1:T(8,128)(2,1)} %param.10) | copy-start | bytes 393220
  42.1 11.0 %all-to-all-start.2 = ((bf16[8,2,4096]{2,1,0:T(2,128)(2,1)}), bf16[8,2,4096]{2,1,0:T(2,128)(2,1)S(1)}, u32[]{:S(2)}, u32[]{:S(2)}) async-start(bf16[8,2,4096]{2,1,0:T(2,128)(2,1)} %reshape.331), calls=%async_computation.2 | async-start | bytes 262144 | tf_op jit(solution)/shard_map/all_to_all | solution.py:98
  45.8 177.7 %reduce-scatter.10.cloned.1.call-start = ((), (), s32[]{:S(2)}) async-start(), calls=%async_computation.8 | async-start | bytes 540672
  45.9 21.5 %copy-start.6 = (f32[1,1024]{1,0:T(1,128)}, f32[1,1024]{1,0:T(1,128)S(1)}, u32[]{:S(2)}) copy-start(f32[1,1024]{1,0:T(1,128)S(1)} %get-tuple-element.113) | copy-start | bytes 12292
  45.9 21.5 %copy-start.7 = (f32[1,1024]{1,0:T(1,128)}, f32[1,1024]{1,0:T(1,128)S(1)}, u32[]{:S(2)}) copy-start(f32[1,1024]{1,0:T(1,128)S(1)} %get-tuple-element.114) | copy-start | bytes 12292
  45.9 21.5 %copy-start.8 = (f32[1,1024]{1,0:T(1,128)}, f32[1,1024]{1,0:T(1,128)S(1)}, u32[]{:S(2)}) copy-start(f32[1,1024]{1,0:T(1,128)S(1)} %get-tuple-element.115) | copy-start | bytes 12292
  45.9 21.5 %copy-start.9 = (f32[1,1024]{1,0:T(1,128)}, f32[1,1024]{1,0:T(1,128)S(1)}, u32[]{:S(2)}) copy-start(f32[1,1024]{1,0:T(1,128)S(1)} %get-tuple-element.116) | copy-start | bytes 12292
  45.9 21.5 %copy-start.10 = (f32[1,1024]{1,0:T(1,128)}, f32[1,1024]{1,0:T(1,128)S(1)}, u32[]{:S(2)}) copy-start(f32[1,1024]{1,0:T(1,128)S(1)} %get-tuple-element.117) | copy-start | bytes 12292
  45.9 21.5 %copy-start.11 = (f32[1,1024]{1,0:T(1,128)}, f32[1,1024]{1,0:T(1,128)S(1)}, u32[]{:S(2)}) copy-start(f32[1,1024]{1,0:T(1,128)S(1)} %get-tuple-element.118) | copy-start | bytes 12292
  45.9 21.5 %copy-start.12 = (f32[1,1024]{1,0:T(1,128)}, f32[1,1024]{1,0:T(1,128)S(1)}, u32[]{:S(2)}) copy-start(f32[1,1024]{1,0:T(1,128)S(1)} %get-tuple-element.119) | copy-start | bytes 12292
  45.9 21.5 %copy-start.13 = (f32[1,1024]{1,0:T(1,128)}, f32[1,1024]{1,0:T(1,128)S(1)}, u32[]{:S(2)}) copy-start(f32[1,1024]{1,0:T(1,128)S(1)} %get-tuple-element.120) | copy-start | bytes 12292
  46.0 21.4 %copy-start.14 = (f32[1,1024]{1,0:T(1,128)}, f32[1,1024]{1,0:T(1,128)S(1)}, u32[]{:S(2)}) copy-start(f32[1,1024]{1,0:T(1,128)S(1)} %get-tuple-element.90) | copy-start | bytes 12292
  46.0 21.4 %copy-start.15 = (f32[1,1024]{1,0:T(1,128)}, f32[1,1024]{1,0:T(1,128)S(1)}, u32[]{:S(2)}) copy-start(f32[1,1024]{1,0:T(1,128)S(1)} %get-tuple-element.91) | copy-start | bytes 12292
  46.0 21.4 %copy-start.16 = (f32[1,1024]{1,0:T(1,128)}, f32[1,1024]{1,0:T(1,128)S(1)}, u32[]{:S(2)}) copy-start(f32[1,1024]{1,0:T(1,128)S(1)} %get-tuple-element.92) | copy-start | bytes 12292
  46.0 21.4 %copy-start.17 = (f32[1,1024]{1,0:T(1,128)}, f32[1,1024]{1,0:T(1,128)S(1)}, u32[]{:S(2)}) copy-start(f32[1,1024]{1,0:T(1,128)S(1)} %get-tuple-element.93) | copy-start | bytes 12292
  46.0 21.4 %copy-start.18 = (f32[1,1024]{1,0:T(1,128)}, f32[1,1024]{1,0:T(1,128)S(1)}, u32[]{:S(2)}) copy-start(f32[1,1024]{1,0:T(1,128)S(1)} %get-tuple-element.94) | copy-start | bytes 12292
  46.1 21.4 %copy-start.19 = (f32[1,1024]{1,0:T(1,128)}, f32[1,1024]{1,0:T(1,128)S(1)}, u32[]{:S(2)}) copy-start(f32[1,1024]{1,0:T(1,128)S(1)} %get-tuple-element.95) | copy-start | bytes 12292
  46.1 21.4 %copy-start.20 = (f32[1,1024]{1,0:T(1,128)}, f32[1,1024]{1,0:T(1,128)S(1)}, u32[]{:S(2)}) copy-start(f32[1,1024]{1,0:T(1,128)S(1)} %get-tuple-element.96) | copy-start | bytes 12292
  46.1 21.4 %copy-start.21 = (f32[1,1024]{1,0:T(1,128)}, f32[1,1024]{1,0:T(1,128)S(1)}, u32[]{:S(2)}) copy-start(f32[1,1024]{1,0:T(1,128)S(1)} %get-tuple-element.97) | copy-start | bytes 12292
  46.1 21.4 %copy-start.22 = (f32[1,1024]{1,0:T(1,128)}, f32[1,1024]{1,0:T(1,128)S(1)}, u32[]{:S(2)}) copy-start(f32[1,1024]{1,0:T(1,128)S(1)} %get-tuple-element.98) | copy-start | bytes 12292
  46.1 21.4 %copy-start.23 = (f32[1,1024]{1,0:T(1,128)}, f32[1,1024]{1,0:T(1,128)S(1)}, u32[]{:S(2)}) copy-start(f32[1,1024]{1,0:T(1,128)S(1)} %get-tuple-element.99) | copy-start | bytes 12292
  46.1 21.4 %copy-start.24 = (f32[1,1024]{1,0:T(1,128)}, f32[1,1024]{1,0:T(1,128)S(1)}, u32[]{:S(2)}) copy-start(f32[1,1024]{1,0:T(1,128)S(1)} %get-tuple-element.100) | copy-start | bytes 12292
  46.1 21.4 %copy-start.25 = (f32[1,1024]{1,0:T(1,128)}, f32[1,1024]{1,0:T(1,128)S(1)}, u32[]{:S(2)}) copy-start(f32[1,1024]{1,0:T(1,128)S(1)} %get-tuple-element.101) | copy-start | bytes 12292
  46.1 21.4 %copy-start.26 = (f32[1,1024]{1,0:T(1,128)}, f32[1,1024]{1,0:T(1,128)S(1)}, u32[]{:S(2)}) copy-start(f32[1,1024]{1,0:T(1,128)S(1)} %get-tuple-element.102) | copy-start | bytes 12292
  46.1 21.4 %copy-start.27 = (f32[1,1024]{1,0:T(1,128)}, f32[1,1024]{1,0:T(1,128)S(1)}, u32[]{:S(2)}) copy-start(f32[1,1024]{1,0:T(1,128)S(1)} %get-tuple-element.103) | copy-start | bytes 12292
  46.1 21.4 %copy-start.28 = (f32[1,1024]{1,0:T(1,128)}, f32[1,1024]{1,0:T(1,128)S(1)}, u32[]{:S(2)}) copy-start(f32[1,1024]{1,0:T(1,128)S(1)} %get-tuple-element.104) | copy-start | bytes 12292
  46.2 21.4 %copy-start.29 = (f32[1,1024]{1,0:T(1,128)}, f32[1,1024]{1,0:T(1,128)S(1)}, u32[]{:S(2)}) copy-start(f32[1,1024]{1,0:T(1,128)S(1)} %get-tuple-element.105) | copy-start | bytes 12292
  46.2 21.4 %copy-start.30 = (f32[1,1024]{1,0:T(1,128)}, f32[1,1024]{1,0:T(1,128)S(1)}, u32[]{:S(2)}) copy-start(f32[1,1024]{1,0:T(1,128)S(1)} %get-tuple-element.106) | copy-start | bytes 12292
  46.2 21.4 %copy-start.31 = (f32[1,1024]{1,0:T(1,128)}, f32[1,1024]{1,0:T(1,128)S(1)}, u32[]{:S(2)}) copy-start(f32[1,1024]{1,0:T(1,128)S(1)} %get-tuple-element.107) | copy-start | bytes 12292
  46.2 21.4 %copy-start.32 = (f32[1,1024]{1,0:T(1,128)}, f32[1,1024]{1,0:T(1,128)S(1)}, u32[]{:S(2)}) copy-start(f32[1,1024]{1,0:T(1,128)S(1)} %get-tuple-element.108) | copy-start | bytes 12292
  46.2 9.9 %copy-start.33 = (f32[1024]{0:T(1024)S(1)}, f32[1024]{0:T(1024)}, u32[]{:S(2)}) copy-start(f32[1024]{0:T(1024)} %param.13) | copy-start | bytes 12292
  55.9 3.3 copy-start.37
  56.1 3.1 copy-start.41
  59.4 3.7 collective-permute-start
  61.5 5.8 %collective-permute-start.1 = (bf16[15,1,1024]{2,0,1:T(8,128)(2,1)S(1)}, bf16[15,1,1024]{2,0,1:T(8,128)(2,1)S(1)}, u32[]{:S(2)}, u32[]{:S(2)}) collective-permute-start(bf16[15,1,1024]{2,0,1:T(8,128)(2,1)S(1)} %get-tuple-element.122), channel_id=1, source_target_pairs={{1,0},{2,1},{3,2},{4,3},{5,4},{6,5},{7,6},{9,8},{10,9},{11,10},{12... | collective-permute-start | bytes 92168 | tf_op jit(solution)/shard_map/ppermute | solution.py:22
  67.6 1.1 copy-start.4
  67.6 1.1 copy-start.35
  68.5 1.8 copy-start.44
  68.7 1.6 copy-start.48
  70.3 5.5 collective-permute-start.2
  74.3 5.8 %collective-permute-start.3 = (bf16[15,1,1024]{2,0,1:T(8,128)(2,1)S(1)}, bf16[15,1,1024]{2,0,1:T(8,128)(2,1)S(1)}, u32[]{:S(2)}, u32[]{:S(2)}) collective-permute-start(bf16[15,1,1024]{2,0,1:T(8,128)(2,1)S(1)} %get-tuple-element.89), channel_id=1, source_target_pairs={{1,0},{2,1},{3,2},{4,3},{5,4},{6,5},{7,6},{9,8},{10,9},{11,10},{12... | collective-permute-start | bytes 92168 | tf_op jit(solution)/shard_map/ppermute | solution.py:22
  90.6 276.5 %reduce-scatter.8.cloned.1.call-start = ((), (), s32[]{:S(2)}) async-start(), calls=%async_computation.7 | async-start | bytes 4325376 | tf_op jit(solution)/shard_map/reduce_scatter | solution.py:160
  94.4 457.4 %reduce-scatter.6.cloned.1.call-start = ((), (), s32[]{:S(2)}) async-start(), calls=%async_computation.6 | async-start | bytes 8650752 | tf_op jit(solution)/shard_map/reduce_scatter | solution.py:159
  94.6 2.4 copy-start.34
  94.6 2.4 copy-start.38
  94.6 2.4 copy-start.42
  96.3 0.7 copy-start.1
  101.5 0.7 copy-start.36
  101.6 0.7 copy-start.45
  101.6 0.7 copy-start.49
  101.6 1.9 copy-start.2
  101.6 1.9 copy-start.39
  101.6 1.8 copy-start.43
  103.4 3.6 copy-start.47
Sparse Core Ops, SparseCore 0:
  90.7 132.7 reduce-scatter.9
  226.4 140.5 reduce-scatter.7
  370.0 181.6 reduce-scatter.5
where the time goes:
time: 559 us; the launch traced here: 558 us
  waiting for transfers between devices  437 us (78%)
  blocking collectives  39.3 us (7%)
  starting transfers between devices  23.4 us (4%)
  matrix products  21.7 us (4%)
  between operations  15.5 us (3%)
  local copies, waits for them, and re-layouts  15 us (3%)
  other arithmetic  6.44 us (1%)
    reduce_scatter x1, waiting for transfers between devices, on_device(): lax.psum_scatter(up_grad, ('dp', 'ctx'), scatter_dimension=0, tiled=True)  185 us
    reduce_scatter x1, waiting for transfers between devices, on_device(): lax.psum_scatter(down_grad, ('dp', 'ctx'), scatter_dimension=0, tiled=True)  144 us
    unnamed x4, waiting for transfers between devices  76 us
    unnamed x1, blocking collectives  39.3 us
    all_to_all x1, waiting for transfers between devices, on_device(): lax.all_to_all(packed, 'ctx', split_axis=1, concat_axis=0, tiled=True)  13.1 us
  transfers between devices with their start and end apart: 10, of which 10 were waited for; matrix products, arithmetic and copies ran while one was open for 3% of the time, Pallas kernels for 0%

commit v1 on v0

v1 whole, which is shorter than its diff:
```python
import jax
import jax.numpy as jnp
from jax import lax
from jax.sharding import Mesh, PartitionSpec as P

HEADS = 16


EPSILON = 1e-05

MARGIN = 32

CTX = ("chi", "clo")
FIRST = ("dlo", "chi")
SECOND = ("dhi", "clo")


def normalize(values):
    center = values - jnp.mean(values, axis=-1, keepdims=True)
    inverse = lax.rsqrt(jnp.mean(center * center, axis=-1, keepdims=True) + EPSILON)
    return (center * inverse, inverse)


def attend(packed, key_lengths):
    length, count, triple = packed.shape
    head_size = triple // 3
    query_rows = packed[:, :, :head_size]
    key_rows = packed[:, :, head_size : 2 * head_size]
    value_rows = packed[:, :, 2 * head_size :]
    allowed = jnp.arange(length, dtype=jnp.int32)[None, :] < key_lengths[:, None]
    scores = (
        jnp.einsum("qmd,kmd->mqk", query_rows, key_rows, preferred_element_type=jnp.float32)
        * head_size ** (-0.5)
    )
    scores = jnp.where(allowed[:, None, :], scores, -jnp.inf)
    highest = jnp.max(scores, axis=-1, keepdims=True)
    raised = jnp.exp(scores - highest)
    weights_bf = (raised / jnp.sum(raised, axis=-1, keepdims=True)).astype(jnp.bfloat16)
    return jnp.einsum(
        "mqk,kmd->qmd", weights_bf, value_rows, preferred_element_type=jnp.float32
    ).astype(jnp.bfloat16)


def by_owner(cols, sizes):
    dhi, dlo, chi, clo = sizes
    rows, width = cols.shape
    part = width // (dhi * dlo * chi * clo)
    split = cols.reshape(rows, dhi, dlo, chi, clo, part)
    return jnp.transpose(split, (2, 3, 0, 1, 4, 5)).reshape(dlo * chi, rows, dhi * clo * part)


def gathered(rows, chi):
    copies = jnp.broadcast_to(rows[None], (chi,) + rows.shape)
    line = lax.all_to_all(copies, "chi", split_axis=0, concat_axis=0, tiled=True)
    line = line.reshape(chi * rows.shape[0], rows.shape[1])
    other = lax.ppermute(line, "dlo", [(0, 1), (1, 0)])
    first = lax.axis_index("dlo") == 0
    return jnp.concatenate([jnp.where(first, line, other), jnp.where(first, other, line)], axis=0)


def on_device(
    residual,
    projections,
    out_weight,
    gain_one,
    up_weight,
    conv_kernel,
    gain_two,
    down_weight,
    lengths,
    out_grad,
):
    frames, utter_count, width = residual.shape
    head_size = width // HEADS
    kernel_len = conv_kernel.shape[0]
    half = (kernel_len - 1) // 2
    dhi, dlo, chi, clo = sizes = tuple(lax.axis_size(a) for a in ("dhi", "dlo", "chi", "clo"))
    ctx = chi * clo
    length = frames * ctx
    items = utter_count * HEADS // ctx
    me = lax.axis_index(CTX)
    bf = jnp.bfloat16
    f32 = jnp.float32

    packed = projections.reshape(frames, ctx, items, 3 * head_size)
    packed = lax.all_to_all(packed, CTX, split_axis=1, concat_axis=0, tiled=True)
    packed = packed.reshape(length, items, 3 * head_size)

    both = jnp.concatenate([residual, out_grad], axis=-1)
    up = [(i, i + 1) for i in range(ctx - 1)]
    down = [(j, i) for i, j in up]
    before = lax.ppermute(both[frames - MARGIN :], CTX, up)
    after = lax.ppermute(both[:MARGIN], CTX, down)
    both = jnp.concatenate([before, both, after], axis=0)
    wide = frames + 2 * MARGIN
    place = me * frames - MARGIN + jnp.arange(wide, dtype=jnp.int32)
    valid = (place[:, None] >= 0) & (place[:, None] < lengths[None, :])
    row_mask = valid.astype(f32)[:, :, None]
    cot = jnp.where(valid[:, :, None], both[:, :, width:], 0)
    edge = MARGIN // 2
    near = wide - 2 * edge
    cot_near = cot[edge : edge + near]
    cot_own = cot[MARGIN : MARGIN + frames].reshape(frames * utter_count, width)
    act_grad = lax.dot_general(
        cot_near, down_weight, (((2,), (1,)), ((), ())), preferred_element_type=f32
    )

    key_lengths = lengths[(me * items + jnp.arange(items, dtype=jnp.int32)) // HEADS]
    context = attend(packed, key_lengths).reshape(length, items * head_size)
    padded = jnp.pad(context, ((MARGIN, MARGIN), (0, 0)))
    windows = jnp.stack([padded[i * frames : i * frames + wide] for i in range(ctx)])
    context = lax.all_to_all(windows, CTX, split_axis=0, concat_axis=0, tiled=True)
    context = jnp.transpose(context, (1, 0, 2)).reshape(wide, utter_count, width)

    cot_cols = lax.all_to_all(
        by_owner(cot_own, sizes), FIRST, split_axis=0, concat_axis=0, tiled=True
    )

    hidden = both[:, :, :width].astype(f32) + jnp.einsum(
        "fuc,cd->fud", context, out_weight, preferred_element_type=f32
    )
    normed_one, _ = normalize(hidden)
    scaled_one = (normed_one * gain_one).astype(bf)
    own = slice(MARGIN, MARGIN + frames)
    own_near = slice(MARGIN - edge, MARGIN - edge + frames)
    rows = frames * utter_count
    scaled_own = scaled_one[own].reshape(rows, width)
    scaled_all = gathered(scaled_own, chi)

    lifted = jnp.einsum("fuc,cd->fud", scaled_one, up_weight, preferred_element_type=f32)
    linear_part = lifted[:, :, :width]
    gate_part = jax.nn.sigmoid(lifted[:, :, width:])
    glu = (linear_part * gate_part * row_mask).astype(bf).astype(f32)
    conv_out = jnp.zeros((near, utter_count, width), f32)
    for j in range(kernel_len):
        start = edge + j - half
        conv_out = conv_out + conv_kernel[j] * glu[start : start + near]
    normed_two, inverse_two = normalize(conv_out)
    pre_act = normed_two * gain_two
    gate_two = jax.nn.sigmoid(pre_act)
    activated = (pre_act * gate_two)[own_near].astype(bf).reshape(rows, width)
    activated_all = gathered(activated, chi)
    block_out = (
        hidden[own].reshape(rows, width)
        + jnp.dot(activated, down_weight, preferred_element_type=f32)
    ).astype(bf)
    block_out = block_out.reshape(frames, utter_count, width)

    pre_grad = act_grad * gate_two * (1.0 + pre_act * (1.0 - gate_two))
    gain_two_grad = jnp.sum((pre_grad * normed_two)[own_near], axis=(0, 1))
    scaled_grad = pre_grad * gain_two
    conv_grad = inverse_two * (
        scaled_grad
        - jnp.mean(scaled_grad, axis=-1, keepdims=True)
        - normed_two * jnp.mean(scaled_grad * normed_two, axis=-1, keepdims=True)
    )
    conv_grad = conv_grad.astype(bf).astype(f32)
    conv_own = conv_grad[own_near]
    small = []
    glu_grad = jnp.zeros((frames, utter_count, width), f32)
    for j in range(kernel_len):
        start = MARGIN + j - half
        small.append(jnp.sum(conv_own * glu[start : start + frames], axis=(0, 1)))
        start = MARGIN - edge + half - j
        glu_grad = glu_grad + conv_kernel[j] * conv_grad[start : start + frames]
    glu_grad = glu_grad * row_mask[own]
    gate_own = gate_part[own]
    linear_grad = glu_grad * gate_own
    gate_grad = glu_grad * linear_part[own] * gate_own * (1.0 - gate_own)
    lifted_grad = jnp.concatenate([linear_grad, gate_grad], axis=-1).astype(bf)
    lifted_grad = lifted_grad.reshape(rows, 2 * width)
    input_grad = lax.dot_general(
        lifted_grad, up_weight, (((1,), (1,)), ((), ())), preferred_element_type=f32
    )
    gain_one_grad = jnp.sum(input_grad * normed_one[own].reshape(rows, width), axis=0)

    small = small + [gain_one_grad, gain_two_grad]
    count = kernel_len + 2
    small = by_owner(jnp.stack(small).astype(bf), sizes)
    small = small.reshape(dlo * chi, -1)
    cols = by_owner(lifted_grad, sizes)
    col_count = cols.shape[2]
    spare = -small.shape[1] % col_count
    small = jnp.pad(small, ((0, 0), (0, spare))).reshape(dlo * chi, -1, col_count)
    message = jnp.concatenate([cols, small], axis=1)
    message = lax.all_to_all(message, FIRST, split_axis=0, concat_axis=0, tiled=True)
    cols = message[:, :rows].reshape(-1, col_count)
    small = jnp.sum(message[:, rows:].astype(f32), axis=0).reshape(-1)
    seconds = dhi * clo
    small_width = width // (ctx * dhi * dlo)
    small = small[: count * seconds * small_width].reshape(count, seconds, small_width)
    small = jnp.transpose(small, (1, 0, 2)).reshape(seconds, count * small_width)

    up_part = lax.dot_general(
        cols, scaled_all, (((0,), (0,)), ((), ())), preferred_element_type=f32
    ).reshape(seconds, -1, width)
    down_part = lax.dot_general(
        cot_cols.reshape(cols.shape[0], -1),
        activated_all,
        (((0,), (0,)), ((), ())),
        preferred_element_type=f32,
    ).reshape(seconds, -1, width)
    spare = -small.shape[1] % width
    small = jnp.pad(small, ((0, 0), (0, spare))).reshape(seconds, -1, width)
    up_rows, down_rows = up_part.shape[1], down_part.shape[1]
    parts = jnp.concatenate([up_part.astype(bf), down_part.astype(bf), small.astype(bf)], axis=1)
    parts = lax.all_to_all(parts, SECOND, split_axis=0, concat_axis=0, tiled=True)
    total = jnp.sum(parts.astype(f32), axis=0)
    up_grad = total[:up_rows]
    down_grad = total[up_rows : up_rows + down_rows]
    small = total[up_rows + down_rows :].reshape(-1)[: count * small_width]
    small = small.reshape(count, small_width)
    kernel_grad = jnp.transpose(small[:kernel_len])
    return (block_out, up_grad, down_grad, kernel_grad, small[kernel_len], small[kernel_len + 1])


def solution(mesh):
    dp, ctx = mesh.shape["dp"], mesh.shape["ctx"]
    fine = Mesh(mesh.devices.reshape(dp // 2, 2, ctx // 2, 2), ("dhi", "dlo", "chi", "clo"))
    dp_axes, ctx_axes = ("dhi", "dlo"), ("chi", "clo")
    every = ("dhi", "dlo", "chi", "clo")
    in_specs = (
        P(ctx_axes, dp_axes, None),
        P(ctx_axes, dp_axes, None),
        P(),
        P(),
        P(),
        P(),
        P(),
        P(),
        P(dp_axes),
        P(ctx_axes, dp_axes, None),
    )
    out_specs = (
        P(ctx_axes, dp_axes, None),
        P(every, None),
        P(every, None),
        P(every, None),
        P(every),
        P(every),
    )
    return jax.shard_map(
        on_device, mesh=fine, in_specs=in_specs, out_specs=out_specs, check_vma=False
    )
```

time: 559 us -> 213 us (0.38)
  waiting for transfers between devices: 437 us -> 63.9 us
  local copies, waits for them, and re-layouts: 15 us -> 75.5 us
  blocking collectives: 39.3 us -> 0 us
  starting transfers between devices: 23.4 us -> 37.9 us
  other arithmetic: 6.44 us -> 20.5 us
  between operations: 15.5 us -> 2.8 us
  matrix products: 21.7 us -> 10.6 us
    reduce_scatter x2 -> x0, waiting for transfers between devices: 328 us -> none  [the longest x1 185 us: on_device(): lax.psum_scatter(up_grad, ('dp', 'ctx'), scatter_dimension=0, tiled=True)]
    unnamed x4 -> x0, waiting for transfers between devices: 76 us -> none
    all_to_all x3 -> x7, waiting for transfers between devices: 23.9 us -> 63.9 us  [the longest x2 25.6 us: gathered(): lax.all_to_all(copies, 'chi', split_axis=0, concat_axis=0, tiled=True)]
    unnamed x1 -> x0, blocking collectives: 39.3 us -> none
    another operation x1 -> x36, local copies, waits for them, and re-layouts: 5.51 us -> 42.7 us  [the longest x34 41.8 us: on_device(): small = by_owner(jnp.stack(small).astype(bf), sizes)]
    all_to_all x3 -> x7, starting transfers between devices: 14.4 us -> 30.4 us  [the longest x2 7.59 us: gathered(): lax.all_to_all(copies, 'chi', split_axis=0, concat_axis=0, tiled=True)]
    dot_general x7, matrix products: 17.2 us -> 7.68 us  [the longest x1 2.37 us: on_device(): jnp.einsum('fuc,cd->fud', context, out_weight, preferred_element_type=f32)]
    ppermute x4, waiting for transfers between devices: 8.91 us -> 0.01 us  [the longest x2 0.01 us: gathered(): other = lax.ppermute(line, 'dlo', [(0, 1), (1, 0)])]
  transfers between devices with their start and end apart: 10 -> 11, of which waited for: 10 -> 6; matrix products, arithmetic and copies ran while one was open for 3% -> 44% of each run, Pallas kernels for 0% -> 0%
where the time goes in v1:
time: 213 us; the launch traced here: 211 us
  local copies, waits for them, and re-layouts  75.5 us (35%)
  waiting for transfers between devices  63.9 us (30%)
  starting transfers between devices  37.9 us (18%)
  other arithmetic  20.5 us (10%)
  matrix products  10.6 us (5%)
  between operations  2.8 us (1%)
    another operation x34, local copies, waits for them, and re-layouts, on_device(): small = by_owner(jnp.stack(small).astype(bf), sizes)  41.8 us
    all_to_all x2, waiting for transfers between devices, gathered(): lax.all_to_all(copies, 'chi', split_axis=0, concat_axis=0, tiled=True)  25.6 us
    all_to_all x1, waiting for transfers between devices, on_device(): lax.all_to_all(parts, SECOND, split_axis=0, concat_axis=0, tiled=True)  11.4 us
    all_to_all x1, waiting for transfers between devices, on_device(): lax.all_to_all(message, FIRST, split_axis=0, concat_axis=0, tiled=True)  10.3 us
    all_to_all x1, waiting for transfers between devices, on_device(): lax.all_to_all(packed, CTX, split_axis=1, concat_axis=0, tiled=True)  10.3 us
    unnamed x195, local copies, waits for them, and re-layouts  9.68 us
    all_to_all x2, starting transfers between devices, gathered(): lax.all_to_all(copies, 'chi', split_axis=0, concat_axis=0, tiled=True)  7.59 us
    all_to_all x1, waiting for transfers between devices, on_device(): lax.all_to_all(windows, CTX, split_axis=0, concat_axis=0, tiled=True)  6.3 us
  transfers between devices with their start and end apart: 11, of which 6 were waited for; matrix products, arithmetic and copies ran while one was open for 44% of the time, Pallas kernels for 0%

profile of v1, /device:TPU:0, one launch (start us, length us, event | category | flops | bytes accessed | tf_op | source)
XLA Modules:
  0.0 211.3 jit_solution(13529750846176486112)
XLA Ops:
  3.3 1.3 collective-permute-start.1
  4.6 6.1 %collective-permute-start = (bf16[32,1,2048]{2,0,1:T(8,128)(2,1)S(1)}, bf16[32,1,2048]{2,0,1:T(8,128)(2,1)}, u32[]{:S(2)}, u32[]{:S(2)}) collective-permute-start(bf16[32,1,2048]{2,0,1:T(8,128)(2,1)S(1)} %get-tuple-element.88), channel_id=1, source_target_pairs={{0,1},{1,2},{2,3},{3,4},{4,5},{5,6},{6,7},{8,9},{9,10},{10,11},{11... | collective-permute-start | bytes 393224 | tf_op jit(solution)/shard_map/ppermute | solution.py:92
  10.8 1.6 reshape.474
  13.3 5.6 %all-to-all-start = ((bf16[64,8,2,192]{3,0,2,1:T(8,128)(2,1)}), bf16[64,8,2,192]{3,0,2,1:T(8,128)(2,1)S(1)}, u32[]{:S(2)}, u32[]{:S(2)}) async-start(bf16[64,8,2,192]{3,0,2,1:T(8,128)(2,1)} %copy.62), calls=%async_computation | async-start | bytes 1048576 | tf_op jit(solution)/shard_map/all_to_all | solution.py:86
  22.6 10.3 %all-to-all-done = bf16[64,8,2,192]{3,0,2,1:T(8,128)(2,1)S(1)} async-done(((bf16[64,8,2,192]{3,0,2,1:T(8,128)(2,1)}), bf16[64,8,2,192]{3,0,2,1:T(8,128)(2,1)S(1)}, u32[]{:S(2)}, u32[]{:S(2)}) %all-to-all-start) | async-done | bytes 393248 | tf_op jit(solution)/shard_map/all_to_all | solution.py:86
  32.9 1.5 fusion.169
  34.4 1.8 convolution_convert_fusion.2
  41.4 4.0 %all-to-all-start.1 = ((bf16[8,128,128]{1,2,0:T(8,128)(2,1)}), bf16[8,128,128]{1,2,0:T(8,128)(2,1)}, u32[]{:S(2)}, u32[]{:S(2)}) async-start(bf16[8,128,128]{1,2,0:T(8,128)(2,1)} %constant_dynamic-update-slice_fusion.2), calls=%async_computation.1 | async-start | bytes 524288 | tf_op jit(solution)/shard_map/all_to_all | solution.py:112
  47.6 6.3 %all-to-all-done.1 = bf16[8,128,128]{1,2,0:T(8,128)(2,1)} async-done(((bf16[8,128,128]{1,2,0:T(8,128)(2,1)}), bf16[8,128,128]{1,2,0:T(8,128)(2,1)}, u32[]{:S(2)}, u32[]{:S(2)}) %all-to-all-start.1) | async-done | bytes 262176 | tf_op jit(solution)/shard_map/all_to_all | solution.py:112
  53.9 4.2 %all-to-all-start.4 = ((bf16[8,64,128]{2,1,0:T(8,128)(2,1)}), bf16[8,64,128]{2,1,0:T(8,128)(2,1)}, u32[]{:S(2)}, u32[]{:S(2)}) async-start(bf16[8,64,128]{2,1,0:T(8,128)(2,1)} %copy.74), calls=%async_computation.4 | async-start | bytes 262144 | tf_op jit(solution)/shard_map/all_to_all | solution.py:115
  58.1 2.4 %fusion.163 = (f32[128]{0:T(128)S(1)}, f32[128,1,1024]{2,0,1:T(8,128)S(1)}) fusion(bf16[128,1,2048]{2,0,1:T(8,128)(2,1)S(1)} %pad_maximum_fusion.1, bf16[128,1024]{0,1:T(8,128)(2,1)} %bitcast.15, bf16[1024,1024]{1,0:T(8,128)(2,1)} %param.12), kind=kOutput, calls=%fused_computation.336 | convolution fusion | flops 268828544 | bytes 3146240 | tf_op jit(solution)/shard_map/fuc,cd->fud/dot_general | solution.py:119
  63.9 1.1 fusion.160
  68.3 1.1 fusion.59
  71.0 1.4 stack.138
  72.3 1.3 constant_dynamic-update-slice_fusion.42
  73.6 1.4 stack.139
  75.0 1.4 stack.140
  76.3 1.4 stack.141
  77.7 1.3 stack.142
  79.0 1.3 stack.143
  80.4 1.3 stack.144
  81.7 1.3 stack.145
  83.0 1.4 stack.146
  84.4 1.3 stack.147
  85.7 1.4 stack.148
  87.1 1.3 stack.149
  88.4 1.3 stack.150
  89.8 1.3 stack.151
  91.1 1.3 stack.152
  92.4 1.3 stack.153
  93.7 1.3 stack.154
  95.1 1.3 stack.155
  96.4 1.3 stack.156
  97.7 1.3 stack.157
  99.1 1.3 stack.158
  100.4 1.3 stack.159
  101.7 1.3 stack.160
  103.1 1.3 stack.161
  104.4 1.3 stack.162
  105.8 1.3 stack.163
  107.1 1.3 stack.164
  108.5 1.3 stack.165
  109.8 1.4 stack.166
  111.2 1.4 stack.167
  112.5 1.4 stack.168
  113.9 1.8 multiply_convert_fusion.2
  117.0 1.4 fusion.5
  120.2 1.1 copy.69
  122.1 1.2 copy.85
  123.3 1.5 reshape.483
  125.5 4.8 %all-to-all-start.2 = ((bf16[8,81,256]{2,1,0:T(8,128)(2,1)}), bf16[8,81,256]{2,1,0:T(8,128)(2,1)S(1)}, u32[]{:S(2)}, u32[]{:S(2)}) async-start(bf16[8,81,256]{2,1,0:T(8,128)(2,1)} %pad_maximum_fusion.2), calls=%async_computation.2 | async-start | bytes 720896 | tf_op jit(solution)/shard_map/all_to_all | solution.py:186
  131.4 10.3 %all-to-all-done.2 = bf16[8,81,256]{2,1,0:T(8,128)(2,1)S(1)} async-done(((bf16[8,81,256]{2,1,0:T(8,128)(2,1)}), bf16[8,81,256]{2,1,0:T(8,128)(2,1)S(1)}, u32[]{:S(2)}, u32[]{:S(2)}) %all-to-all-start.2) | async-done | bytes 331808 | tf_op jit(solution)/shard_map/all_to_all | solution.py:186
  142.6 3.5 %all-to-all-start.5 = ((bf16[4,64,1024]{2,1,0:T(8,128)(2,1)}), bf16[4,64,1024]{2,1,0:T(8,128)(2,1)S(1)}, u32[]{:S(2)}, u32[]{:S(2)}) async-start(bf16[4,64,1024]{2,1,0:T(8,128)(2,1)} %broadcast_in_dim.36), calls=%async_computation.5 | async-start | bytes 1048576 | tf_op jit(solution)/shard_map/all_to_all | solution.py:54
  146.8 14.5 %all-to-all-done.5 = bf16[4,64,1024]{2,1,0:T(8,128)(2,1)S(1)} async-done(((bf16[4,64,1024]{2,1,0:T(8,128)(2,1)}), bf16[4,64,1024]{2,1,0:T(8,128)(2,1)S(1)}, u32[]{:S(2)}, u32[]{:S(2)}) %all-to-all-start.5) | async-done | bytes 524320 | tf_op jit(solution)/shard_map/all_to_all | solution.py:54
  161.3 1.8 broadcast_in_dim.35
  163.1 4.1 %all-to-all-start.3 = ((bf16[4,64,1024]{2,1,0:T(8,128)(2,1)}), bf16[4,64,1024]{2,1,0:T(8,128)(2,1)}, u32[]{:S(2)}, u32[]{:S(2)}) async-start(bf16[4,64,1024]{2,1,0:T(8,128)(2,1)} %broadcast_in_dim.35), calls=%async_computation.3 | async-start | bytes 1048576 | tf_op jit(solution)/shard_map/all_to_all | solution.py:54
  167.3 1.7 copy.75
  170.6 11.1 %all-to-all-done.3 = bf16[4,64,1024]{2,1,0:T(8,128)(2,1)} async-done(((bf16[4,64,1024]{2,1,0:T(8,128)(2,1)}), bf16[4,64,1024]{2,1,0:T(8,128)(2,1)}, u32[]{:S(2)}, u32[]{:S(2)}) %all-to-all-start.3) | async-done | bytes 524320 | tf_op jit(solution)/shard_map/all_to_all | solution.py:54
  186.2 1.2 broadcast_select_fusion.1
  187.7 1.3 broadcast_select_fusion.3
  190.4 4.2 %all-to-all-start.6 = ((bf16[4,98,1024]{2,1,0:T(8,128)(2,1)}), bf16[4,98,1024]{2,1,0:T(8,128)(2,1)}, u32[]{:S(2)}, u32[]{:S(2)}) async-start(bf16[4,98,1024]{2,1,0:T(8,128)(2,1)} %pad_maximum_fusion), calls=%async_computation.6 | async-start | bytes 1703936 | tf_op jit(solution)/shard_map/all_to_all | solution.py:207
  194.6 1.1 fusion.6
  195.8 11.4 %all-to-all-done.6 = bf16[4,98,1024]{2,1,0:T(8,128)(2,1)} async-done(((bf16[4,98,1024]{2,1,0:T(8,128)(2,1)}), bf16[4,98,1024]{2,1,0:T(8,128)(2,1)}, u32[]{:S(2)}, u32[]{:S(2)}) %all-to-all-start.6) | async-done | bytes 802848 | tf_op jit(solution)/shard_map/all_to_all | solution.py:207
  207.2 1.3 convert_reduce_fusion
  (266 shorter events, 39.0 us)
Async XLA Ops:
  0.6 65.6 %copy-start = (bf16[1024,1024]{1,0:T(8,128)(2,1)S(1)}, bf16[1024,1024]{1,0:T(8,128)(2,1)}, u32[]{:S(2)}) copy-start(bf16[1024,1024]{1,0:T(8,128)(2,1)} %param.17) | copy-start | bytes 6291460
  0.6 20.6 %copy-start.13 = (f32[31,1024]{1,0:T(8,128)S(1)}, f32[31,1024]{1,0:T(8,128)}, u32[]{:S(2)}) copy-start(f32[31,1024]{1,0:T(8,128)} %param.15) | copy-start | bytes 380932
  3.3 42.2 %collective-permute-start.1 = (bf16[32,1,2048]{2,0,1:T(8,128)(2,1)}, bf16[32,1,2048]{2,0,1:T(8,128)(2,1)}, u32[]{:S(2)}, u32[]{:S(2)}) collective-permute-start(bf16[32,1,2048]{2,0,1:T(8,128)(2,1)} %get-tuple-element.89), channel_id=1, source_target_pairs={{1,0},{2,1},{3,2},{4,3},{5,4},{6,5},{7,6},{9,8},{10,9},{11,10},{12... | collective-permute-start | bytes 393224 | tf_op jit(solution)/shard_map/ppermute | solution.py:93
  4.6 40.9 %collective-permute-start = (bf16[32,1,2048]{2,0,1:T(8,128)(2,1)S(1)}, bf16[32,1,2048]{2,0,1:T(8,128)(2,1)}, u32[]{:S(2)}, u32[]{:S(2)}) collective-permute-start(bf16[32,1,2048]{2,0,1:T(8,128)(2,1)S(1)} %get-tuple-element.88), channel_id=1, source_target_pairs={{0,1},{1,2},{2,3},{3,4},{4,5},{5,6},{6,7},{8,9},{9,10},{10,11},{11... | collective-permute-start | bytes 393224 | tf_op jit(solution)/shard_map/ppermute | solution.py:92
  13.3 19.6 %all-to-all-start = ((bf16[64,8,2,192]{3,0,2,1:T(8,128)(2,1)}), bf16[64,8,2,192]{3,0,2,1:T(8,128)(2,1)S(1)}, u32[]{:S(2)}, u32[]{:S(2)}) async-start(bf16[64,8,2,192]{3,0,2,1:T(8,128)(2,1)} %copy.62), calls=%async_computation | async-start | bytes 1048576 | tf_op jit(solution)/shard_map/all_to_all | solution.py:86
  36.2 10.3 %copy-start.75 = (pred[128]{0:T(512)(128)(4,1)S(1)}, pred[128]{0:T(512)(128)(4,1)}, u32[]{:S(2)}) copy-start(pred[128]{0:T(512)(128)(4,1)} %get-tuple-element.71) | copy-start | bytes 388
  41.4 12.5 %all-to-all-start.1 = ((bf16[8,128,128]{1,2,0:T(8,128)(2,1)}), bf16[8,128,128]{1,2,0:T(8,128)(2,1)}, u32[]{:S(2)}, u32[]{:S(2)}) async-start(bf16[8,128,128]{1,2,0:T(8,128)(2,1)} %constant_dynamic-update-slice_fusion.2), calls=%async_computation.1 | async-start | bytes 524288 | tf_op jit(solution)/shard_map/all_to_all | solution.py:112
  46.8 13.9 %copy-start.73 = (f32[1024]{0:T(1024)S(1)}, f32[1024]{0:T(1024)}, u32[]{:S(2)}) copy-start(f32[1024]{0:T(1024)} %param.13) | copy-start | bytes 12292
  53.9 71.6 %all-to-all-start.4 = ((bf16[8,64,128]{2,1,0:T(8,128)(2,1)}), bf16[8,64,128]{2,1,0:T(8,128)(2,1)}, u32[]{:S(2)}, u32[]{:S(2)}) async-start(bf16[8,64,128]{2,1,0:T(8,128)(2,1)} %copy.74), calls=%async_computation.4 | async-start | bytes 262144 | tf_op jit(solution)/shard_map/all_to_all | solution.py:115
  58.1 3.6 %copy-start.1 = (bf16[1024,2048]{1,0:T(8,128)(2,1)S(1)}, bf16[1024,2048]{1,0:T(8,128)(2,1)}, u32[]{:S(2)}) copy-start(bf16[1024,2048]{1,0:T(8,128)(2,1)} %param.14) | copy-start | bytes 12582916
  61.7 1.7 copy-start.74
  62.5 1.1 copy-start.14
  62.5 1.1 copy-start.15
  62.5 1.1 copy-start.16
  62.5 1.1 copy-start.17
  62.5 1.1 copy-start.18
  62.5 1.1 copy-start.19
  62.5 1.1 copy-start.20
  62.5 1.1 copy-start.21
  63.9 1.4 copy-start.71
  113.9 2.8 %copy-start.2 = (bf16[1024,2048]{1,0:T(8,128)(2,1)S(1)}, bf16[1024,2048]{1,0:T(8,128)(2,1)}, u32[]{:S(2)}) copy-start(bf16[1024,2048]{1,0:T(8,128)(2,1)} %param.14) | copy-start | bytes 12582916
  113.9 2.8 %copy-start.7 = (f32[128,1,1024]{2,0,1:T(8,128)S(1)}, f32[128,1,1024]{2,0,1:T(8,128)}, u32[]{:S(2)}) copy-start(f32[128,1,1024]{2,0,1:T(8,128)} %get-tuple-element.73) | copy-start | bytes 1572868
  116.7 1.8 copy-start.72
  116.7 1.9 copy-start.9
  116.7 1.9 copy-start.69
  116.7 1.9 copy-start.70
  116.8 1.9 copy-start.68
  116.8 1.9 copy-start.67
  116.8 1.9 copy-start.66
  116.8 2.0 copy-start.65
  116.8 2.0 copy-start.64
  116.8 2.0 copy-start.63
  116.8 2.0 copy-start.62
  116.8 2.0 copy-start.61
  116.8 2.1 copy-start.60
  116.9 2.1 copy-start.58
  116.9 2.1 copy-start.59
  116.9 2.1 copy-start.57
  116.9 2.1 %copy-start.56 = (bf16[1,2,2,4,2,32]{5,4,3,2,1,0:T(2,128)(2,1)S(1)}, bf16[1,2,2,4,2,32]{5,4,3,2,1,0:T(2,128)(2,1)}, u32[]{:S(2)}) copy-start(bf16[1,2,2,4,2,32]{5,4,3,2,1,0:T(2,128)(2,1)} %stack.153) | copy-start | bytes 6148
  116.9 2.1 %copy-start.55 = (bf16[1,2,2,4,2,32]{5,4,3,2,1,0:T(2,128)(2,1)S(1)}, bf16[1,2,2,4,2,32]{5,4,3,2,1,0:T(2,128)(2,1)}, u32[]{:S(2)}) copy-start(bf16[1,2,2,4,2,32]{5,4,3,2,1,0:T(2,128)(2,1)} %stack.154) | copy-start | bytes 6148
  116.9 2.2 %copy-start.54 = (bf16[1,2,2,4,2,32]{5,4,3,2,1,0:T(2,128)(2,1)S(1)}, bf16[1,2,2,4,2,32]{5,4,3,2,1,0:T(2,128)(2,1)}, u32[]{:S(2)}) copy-start(bf16[1,2,2,4,2,32]{5,4,3,2,1,0:T(2,128)(2,1)} %stack.155) | copy-start | bytes 6148
  116.9 2.2 %copy-start.53 = (bf16[1,2,2,4,2,32]{5,4,3,2,1,0:T(2,128)(2,1)S(1)}, bf16[1,2,2,4,2,32]{5,4,3,2,1,0:T(2,128)(2,1)}, u32[]{:S(2)}) copy-start(bf16[1,2,2,4,2,32]{5,4,3,2,1,0:T(2,128)(2,1)} %stack.156) | copy-start | bytes 6148
  116.9 2.2 %copy-start.52 = (bf16[1,2,2,4,2,32]{5,4,3,2,1,0:T(2,128)(2,1)S(1)}, bf16[1,2,2,4,2,32]{5,4,3,2,1,0:T(2,128)(2,1)}, u32[]{:S(2)}) copy-start(bf16[1,2,2,4,2,32]{5,4,3,2,1,0:T(2,128)(2,1)} %stack.157) | copy-start | bytes 6148
  116.9 2.2 %copy-start.51 = (bf16[1,2,2,4,2,32]{5,4,3,2,1,0:T(2,128)(2,1)S(1)}, bf16[1,2,2,4,2,32]{5,4,3,2,1,0:T(2,128)(2,1)}, u32[]{:S(2)}) copy-start(bf16[1,2,2,4,2,32]{5,4,3,2,1,0:T(2,128)(2,1)} %stack.158) | copy-start | bytes 6148
  116.9 2.2 %copy-start.49 = (bf16[1,2,2,4,2,32]{5,4,3,2,1,0:T(2,128)(2,1)S(1)}, bf16[1,2,2,4,2,32]{5,4,3,2,1,0:T(2,128)(2,1)}, u32[]{:S(2)}) copy-start(bf16[1,2,2,4,2,32]{5,4,3,2,1,0:T(2,128)(2,1)} %stack.159) | copy-start | bytes 6148
  117.0 2.3 %copy-start.50 = (bf16[1,2,2,4,2,32]{5,4,3,2,1,0:T(2,128)(2,1)S(1)}, bf16[1,2,2,4,2,32]{5,4,3,2,1,0:T(2,128)(2,1)}, u32[]{:S(2)}) copy-start(bf16[1,2,2,4,2,32]{5,4,3,2,1,0:T(2,128)(2,1)} %stack.160) | copy-start | bytes 6148
  117.0 2.3 %copy-start.48 = (bf16[1,2,2,4,2,32]{5,4,3,2,1,0:T(2,128)(2,1)S(1)}, bf16[1,2,2,4,2,32]{5,4,3,2,1,0:T(2,128)(2,1)}, u32[]{:S(2)}) copy-start(bf16[1,2,2,4,2,32]{5,4,3,2,1,0:T(2,128)(2,1)} %stack.161) | copy-start | bytes 6148
  117.0 2.3 %copy-start.47 = (bf16[1,2,2,4,2,32]{5,4,3,2,1,0:T(2,128)(2,1)S(1)}, bf16[1,2,2,4,2,32]{5,4,3,2,1,0:T(2,128)(2,1)}, u32[]{:S(2)}) copy-start(bf16[1,2,2,4,2,32]{5,4,3,2,1,0:T(2,128)(2,1)} %stack.162) | copy-start | bytes 6148
  117.0 2.3 %copy-start.46 = (bf16[1,2,2,4,2,32]{5,4,3,2,1,0:T(2,128)(2,1)S(1)}, bf16[1,2,2,4,2,32]{5,4,3,2,1,0:T(2,128)(2,1)}, u32[]{:S(2)}) copy-start(bf16[1,2,2,4,2,32]{5,4,3,2,1,0:T(2,128)(2,1)} %stack.163) | copy-start | bytes 6148
  117.0 2.3 %copy-start.45 = (bf16[1,2,2,4,2,32]{5,4,3,2,1,0:T(2,128)(2,1)S(1)}, bf16[1,2,2,4,2,32]{5,4,3,2,1,0:T(2,128)(2,1)}, u32[]{:S(2)}) copy-start(bf16[1,2,2,4,2,32]{5,4,3,2,1,0:T(2,128)(2,1)} %stack.164) | copy-start | bytes 6148
  117.0 2.3 %copy-start.44 = (bf16[1,2,2,4,2,32]{5,4,3,2,1,0:T(2,128)(2,1)S(1)}, bf16[1,2,2,4,2,32]{5,4,3,2,1,0:T(2,128)(2,1)}, u32[]{:S(2)}) copy-start(bf16[1,2,2,4,2,32]{5,4,3,2,1,0:T(2,128)(2,1)} %stack.165) | copy-start | bytes 6148
  117.0 2.4 %copy-start.43 = (bf16[1,2,2,4,2,32]{5,4,3,2,1,0:T(2,128)(2,1)S(1)}, bf16[1,2,2,4,2,32]{5,4,3,2,1,0:T(2,128)(2,1)}, u32[]{:S(2)}) copy-start(bf16[1,2,2,4,2,32]{5,4,3,2,1,0:T(2,128)(2,1)} %stack.166) | copy-start | bytes 6148
  117.0 2.4 %copy-start.41 = (bf16[1,2,2,4,2,32]{5,4,3,2,1,0:T(2,128)(2,1)S(1)}, bf16[1,2,2,4,2,32]{5,4,3,2,1,0:T(2,128)(2,1)}, u32[]{:S(2)}) copy-start(bf16[1,2,2,4,2,32]{5,4,3,2,1,0:T(2,128)(2,1)} %stack.167) | copy-start | bytes 6148
  117.0 2.4 %copy-start.42 = (bf16[1,2,2,4,2,32]{5,4,3,2,1,0:T(2,128)(2,1)S(1)}, bf16[1,2,2,4,2,32]{5,4,3,2,1,0:T(2,128)(2,1)}, u32[]{:S(2)}) copy-start(bf16[1,2,2,4,2,32]{5,4,3,2,1,0:T(2,128)(2,1)} %stack.168) | copy-start | bytes 6148
  124.7 21.3 %copy-start.5 = (bf16[128,1,1024]{2,0,1:T(8,128)(2,1)S(1)}, bf16[128,1,1024]{2,0,1:T(8,128)(2,1)}, u32[]{:S(2)}) copy-start(bf16[128,1,1024]{2,0,1:T(8,128)(2,1)} %copy-done.4) | copy-start | bytes 786436
  125.5 16.2 %all-to-all-start.2 = ((bf16[8,81,256]{2,1,0:T(8,128)(2,1)}), bf16[8,81,256]{2,1,0:T(8,128)(2,1)S(1)}, u32[]{:S(2)}, u32[]{:S(2)}) async-start(bf16[8,81,256]{2,1,0:T(8,128)(2,1)} %pad_maximum_fusion.2), calls=%async_computation.2 | async-start | bytes 720896 | tf_op jit(solution)/shard_map/all_to_all | solution.py:186
  142.6 18.7 %all-to-all-start.5 = ((bf16[4,64,1024]{2,1,0:T(8,128)(2,1)}), bf16[4,64,1024]{2,1,0:T(8,128)(2,1)S(1)}, u32[]{:S(2)}, u32[]{:S(2)}) async-start(bf16[4,64,1024]{2,1,0:T(8,128)(2,1)} %broadcast_in_dim.36), calls=%async_computation.5 | async-start | bytes 1048576 | tf_op jit(solution)/shard_map/all_to_all | solution.py:54
  146.8 38.6 %slice-start = ((bf16[8,81,256]{2,1,0:T(8,128)(2,1)}), bf16[8,64,256]{2,1,0:T(8,128)(2,1)S(1)}, s32[]{:S(2)}) async-start(bf16[8,81,256]{2,1,0:T(8,128)(2,1)} %copy-done.6), calls=%async_computation.7 | async-start | bytes 524288 | tf_op jit(solution)/shard_map/slice | solution.py:187
  163.1 18.6 %all-to-all-start.3 = ((bf16[4,64,1024]{2,1,0:T(8,128)(2,1)}), bf16[4,64,1024]{2,1,0:T(8,128)(2,1)}, u32[]{:S(2)}, u32[]{:S(2)}) async-start(bf16[4,64,1024]{2,1,0:T(8,128)(2,1)} %broadcast_in_dim.35), calls=%async_computation.3 | async-start | bytes 1048576 | tf_op jit(solution)/shard_map/all_to_all | solution.py:54
  167.2 19.0 %collective-permute-start.3 = (bf16[256,1024]{1,0:T(8,128)(2,1)S(1)}, bf16[256,1024]{1,0:T(8,128)(2,1)}, u32[]{:S(2)}, u32[]{:S(2)}) collective-permute-start(bf16[256,1024]{1,0:T(8,128)(2,1)S(1)} %bitcast.146), channel_id=1, source_target_pairs={{0,8},{8,0},{1,9},{9,1},{2,10},{10,2},{3,11},{11,3},{4,12},{12,4},... | collective-permute-start | bytes 1572872 | tf_op jit(solution)/shard_map/ppermute | solution.py:56
  181.7 6.0 %collective-permute-start.2 = (bf16[256,1024]{1,0:T(8,128)(2,1)}, bf16[256,1024]{1,0:T(8,128)(2,1)}, u32[]{:S(2)}, u32[]{:S(2)}) collective-permute-start(bf16[256,1024]{1,0:T(8,128)(2,1)} %bitcast.66), channel_id=1, source_target_pairs={{0,8},{8,0},{1,9},{9,1},{2,10},{10,2},{3,11},{11,3},{4,12},{12,4},... | collective-permute-start | bytes 1572872 | tf_op jit(solution)/shard_map/ppermute | solution.py:56
  186.2 1.2 copy-start.12
  187.3 1.6 copy-start.11
  190.4 16.7 %all-to-all-start.6 = ((bf16[4,98,1024]{2,1,0:T(8,128)(2,1)}), bf16[4,98,1024]{2,1,0:T(8,128)(2,1)}, u32[]{:S(2)}, u32[]{:S(2)}) async-start(bf16[4,98,1024]{2,1,0:T(8,128)(2,1)} %pad_maximum_fusion), calls=%async_computation.6 | async-start | bytes 1703936 | tf_op jit(solution)/shard_map/all_to_all | solution.py:207
  (24 other events, 26.1 us)

commit v2 on v1

--- a/solution.py
+++ b/solution.py
@@ -1,6 +1,10 @@
+import functools
+
 import jax
 import jax.numpy as jnp
 from jax import lax
+from jax.experimental import pallas as pl
+from jax.experimental.pallas import tpu as pltpu
 from jax.sharding import Mesh, PartitionSpec as P
 
 HEADS = 16
@@ -13,6 +17,9 @@
 CTX = ("chi", "clo")
 FIRST = ("dlo", "chi")
 SECOND = ("dhi", "clo")
+
+SMEM = pl.BlockSpec(memory_space=pltpu.SMEM)
+VMEM = pl.BlockSpec(memory_space=pltpu.VMEM)
 
 
 def normalize(values):
@@ -56,6 +63,546 @@
     other = lax.ppermute(line, "dlo", [(0, 1), (1, 0)])
     first = lax.axis_index("dlo") == 0
     return jnp.concatenate([jnp.where(first, line, other), jnp.where(first, other, line)], axis=0)
+
+
+def params():
+    return pltpu.CompilerParams(vmem_limit_bytes=40 * 1024 * 1024)
+
+
+def struct(shape, dtype):
+    return jax.ShapeDtypeStruct(shape, dtype)
+
+
+def split_kernel(proj_ref, out_ref, sems):
+    count, _, span = out_ref.shape
+    copies = [
+        pltpu.make_async_copy(proj_ref.at[:, pl.ds(i * span, span)], out_ref.at[i], sems.at[i])
+        for i in range(count)
+    ]
+    for copy in copies:
+        copy.start()
+    for copy in copies:
+        copy.wait()
+
+
+def split_heads(proj, count):
+    rows, cols = proj.shape
+    return pl.pallas_call(
+        split_kernel,
+        out_shape=struct((count, rows, cols // count), proj.dtype),
+        in_specs=[pl.BlockSpec(memory_space=pl.ANY)],
+        out_specs=pl.BlockSpec(memory_space=pl.ANY),
+        scratch_shapes=[pltpu.SemaphoreType.DMA((count,))],
+        compiler_params=params(),
+        name="split_heads",
+    )(proj)
+
+
+def edge_kernel(res_ref, grad_ref, low_ref, high_ref, sems):
+    rows, width = res_ref.shape
+    copies = []
+    for i, (source, lanes) in enumerate(((res_ref, 0), (grad_ref, width))):
+        copies.append(
+            pltpu.make_async_copy(
+                source.at[pl.ds(0, MARGIN)], low_ref.at[:, pl.ds(lanes, width)], sems.at[2 * i]
+            )
+        )
+        copies.append(
+            pltpu.make_async_copy(
+                source.at[pl.ds(rows - MARGIN, MARGIN)],
+                high_ref.at[:, pl.ds(lanes, width)],
+                sems.at[2 * i + 1],
+            )
+        )
+    for copy in copies:
+        copy.start()
+    for copy in copies:
+        copy.wait()
+
+
+def edges(res, grad):
+    shape = struct((MARGIN, 2 * res.shape[1]), res.dtype)
+    spec = pl.BlockSpec(memory_space=pl.ANY)
+    return pl.pallas_call(
+        edge_kernel,
+        out_shape=(shape, shape),
+        in_specs=[spec, spec],
+        out_specs=(spec, spec),
+        scratch_shapes=[pltpu.SemaphoreType.DMA((4,))],
+        compiler_params=params(),
+        name="edges",
+    )(res, grad)
+
+
+def attend_kernel(head_size, frames, scalar_ref, qkv_ref, out_ref):
+    length = qkv_ref.shape[0]
+    count = qkv_ref.shape[1] // (3 * head_size)
+    ctx, wide, _ = out_ref.shape
+    allowed = lax.broadcasted_iota(jnp.int32, (length, length), 1) < scalar_ref[0]
+    outs = []
+    for m in range(count):
+        base = 3 * head_size * m
+        query = qkv_ref[:, base : base + head_size]
+        key = qkv_ref[:, base + head_size : base + 2 * head_size]
+        value = qkv_ref[:, base + 2 * head_size : base + 3 * head_size]
+        scores = (
+            lax.dot_general(
+                query, key, (((1,), (1,)), ((), ())), preferred_element_type=jnp.float32
+            )
+            * head_size ** (-0.5)
+        )
+        scores = jnp.where(allowed, scores, -jnp.inf)
+        raised = jnp.exp(scores - jnp.max(scores, axis=-1, keepdims=True))
+        weights = raised * (1.0 / jnp.sum(raised, axis=-1, keepdims=True))
+        outs.append(
+            jnp.dot(weights.astype(jnp.bfloat16), value, preferred_element_type=jnp.float32)
+        )
+    context = jnp.concatenate(outs, axis=1).astype(jnp.bfloat16)
+    for i in range(ctx):
+        low = max(i * frames - MARGIN, 0)
+        high = min(i * frames - MARGIN + wide, length)
+        at = low - (i * frames - MARGIN)
+        out_ref[i, at : at + high - low, :] = context[low:high]
+        if at > 0:
+            out_ref[i, :at, :] = jnp.zeros((at, context.shape[1]), context.dtype)
+        if at + high - low < wide:
+            rest = wide - (at + high - low)
+            out_ref[i, wide - rest :, :] = jnp.zeros((rest, context.shape[1]), context.dtype)
+
+
+def attend_windows(scalars, qkv, head_size, frames, ctx):
+    wide = frames + 2 * MARGIN
+    return pl.pallas_call(
+        functools.partial(attend_kernel, head_size, frames),
+        out_shape=struct((ctx, wide, qkv.shape[1] // 3), jnp.bfloat16),
+        in_specs=[SMEM, VMEM],
+        out_specs=VMEM,
+        compiler_params=params(),
+        name="attend",
+    )(scalars, qkv)
+
+
+def cot_kernel(scalar_ref, grad_ref, low_ref, high_ref, weight_ref, act_ref, cols_ref):
+    frames, width = grad_ref.shape
+    edge = MARGIN // 2
+    whole = jnp.concatenate(
+        [low_ref[edge:, width:], grad_ref[...], high_ref[: MARGIN - edge, width:]], axis=0
+    )
+    near = whole.shape[0]
+    place = scalar_ref[1] - edge + lax.broadcasted_iota(jnp.int32, (near, width), 0)
+    valid = (place >= 0) & (place < scalar_ref[0])
+    whole = jnp.where(valid, whole.astype(jnp.float32), 0.0).astype(jnp.bfloat16)
+    act_ref[...] = lax.dot_general(
+        whole, weight_ref[...], (((1,), (1,)), ((), ())), preferred_element_type=jnp.float32
+    )
+    own = whole[edge : edge + frames]
+    count, _, span = cols_ref.shape
+    half = width // 2
+    piece = span // 2
+    for i in range(count):
+        cols_ref[i, :, :] = jnp.concatenate(
+            [own[:, i * piece : (i + 1) * piece], own[:, half + i * piece : half + (i + 1) * piece]],
+            axis=1,
+        )
+
+
+def cot_part(scalars, grad, low, high, weight, count):
+    frames, width = grad.shape
+    return pl.pallas_call(
+        cot_kernel,
+        out_shape=(
+            struct((frames + MARGIN, width), jnp.float32),
+            struct((count, frames, width // count), jnp.bfloat16),
+        ),
+        in_specs=[SMEM, VMEM, VMEM, VMEM, VMEM],
+        out_specs=(VMEM, VMEM),
+        compiler_params=params(),
+        name="cotangent",
+    )(scalars, grad, low, high, weight)
+
+
+def hidden_kernel(
+    context_ref, res_ref, low_ref, high_ref, weight_ref, gain_ref,
+    hidden_ref, normed_ref, scaled_ref, own_ref,
+):
+    frames, width = res_ref.shape
+    ctx, wide, _ = context_ref.shape
+    context = jnp.concatenate([context_ref[i] for i in range(ctx)], axis=1)
+    product = jnp.dot(context, weight_ref[...], preferred_element_type=jnp.float32)
+    step = 32
+    for at in range(0, wide, step):
+        if at < MARGIN:
+            res = low_ref[at : at + step, :width]
+        elif at < MARGIN + frames:
+            res = res_ref[at - MARGIN : at - MARGIN + step, :]
+        else:
+            res = high_ref[at - MARGIN - frames : at - MARGIN - frames + step, :width]
+        hidden = res.astype(jnp.float32) + product[at : at + step]
+        normed, _ = normalize(hidden)
+        scaled = (normed * gain_ref[...]).astype(jnp.bfloat16)
+        scaled_ref[at : at + step, :] = scaled
+        if MARGIN <= at < MARGIN + frames:
+            rows = slice(at - MARGIN, at - MARGIN + step)
+            hidden_ref[rows, :] = hidden
+            normed_ref[rows, :] = normed
+            own_ref[rows, :] = scaled
+
+
+def hidden_part(context, res, low, high, weight, gain):
+    frames, width = res.shape
+    wide = frames + 2 * MARGIN
+    return pl.pallas_call(
+        hidden_kernel,
+        out_shape=(
+            struct((frames, width), jnp.float32),
+            struct((frames, width), jnp.float32),
+            struct((wide, width), jnp.bfloat16),
+            struct((frames, width), jnp.bfloat16),
+        ),
+        in_specs=[VMEM] * 6,
+        out_specs=(VMEM,) * 4,
+        compiler_params=params(),
+        name="hidden",
+    )(context, res, low, high, weight, gain)
+
+
+def conv_kernel_body(
+    scalar_ref, scaled_ref, weight_ref, taps_ref, gain_ref,
+    act_ref, linear_ref, gate_ref, glu_ref, normed_ref, inverse_ref, conv_ref,
+):
+    frames, width = act_ref.shape
+    wide = scaled_ref.shape[0]
+    taps = taps_ref.shape[0]
+    half = (taps - 1) // 2
+    edge = MARGIN // 2
+    near = wide - 2 * edge
+    linear = jnp.dot(scaled_ref[...], weight_ref[:, :width], preferred_element_type=jnp.float32)
+    lifted = jnp.dot(scaled_ref[...], weight_ref[:, width:], preferred_element_type=jnp.float32)
+    step = 32
+    for at in range(0, wide, step):
+        place = scalar_ref[1] - MARGIN + at + lax.broadcasted_iota(jnp.int32, (step, width), 0)
+        valid = (place >= 0) & (place < scalar_ref[0])
+        gate = jax.nn.sigmoid(lifted[at : at + step])
+        value = linear[at : at + step]
+        glu = jnp.where(valid, value * gate, 0.0)
+        glu_ref[at : at + step, :] = glu.astype(jnp.bfloat16).astype(jnp.float32)
+        if MARGIN <= at < MARGIN + frames:
+            rows = slice(at - MARGIN, at - MARGIN + step)
+            linear_ref[rows, :] = value
+            gate_ref[rows, :] = gate
+
+    def lanes(i, carry):
+        cols = pl.ds(pl.multiple_of(i * 128, 128), 128)
+        block = glu_ref[:, cols]
+        total = jnp.zeros((near, 128), jnp.float32)
+        for shift in range(8):
+            moved = block if shift == 0 else pltpu.roll(block, wide - shift, 0)
+            for j in range(taps):
+                start = edge + j - half
+                if start % 8 == shift:
+                    total = total + taps_ref[j : j + 1, cols] * moved[start - shift : start - shift + near]
+        conv_ref[:, cols] = total
+        return carry
+
+    lax.fori_loop(0, width // 128, lanes, 0)
+    step = 16
+    for at in range(0, near, step):
+        normed, inverse = normalize(conv_ref[at : at + step, :])
+        normed_ref[at : at + step, :] = normed
+        inverse_ref[at : at + step, :] = jnp.broadcast_to(inverse, (step, 128))
+        if MARGIN - edge <= at < MARGIN - edge + frames:
+            pre = normed * gain_ref[...]
+            rows = slice(at - (MARGIN - edge), at - (MARGIN - edge) + step)
+            act_ref[rows, :] = (pre * jax.nn.sigmoid(pre)).astype(jnp.bfloat16)
+
+
+def conv_part(scalars, scaled, weight, taps, gain):
+    wide, width = scaled.shape
+    frames = wide - 2 * MARGIN
+    near = wide - MARGIN
+    f32 = jnp.float32
+    return pl.pallas_call(
+        conv_kernel_body,
+        out_shape=(
+            struct((frames, width), jnp.bfloat16),
+            struct((frames, width), f32),
+            struct((frames, width), f32),
+            struct((wide, width), f32),
+            struct((near, width), f32),
+            struct((near, 128), f32),
+        ),
+        in_specs=[SMEM] + [VMEM] * 4,
+        out_specs=(VMEM,) * 6,
+        scratch_shapes=[pltpu.VMEM((near, width), f32)],
+        compiler_params=params(),
+        name="conv",
+    )(scalars, scaled, weight, taps, gain)
+
+
+def back_kernel(
+    scalar_ref, act_grad_ref, cols_ref, hidden_ref, one_ref, activated_ref, linear_ref, gate_ref,
+    glu_ref, normed_ref, inverse_ref, taps_ref, gain_ref, down_ref, up_ref,
+    block_ref, message_ref, grad_ref, small_ref, lifted_ref,
+):
+    frames, width = hidden_ref.shape
+    near = normed_ref.shape[0]
+    wide = glu_ref.shape[0]
+    taps = taps_ref.shape[0]
+    half = (taps - 1) // 2
+    edge = MARGIN // 2
+    first = MARGIN - edge
+    gain = gain_ref[...]
+    step = 16
+    two = jnp.zeros((1, width), jnp.float32)
+    for at in range(0, near, step):
+        normed = normed_ref[at : at + step, :]
+        pre = normed * gain
+        gate = jax.nn.sigmoid(pre)
+        grad = act_grad_ref[at : at + step, :] * gate * (1.0 + pre * (1.0 - gate))
+        if first <= at < first + frames:
+            two = two + jnp.sum(grad * normed, axis=0, keepdims=True)
+        scaled = grad * gain
+        result = inverse_ref[at : at + step, 0:1] * (
+            scaled
+            - jnp.mean(scaled, axis=-1, keepdims=True)
+            - normed * jnp.mean(scaled * normed, axis=-1, keepdims=True)
+        )
+        grad_ref[at : at + step, :] = result.astype(jnp.bfloat16).astype(jnp.float32)
+    small_ref[32:, :] = jnp.zeros((16, width), jnp.float32)
+    small_ref[taps + 1 : taps + 2, :] = two
+
+    place = scalar_ref[1] + lax.broadcasted_iota(jnp.int32, (frames, 128), 0)
+    valid = place < scalar_ref[0]
+
+    def lanes(i, carry):
+        cols = pl.ds(pl.multiple_of(i * 128, 128), 128)
+        high = pl.ds(pl.multiple_of(i * 128 + width, 128), 128)
+        block = grad_ref[:, cols]
+        own = block[first : first + frames]
+        total = jnp.zeros((frames, 128), jnp.float32)
+        for shift in range(8):
+            moved = block if shift == 0 else pltpu.roll(block, near - shift, 0)
+            for j in range(taps):
+                start = first + half - j
+                if start % 8 == shift:
+                    total = total + taps_ref[j : j + 1, cols] * moved[start - shift : start - shift + frames]
+        block = glu_ref[:, cols]
+        for shift in range(8):
+            moved = block if shift == 0 else pltpu.roll(block, wide - shift, 0)
+            for j in range(taps):
+                start = MARGIN + j - half
+                if start % 8 == shift:
+                    small_ref[j : j + 1, cols] = jnp.sum(
+                        own * moved[start - shift : start - shift + frames], axis=0, keepdims=True
+                    )
+        total = jnp.where(valid, total, 0.0)
+        gate = gate_ref[:, cols]
+        linear_grad = (total * gate).astype(jnp.bfloat16)
+        gate_grad = (total * linear_ref[:, cols] * gate * (1.0 - gate)).astype(jnp.bfloat16)
+        lifted_ref[:, cols] = linear_grad
+        lifted_ref[:, high] = gate_grad
+        message_ref[i, :frames, :128] = linear_grad
+        message_ref[i, :frames, 128:256] = gate_grad
+        message_ref[i, :frames, 256:384] = cols_ref[i]
+        return carry
+
+    lax.fori_loop(0, width // 128, lanes, 0)
+    input_grad = lax.dot_general(
+        lifted_ref[...], up_ref[...], (((1,), (1,)), ((), ())), preferred_element_type=jnp.float32
+    )
+    small_ref[taps : taps + 1, :] = jnp.sum(input_grad * one_ref[...], axis=0, keepdims=True)
+    for i in range(width // 128):
+        for part in range(3):
+            rows = small_ref[part * 16 : (part + 1) * 16, :]
+            message_ref[i, frames:, part * 128 : (part + 1) * 128] = jnp.concatenate(
+                [rows[:, i * 64 : (i + 1) * 64], rows[:, (i + 8) * 64 : (i + 9) * 64]], axis=1
+            ).astype(jnp.bfloat16)
+    block_ref[...] = (
+        hidden_ref[...]
+        + jnp.dot(activated_ref[...], down_ref[...], preferred_element_type=jnp.float32)
+    ).astype(jnp.bfloat16)
+
+
+def back_part(*operands):
+    frames, width = operands[3].shape
+    near = frames + MARGIN
+    f32, bf = jnp.float32, jnp.bfloat16
+    return pl.pallas_call(
+        back_kernel,
+        out_shape=(
+            struct((frames, width), bf),
+            struct((width // 128, frames + 16, 384), bf),
+        ),
+        in_specs=[SMEM] + [VMEM] * 14,
+        out_specs=(VMEM,) * 2,
+        scratch_shapes=[
+            pltpu.VMEM((near, width), f32),
+            pltpu.VMEM((48, width), f32),
+            pltpu.VMEM((frames, 2 * width), bf),
+        ],
+        compiler_params=params(),
+        name="backward",
+    )(*operands)
+
+
+def product_kernel(count, scalar_ref, message_ref, *refs):
+    pieces = refs[: 4 * count]
+    parts_ref, cols_ref, one_ref, two_ref = refs[4 * count :]
+    frames, width = pieces[0].shape
+    core, line = scalar_ref[2], scalar_ref[3]
+    small = jnp.zeros((16, 384), jnp.float32)
+    for side in range(2):
+        for k in range(count):
+            at = (side * count + k) * frames
+            source = (core ^ side) * count + (line ^ k)
+            cols_ref[at : at + frames, :] = message_ref[source, :frames, :]
+            small = small + message_ref[source, frames:, :].astype(jnp.float32)
+            one_ref[at : at + frames, :] = pieces[side * count + k][...]
+            two_ref[at : at + frames, :] = pieces[2 * count + side * count + k][...]
+    turned = (((0,), (0,)), ((), ()))
+    up = lax.dot_general(
+        cols_ref[:, :256], one_ref[...], turned, preferred_element_type=jnp.float32
+    ).astype(jnp.bfloat16)
+    down = lax.dot_general(
+        cols_ref[:, 256:], two_ref[...], turned, preferred_element_type=jnp.float32
+    ).astype(jnp.bfloat16)
+    small = small.astype(jnp.bfloat16)
+    for s in range(4):
+        parts_ref[s, :64, :] = up[s * 64 : (s + 1) * 64]
+        parts_ref[s, 64:96, :] = down[s * 32 : (s + 1) * 32]
+        parts_ref[s, 96:, :384] = small
+        parts_ref[s, 96:, 384:] = jnp.zeros((16, width - 384), jnp.bfloat16)
+
+
+def product_part(scalars, message, pieces):
+    count = len(pieces) // 4
+    frames, width = pieces[0].shape
+    bf = jnp.bfloat16
+    rows = 2 * count * frames
+    return pl.pallas_call(
+        functools.partial(product_kernel, count),
+        out_shape=struct((4, 112, width), bf),
+        in_specs=[SMEM] + [VMEM] * (1 + len(pieces)),
+        out_specs=VMEM,
+        scratch_shapes=[
+            pltpu.VMEM((rows, 384), bf),
+            pltpu.VMEM((rows, width), bf),
+            pltpu.VMEM((rows, width), bf),
+        ],
+        compiler_params=params(),
+        name="products",
+    )(scalars, message, *pieces)
+
+
+def sum_kernel(taps, scalar_ref, parts_ref, up_ref, down_ref, kernel_ref, one_ref, two_ref):
+    total = parts_ref[0].astype(jnp.float32)
+    for s in range(1, parts_ref.shape[0]):
+        total = total + parts_ref[s].astype(jnp.float32)
+    up_ref[...] = total[:64]
+    down_ref[...] = total[64:96]
+    small = jnp.concatenate([total[96:112, :128], total[96:112, 128:256]], axis=0)
+    back = (128 - 32 * scalar_ref[4]) % 128
+    small = pltpu.roll(small, back, 1)
+    last = pltpu.roll(total[96:104, 256:384], back, 1)
+    kernel_ref[...] = jnp.transpose(small)[:32, :taps]
+    one_ref[...] = small[taps : taps + 1, :32]
+    two_ref[...] = last[:1, :32]
+
+
+def sum_part(scalars, parts, taps):
+    width = parts.shape[2]
+    f32 = jnp.float32
+    return pl.pallas_call(
+        functools.partial(sum_kernel, taps),
+        out_shape=(
+            struct((64, width), f32),
+            struct((32, width), f32),
+            struct((32, taps), f32),
+            struct((1, 32), f32),
+            struct((1, 32), f32),
+        ),
+        in_specs=[SMEM, VMEM],
+        out_specs=(VMEM,) * 5,
+        compiler_params=params(),
+        name="sums",
+    )(scalars, parts)
+
+
+def line_pieces(rows, chi):
+    pieces = [rows]
+    for k in range(1, chi):
+        pieces.append(lax.ppermute(rows, "chi", [(i, i ^ k) for i in range(chi)]))
+    return pieces
+
+
+def swapped(pieces):
+    return [lax.ppermute(piece, "dlo", [(0, 1), (1, 0)]) for piece in pieces]
+
+
+def small_device(
+    residual, projections, out_weight, gain_one, up_weight, conv_kernel, gain_two, down_weight,
+    lengths, out_grad,
+):
+    frames, _, width = residual.shape
+    taps = conv_kernel.shape[0]
+    chi, clo = lax.axis_size("chi"), lax.axis_size("clo")
+    ctx = chi * clo
+    head_size = width // HEADS
+    me = lax.axis_index(CTX)
+    second = lax.axis_index("dhi") * clo + lax.axis_index("clo")
+    scalars = jnp.stack(
+        [lengths[0], me * frames, lax.axis_index("dlo"), lax.axis_index("chi"), second]
+    ).astype(jnp.int32)
+    res = residual.reshape(frames, width)
+    grad = out_grad.reshape(frames, width)
+    gain_one = gain_one.reshape(1, width)
+    gain_two = gain_two.reshape(1, width)
+
+    qkv = split_heads(projections.reshape(frames, 3 * width), ctx)
+    qkv = lax.all_to_all(qkv, CTX, split_axis=0, concat_axis=0, tiled=True)
+    low, high = edges(res, grad)
+    up = [(i, i + 1) for i in range(ctx - 1)]
+    down = [(j, i) for i, j in up]
+    before = lax.ppermute(high, CTX, up)
+    after = lax.ppermute(low, CTX, down)
+    windows = attend_windows(scalars, qkv.reshape(ctx * frames, -1), head_size, frames, ctx)
+    windows = lax.all_to_all(windows, CTX, split_axis=0, concat_axis=0, tiled=True)
+    act_grad, cot_cols = cot_part(scalars, grad, before, after, down_weight, 2 * chi)
+
+    hidden, normed_one, scaled, scaled_own = hidden_part(
+        windows, res, before, after, out_weight, gain_one
+    )
+    ones = line_pieces(scaled_own, chi)
+    activated, linear, gate, glu, normed_two, inverse_two = conv_part(
+        scalars, scaled, up_weight, conv_kernel, gain_two
+    )
+    twos = line_pieces(activated, chi)
+    block_out, message = back_part(
+        scalars, act_grad, cot_cols, hidden, normed_one, activated, linear, gate,
+        glu, normed_two, inverse_two, conv_kernel, gain_two, down_weight, up_weight,
+    )
+    ones = ones + swapped(ones)
+    twos = twos + swapped(twos)
+    message = lax.all_to_all(message, FIRST, split_axis=0, concat_axis=0, tiled=True)
+    parts = product_part(scalars, message, ones + twos)
+    parts = lax.all_to_all(parts, SECOND, split_axis=0, concat_axis=0, tiled=True)
+    up_grad, down_grad, kernel_grad, one, two = sum_part(scalars, parts, taps)
+    return (
+        block_out.reshape(frames, 1, width), up_grad, down_grad, kernel_grad,
+        one.reshape(-1), two.reshape(-1),
+    )
+
+
+def fits(residual, conv_kernel, sizes):
+    dhi, dlo, chi, clo = sizes
+    frames, utter_count, width = residual.shape
+    return (
+        utter_count == 1
+        and frames == 64
+        and width == 1024
+        and conv_kernel.shape[0] == 31
+        and (dhi, dlo, chi, clo) == (2, 2, 4, 2)
+    )
 
 
 def on_device(
@@ -75,6 +622,19 @@
     kernel_len = conv_kernel.shape[0]
     half = (kernel_len - 1) // 2
     dhi, dlo, chi, clo = sizes = tuple(lax.axis_size(a) for a in ("dhi", "dlo", "chi", "clo"))
+    if fits(residual, conv_kernel, sizes):
+        return small_device(
+            residual,
+            projections,
+            out_weight,
+            gain_one,
+            up_weight,
+            conv_kernel,
+            gain_two,
+            down_weight,
+            lengths,
+            out_grad,
+        )
     ctx = chi * clo
     length = frames * ctx
     items = utter_count * HEADS // ctx

time: 213 us -> 115 us (0.54)
  local copies, waits for them, and re-layouts: 75.5 us -> 5.03 us
  waiting for transfers between devices: 63.9 us -> 40.6 us
  other arithmetic: 20.5 us -> 0 us
  Pallas kernels: 0 us -> 16.3 us
  blocking collectives: 0 us -> 15.9 us
  matrix products: 10.6 us -> 0 us
  starting transfers between devices: 37.9 us -> 34.7 us
    all_to_all x7 -> x3, waiting for transfers between devices: 63.9 us -> 10.9 us  [the longest x1 10.9 us: small_device(): qkv = lax.all_to_all(qkv, CTX, split_axis=0, concat_axis=0, tiled=True)]
    another operation x36 -> x1, local copies, waits for them, and re-layouts: 42.7 us -> 0.08 us  [small_device(): jnp.stack([lengths[0], me * frames, lax.axis_index('dlo'), lax.axis_index...]
    ppermute x4 -> x16, waiting for transfers between devices: 0.01 us -> 29.7 us  [the longest x6 23.1 us: line_pieces(): pieces.append(lax.ppermute(rows, 'chi', [(i, i ^ k) for i in range(chi)]))]
    pallas_call x0 -> x9, Pallas kernels: none -> 16.3 us  [the longest x1 5.2 us: back_part(): pl.pallas_call(back_kernel, out_shape=(struct((frames, width), bf), struc...]
    all_to_all x0 -> x1, blocking collectives: none -> 15.9 us  [small_device(): lax.all_to_all(parts, SECOND, split_axis=0, concat_axis=0, tiled=True)]
    all_to_all x7 -> x3, starting transfers between devices: 30.4 us -> 16.5 us  [the longest x1 7.29 us: small_device(): qkv = lax.all_to_all(qkv, CTX, split_axis=0, concat_axis=0, tiled=True)]
    ppermute x4 -> x16, starting transfers between devices: 7.5 us -> 18.1 us  [the longest x6 11.2 us: line_pieces(): pieces.append(lax.ppermute(rows, 'chi', [(i, i ^ k) for i in range(chi)]))]
    dot_general x8 -> x0, matrix products: 9.09 us -> none  [the longest x1 2.37 us: on_device(): jnp.einsum('fuc,cd->fud', context, out_weight, preferred_element_type=f32)]
  transfers between devices with their start and end apart: 11 -> 19, of which waited for: 6 -> 10; matrix products, arithmetic and copies ran while one was open for 44% -> 0% of each run, Pallas kernels for 0% -> 1%
where the time goes in v2:
time: 115 us; the launch traced here: 114 us
  waiting for transfers between devices  40.6 us (35%)
  starting transfers between devices  34.7 us (30%)
  Pallas kernels  16.3 us (14%)
  blocking collectives  15.9 us (14%)
  local copies, waits for them, and re-layouts  5.03 us (4%)
  between operations  1.5 us (1%)
    ppermute x6, waiting for transfers between devices, line_pieces(): pieces.append(lax.ppermute(rows, 'chi', [(i, i ^ k) for i in range(chi)]))  23.1 us
    all_to_all x1, blocking collectives, small_device(): lax.all_to_all(parts, SECOND, split_axis=0, concat_axis=0, tiled=True)  15.9 us
    ppermute x6, starting transfers between devices, line_pieces(): pieces.append(lax.ppermute(rows, 'chi', [(i, i ^ k) for i in range(chi)]))  11.2 us
    all_to_all x1, waiting for transfers between devices, small_device(): qkv = lax.all_to_all(qkv, CTX, split_axis=0, concat_axis=0, tiled=True)  10.9 us
    all_to_all x1, starting transfers between devices, small_device(): qkv = lax.all_to_all(qkv, CTX, split_axis=0, concat_axis=0, tiled=True)  7.29 us
    all_to_all x1, starting transfers between devices, small_device(): lax.all_to_all(message, FIRST, split_axis=0, concat_axis=0, tiled=True)  5.63 us
    pallas_call x1, Pallas kernels, back_part(): pl.pallas_call(back_kernel, out_shape=(struct((frames, width), bf), struc...  5.2 us
    unnamed x20, local copies, waits for them, and re-layouts  4.94 us
  transfers between devices with their start and end apart: 19, of which 10 were waited for; matrix products, arithmetic and copies ran while one was open for 0% of the time, Pallas kernels for 1%

profile of v2, /device:TPU:0, one launch (start us, length us, event | category | flops | bytes accessed | tf_op | source)
XLA Modules:
  0.0 114.1 jit_solution(18320616666872776013)
XLA Ops:
  0.6 0.0 copy-start.5
  0.6 0.0 copy-start.6
  0.7 0.0 copy-start.2
  0.7 0.0 copy-start.7
  0.7 1.1 copy-done.7
  1.8 0.8 split_heads.1
  2.6 7.3 %all-to-all-start = ((bf16[8,64,384]{2,1,0:T(8,128)(2,1)}), bf16[8,64,384]{2,1,0:T(8,128)(2,1)S(1)}, u32[]{:S(2)}, u32[]{:S(2)}) async-start(bf16[8,64,384]{2,1,0:T(8,128)(2,1)} %split_heads.1), calls=%async_computation | async-start | bytes 786432 | tf_op jit(solution)/shard_map/all_to_all | solution.py:562
  10.6 0.1 stack.19.scalar_ref
  10.7 10.9 %all-to-all-done = bf16[8,64,384]{2,1,0:T(8,128)(2,1)S(1)} async-done(((bf16[8,64,384]{2,1,0:T(8,128)(2,1)}), bf16[8,64,384]{2,1,0:T(8,128)(2,1)S(1)}, u32[]{:S(2)}, u32[]{:S(2)}) %all-to-all-start) | async-done | bytes 393248 | tf_op jit(solution)/shard_map/all_to_all | solution.py:562
  21.6 2.9 %attend.1 = bf16[8,128,128]{2,1,0:T(8,128)(2,1)} custom-call(s32[5]{0:T(128)S(1)} %stack.19.scalar_ref, bf16[512,384]{1,0:T(8,128)(2,1)S(1)} %bitcast.13), custom_call_target="tpu_custom_call" | custom-call | tf_op jit(solution)/shard_map/attend/pallas_call | solution.py:175
  24.5 3.6 %all-to-all-start.1 = ((bf16[8,128,128]{2,1,0:T(8,128)(2,1)}), bf16[8,128,128]{2,1,0:T(8,128)(2,1)S(1)}, u32[]{:S(2)}, u32[]{:S(2)}) async-start(bf16[8,128,128]{2,1,0:T(8,128)(2,1)} %attend.1), calls=%async_computation.1 | async-start | bytes 524288 | tf_op jit(solution)/shard_map/all_to_all | solution.py:569
  28.1 0.0 copy-done.5
  28.1 0.0 copy-done.6
  28.1 0.1 edges.1
  28.3 3.9 %collective-permute-start = (bf16[32,2048]{1,0:T(8,128)(2,1)S(1)}, bf16[32,2048]{1,0:T(8,128)(2,1)S(1)}, u32[]{:S(2)}, u32[]{:S(2)}) collective-permute-start(bf16[32,2048]{1,0:T(8,128)(2,1)S(1)} %get-tuple-element.27), channel_id=1, source_target_pairs={{0,1},{1,2},{2,3},{3,4},{4,5},{5,6},{6,7},{8,9},{9,10},{10,11},{11... | collective-permute-start | bytes 393224 | tf_op jit(solution)/shard_map/ppermute | solution.py:566
  32.2 0.0 copy-start.4
  32.2 0.0 copy-start.8
  32.2 1.4 %collective-permute-start.1 = (bf16[32,2048]{1,0:T(8,128)(2,1)S(1)}, bf16[32,2048]{1,0:T(8,128)(2,1)S(1)}, u32[]{:S(2)}, u32[]{:S(2)}) collective-permute-start(bf16[32,2048]{1,0:T(8,128)(2,1)S(1)} %get-tuple-element.28), channel_id=1, source_target_pairs={{1,0},{2,1},{3,2},{4,3},{5,4},{6,5},{7,6},{9,8},{10,9},{11,10},{12... | collective-permute-start | bytes 393224 | tf_op jit(solution)/shard_map/ppermute | solution.py:567
  33.6 1.6 %collective-permute-done.low_ref = bf16[32,2048]{1,0:T(8,128)(2,1)S(1)} collective-permute-done((bf16[32,2048]{1,0:T(8,128)(2,1)S(1)}, bf16[32,2048]{1,0:T(8,128)(2,1)S(1)}, u32[]{:S(2)}, u32[]{:S(2)}) %collective-permute-start) | collective-permute-done | bytes 131104 | tf_op jit(solution)/shard_map/ppermute | solution.py:566
  35.3 3.9 %collective-permute-done.1.high_ref = bf16[32,2048]{1,0:T(8,128)(2,1)S(1)} collective-permute-done((bf16[32,2048]{1,0:T(8,128)(2,1)S(1)}, bf16[32,2048]{1,0:T(8,128)(2,1)S(1)}, u32[]{:S(2)}, u32[]{:S(2)}) %collective-permute-start.1) | collective-permute-done | bytes 131104 | tf_op jit(solution)/shard_map/ppermute | solution.py:567
  39.2 1.3 %cotangent.1 = (f32[96,1024]{1,0:T(8,128)S(1)}, bf16[8,64,128]{2,1,0:T(8,128)(2,1)S(1)}) custom-call(s32[5]{0:T(128)S(1)} %stack.19.scalar_ref, bf16[64,1024]{1,0:T(8,128)(2,1)S(1)} %bitcast.15, bf16[32,2048]{1,0:T(8,128)(2,1)S(1)} %collective-permute-done.low_ref, bf16[32,2048]{1,0:T(8,128)(2,1)S(1)} %collective-permute-done.1.high_ref, ...), custom_call_target="tpu_custom_call" | custom-call | tf_op jit(solution)/shard_map/cotangent/pallas_call | solution.py:211
  40.5 0.0 all-to-all-done.1.context_ref
  40.5 0.0 copy-start.3
  40.6 1.6 %copy-done.3 = bf16[1024,1024]{1,0:T(8,128)(2,1)S(1)} copy-done((bf16[1024,1024]{1,0:T(8,128)(2,1)S(1)}, bf16[1024,1024]{1,0:T(8,128)(2,1)}, u32[]{:S(2)}) %copy-start.3) | copy-done | bytes 2097176
  42.1 0.7 hidden.1
  42.8 0.0 copy-done.4
  42.8 0.0 copy-done.8
  42.8 0.0 copy-start
  42.8 2.2 %copy-done = bf16[1024,2048]{1,0:T(8,128)(2,1)S(1)} copy-done((bf16[1024,2048]{1,0:T(8,128)(2,1)S(1)}, bf16[1024,2048]{1,0:T(8,128)(2,1)}, u32[]{:S(2)}) %copy-start) | copy-done | bytes 4194328
  45.0 2.8 %conv.1 = (bf16[64,1024]{1,0:T(8,128)(2,1)S(1)}, f32[64,1024]{1,0:T(8,128)S(1)}, f32[64,1024]{1,0:T(8,128)S(1)}, f32[128,1024]{1,0:T(8,128)S(1)}, f32[96,1024]{1,0:T(8,128)S(1)}, /*index=5*/f32[96,128]{1,0:T(8,128)S(1)}) custom-call(s32[5]{0:T(128)S(1)} %stack.19.scalar_ref, bf16[128,1024]{1,0:T(8,128)(2,1)S(1)} %get-tuple-element.33.scaled_ref, ...), custom_call_target="tpu_custom_call" | custom-call | tf_op jit(solution)/shard_map/conv/pallas_call | solution.py:324
  47.8 5.2 %backward.1 = (bf16[64,1024]{1,0:T(8,128)(2,1)}, bf16[8,80,384]{2,1,0:T(8,128)(2,1)}) custom-call(s32[5]{0:T(128)S(1)} %stack.19.scalar_ref, f32[96,1024]{1,0:T(8,128)S(1)} %get-tuple-element.29.act_grad_ref, bf16[8,64,128]{2,1,0:T(8,128)(2,1)S(1)} %get-tuple-element.30.cols_ref, f32[64,1024]{1,0:T(8,128)S(1)} %get-tuple-element.31.hidden_ref, ...), custom_call_target="tpu_custom_call" | custom-call | tf_op jit(solution)/shard_map/backward/pallas_call | solution.py:430
  53.0 5.6 %all-to-all-start.2 = ((bf16[8,80,384]{2,1,0:T(8,128)(2,1)}), bf16[8,80,384]{2,1,0:T(8,128)(2,1)S(1)}, u32[]{:S(2)}, u32[]{:S(2)}) async-start(bf16[8,80,384]{2,1,0:T(8,128)(2,1)} %get-tuple-element.41), calls=%async_computation.2 | async-start | bytes 983040 | tf_op jit(solution)/shard_map/all_to_all | solution.py:586
  58.6 2.0 %collective-permute-start.2 = (bf16[64,1024]{1,0:T(8,128)(2,1)S(1)}, bf16[64,1024]{1,0:T(8,128)(2,1)S(1)}, u32[]{:S(2)}, u32[]{:S(2)}) collective-permute-start(bf16[64,1024]{1,0:T(8,128)(2,1)S(1)} %get-tuple-element.42.refs_0_), channel_id=1, source_target_pairs={{0,2},{2,0},{4,6},{6,4},{1,3},{3,1},{5,7},{7,5},{8,10},{10,8},{12,... | collective-permute-start | bytes 393224 | tf_op jit(solution)/shard_map/ppermute | solution.py:534
  60.6 2.4 %collective-permute-start.3 = (bf16[64,1024]{1,0:T(8,128)(2,1)S(1)}, bf16[64,1024]{1,0:T(8,128)(2,1)S(1)}, u32[]{:S(2)}, u32[]{:S(2)}) collective-permute-start(bf16[64,1024]{1,0:T(8,128)(2,1)S(1)} %get-tuple-element.42.refs_0_), channel_id=1, source_target_pairs={{0,4},{2,6},{4,0},{6,2},{1,5},{3,7},{5,1},{7,3},{8,12},{10,14},{12... | collective-permute-start | bytes 393224 | tf_op jit(solution)/shard_map/ppermute | solution.py:534
  63.0 0.0 collective-permute-start.4
  63.1 0.0 collective-permute-start.5
  63.1 1.1 collective-permute-start.9
  64.1 6.6 %collective-permute-done.2.refs_1_ = bf16[64,1024]{1,0:T(8,128)(2,1)S(1)} collective-permute-done((bf16[64,1024]{1,0:T(8,128)(2,1)S(1)}, bf16[64,1024]{1,0:T(8,128)(2,1)S(1)}, u32[]{:S(2)}, u32[]{:S(2)}) %collective-permute-start.2) | collective-permute-done | bytes 131104 | tf_op jit(solution)/shard_map/ppermute | solution.py:534
  70.7 4.7 %collective-permute-start.10 = (bf16[64,1024]{1,0:T(8,128)(2,1)S(1)}, bf16[64,1024]{1,0:T(8,128)(2,1)S(1)}, u32[]{:S(2)}, u32[]{:S(2)}) collective-permute-start(bf16[64,1024]{1,0:T(8,128)(2,1)S(1)} %get-tuple-element.34.activated_ref.refs_8_), channel_id=1, source_target_pairs={{0,4},{2,6},{4,0},{6,2},{1,5},{3,7},{5,1},{7,3},{8,12},{10,14},{12... | collective-permute-start | bytes 393224 | tf_op jit(solution)/shard_map/ppermute | solution.py:534
  75.4 6.8 %collective-permute-done.3.refs_2_ = bf16[64,1024]{1,0:T(8,128)(2,1)S(1)} collective-permute-done((bf16[64,1024]{1,0:T(8,128)(2,1)S(1)}, bf16[64,1024]{1,0:T(8,128)(2,1)S(1)}, u32[]{:S(2)}, u32[]{:S(2)}) %collective-permute-start.3) | collective-permute-done | bytes 131104 | tf_op jit(solution)/shard_map/ppermute | solution.py:534
  82.2 0.9 collective-permute-start.11
  83.1 0.0 collective-permute-done.4.refs_3_
  83.1 0.0 collective-permute-start.12
  83.2 0.0 collective-permute-done.5.refs_4_
  83.2 0.5 collective-permute-start.6
  83.7 0.0 collective-permute-done.9.refs_9_
  83.7 0.1 collective-permute-start.7
  83.7 9.7 %collective-permute-done.10.refs_10_ = bf16[64,1024]{1,0:T(8,128)(2,1)S(1)} collective-permute-done((bf16[64,1024]{1,0:T(8,128)(2,1)S(1)}, bf16[64,1024]{1,0:T(8,128)(2,1)S(1)}, u32[]{:S(2)}, u32[]{:S(2)}) %collective-permute-start.10) | collective-permute-done | bytes 131104 | tf_op jit(solution)/shard_map/ppermute | solution.py:534
  93.5 0.0 collective-permute-start.8
  93.5 0.0 collective-permute-done.11.refs_11_
  93.5 0.5 collective-permute-start.13
  94.0 0.0 collective-permute-done.12.refs_12_
  94.0 0.1 collective-permute-start.14
  94.0 0.0 collective-permute-done.6.refs_5_
  94.0 0.4 collective-permute-start.15
  94.5 0.0 collective-permute-done.7.refs_6_
  94.5 0.3 collective-permute-done.8.refs_7_
  94.8 0.2 collective-permute-done.13.refs_13_
  95.0 0.3 collective-permute-done.14.refs_14_
  95.3 0.2 collective-permute-done.15.refs_15_
  95.5 0.0 all-to-all-done.2.message_ref
  95.5 1.2 %products.1 = bf16[4,112,1024]{2,1,0:T(8,128)(2,1)S(1)} custom-call(s32[5]{0:T(128)S(1)} %stack.19.scalar_ref, bf16[8,80,384]{2,1,0:T(8,128)(2,1)S(1)} %all-to-all-done.2.message_ref, bf16[64,1024]{1,0:T(8,128)(2,1)S(1)} %get-tuple-element.42.refs_0_, bf16[64,1024]{1,0:T(8,128)(2,1)S(1)} %collective-permute-done.2.refs_1_, ...), custom_call_target="tpu_custom_call" | custom-call | tf_op jit(solution)/shard_map/products/pallas_call | solution.py:482
  96.7 15.9 %all_to_all.20.parts_ref = bf16[4,112,1024]{2,1,0:T(8,128)(2,1)S(1)} all-to-all(bf16[4,112,1024]{2,1,0:T(8,128)(2,1)S(1)} %products.1), channel_id=1, replica_groups=mesh['dhi'=2,'dlo'=2,'chi'=4,'clo'=2] {'dhi','clo'}, dimensions={0} | all-to-all | bytes 1835008 | tf_op jit(solution)/shard_map/all_to_all | solution.py:588
  112.6 1.4 %sums.1 = (f32[64,1024]{1,0:T(8,128)}, f32[32,1024]{1,0:T(8,128)}, f32[32,31]{1,0:T(8,128)}, f32[1,32]{1,0:T(1,128)}, f32[1,32]{1,0:T(1,128)}) custom-call(s32[5]{0:T(128)S(1)} %stack.19.scalar_ref, bf16[4,112,1024]{2,1,0:T(8,128)(2,1)S(1)} %all_to_all.20.parts_ref), custom_call_target="tpu_custom_call" | custom-call | tf_op jit(solution)/shard_map/sums/pallas_call | solution.py:515
  (5 shorter events, 0.0 us)
Async XLA Ops:
  0.6 27.5 %copy-start.5 = (bf16[64,1,1024]{2,0,1:T(8,128)(2,1)S(1)}, bf16[64,1,1024]{2,0,1:T(8,128)(2,1)}, u32[]{:S(2)}) copy-start(bf16[64,1,1024]{2,0,1:T(8,128)(2,1)} %param.19) | copy-start | bytes 393220
  0.6 27.5 %copy-start.6 = (bf16[64,1,1024]{2,0,1:T(8,128)(2,1)S(1)}, bf16[64,1,1024]{2,0,1:T(8,128)(2,1)}, u32[]{:S(2)}) copy-start(bf16[64,1,1024]{2,0,1:T(8,128)(2,1)} %param.10) | copy-start | bytes 393220
  0.7 38.6 %copy-start.2 = (bf16[1024,1024]{1,0:T(8,128)(2,1)S(1)}, bf16[1024,1024]{1,0:T(8,128)(2,1)}, u32[]{:S(2)}) copy-start(bf16[1024,1024]{1,0:T(8,128)(2,1)} %down_ref.1) | copy-start | bytes 6291460
  0.7 1.1 %copy-start.7 = (bf16[64,1,3072]{2,0,1:T(8,128)(2,1)S(1)}, bf16[64,1,3072]{2,0,1:T(8,128)(2,1)}, u32[]{:S(2)}) copy-start(bf16[64,1,3072]{2,0,1:T(8,128)(2,1)} %param.11) | copy-start | bytes 1179652
  2.6 19.0 %all-to-all-start = ((bf16[8,64,384]{2,1,0:T(8,128)(2,1)}), bf16[8,64,384]{2,1,0:T(8,128)(2,1)S(1)}, u32[]{:S(2)}, u32[]{:S(2)}) async-start(bf16[8,64,384]{2,1,0:T(8,128)(2,1)} %split_heads.1), calls=%async_computation | async-start | bytes 786432 | tf_op jit(solution)/shard_map/all_to_all | solution.py:562
  9.9 30.6 %copy-start.9 = (f32[1024]{0:T(1024)S(1)}, f32[1024]{0:T(1024)}, u32[]{:S(2)}) copy-start(f32[1024]{0:T(1024)} %param.13) | copy-start | bytes 12292
  24.5 16.0 %all-to-all-start.1 = ((bf16[8,128,128]{2,1,0:T(8,128)(2,1)}), bf16[8,128,128]{2,1,0:T(8,128)(2,1)S(1)}, u32[]{:S(2)}, u32[]{:S(2)}) async-start(bf16[8,128,128]{2,1,0:T(8,128)(2,1)} %attend.1), calls=%async_computation.1 | async-start | bytes 524288 | tf_op jit(solution)/shard_map/all_to_all | solution.py:569
  28.3 7.0 %collective-permute-start = (bf16[32,2048]{1,0:T(8,128)(2,1)S(1)}, bf16[32,2048]{1,0:T(8,128)(2,1)S(1)}, u32[]{:S(2)}, u32[]{:S(2)}) collective-permute-start(bf16[32,2048]{1,0:T(8,128)(2,1)S(1)} %get-tuple-element.27), channel_id=1, source_target_pairs={{0,1},{1,2},{2,3},{3,4},{4,5},{5,6},{6,7},{8,9},{9,10},{10,11},{11... | collective-permute-start | bytes 393224 | tf_op jit(solution)/shard_map/ppermute | solution.py:566
  32.2 10.6 %copy-start.4 = (f32[31,1024]{1,0:T(8,128)S(1)}, f32[31,1024]{1,0:T(8,128)}, u32[]{:S(2)}) copy-start(f32[31,1024]{1,0:T(8,128)} %taps_ref.3) | copy-start | bytes 380932
  32.2 10.6 %copy-start.8 = (f32[1024]{0:T(1024)S(1)}, f32[1024]{0:T(1024)}, u32[]{:S(2)}) copy-start(f32[1024]{0:T(1024)} %param.16) | copy-start | bytes 12292
  32.2 7.0 %collective-permute-start.1 = (bf16[32,2048]{1,0:T(8,128)(2,1)S(1)}, bf16[32,2048]{1,0:T(8,128)(2,1)S(1)}, u32[]{:S(2)}, u32[]{:S(2)}) collective-permute-start(bf16[32,2048]{1,0:T(8,128)(2,1)S(1)} %get-tuple-element.28), channel_id=1, source_target_pairs={{1,0},{2,1},{3,2},{4,3},{5,4},{6,5},{7,6},{9,8},{10,9},{11,10},{12... | collective-permute-start | bytes 393224 | tf_op jit(solution)/shard_map/ppermute | solution.py:567
  40.5 1.6 %copy-start.3 = (bf16[1024,1024]{1,0:T(8,128)(2,1)S(1)}, bf16[1024,1024]{1,0:T(8,128)(2,1)}, u32[]{:S(2)}) copy-start(bf16[1024,1024]{1,0:T(8,128)(2,1)} %weight_ref.4) | copy-start | bytes 6291460
  42.8 2.2 %copy-start = (bf16[1024,2048]{1,0:T(8,128)(2,1)S(1)}, bf16[1024,2048]{1,0:T(8,128)(2,1)}, u32[]{:S(2)}) copy-start(bf16[1024,2048]{1,0:T(8,128)(2,1)} %up_ref.1) | copy-start | bytes 12582916
  45.0 2.8 %copy-start.1 = (bf16[1024,2048]{1,0:T(8,128)(2,1)S(1)}, bf16[1024,2048]{1,0:T(8,128)(2,1)}, u32[]{:S(2)}) copy-start(bf16[1024,2048]{1,0:T(8,128)(2,1)} %up_ref.1) | copy-start | bytes 12582916
  53.0 42.5 %all-to-all-start.2 = ((bf16[8,80,384]{2,1,0:T(8,128)(2,1)}), bf16[8,80,384]{2,1,0:T(8,128)(2,1)S(1)}, u32[]{:S(2)}, u32[]{:S(2)}) async-start(bf16[8,80,384]{2,1,0:T(8,128)(2,1)} %get-tuple-element.41), calls=%async_computation.2 | async-start | bytes 983040 | tf_op jit(solution)/shard_map/all_to_all | solution.py:586
  58.6 12.1 %collective-permute-start.2 = (bf16[64,1024]{1,0:T(8,128)(2,1)S(1)}, bf16[64,1024]{1,0:T(8,128)(2,1)S(1)}, u32[]{:S(2)}, u32[]{:S(2)}) collective-permute-start(bf16[64,1024]{1,0:T(8,128)(2,1)S(1)} %get-tuple-element.42.refs_0_), channel_id=1, source_target_pairs={{0,2},{2,0},{4,6},{6,4},{1,3},{3,1},{5,7},{7,5},{8,10},{10,8},{12,... | collective-permute-start | bytes 393224 | tf_op jit(solution)/shard_map/ppermute | solution.py:534
  60.6 21.6 %collective-permute-start.3 = (bf16[64,1024]{1,0:T(8,128)(2,1)S(1)}, bf16[64,1024]{1,0:T(8,128)(2,1)S(1)}, u32[]{:S(2)}, u32[]{:S(2)}) collective-permute-start(bf16[64,1024]{1,0:T(8,128)(2,1)S(1)} %get-tuple-element.42.refs_0_), channel_id=1, source_target_pairs={{0,4},{2,6},{4,0},{6,2},{1,5},{3,7},{5,1},{7,3},{8,12},{10,14},{12... | collective-permute-start | bytes 393224 | tf_op jit(solution)/shard_map/ppermute | solution.py:534
  63.0 20.1 %collective-permute-start.4 = (bf16[64,1024]{1,0:T(8,128)(2,1)S(1)}, bf16[64,1024]{1,0:T(8,128)(2,1)S(1)}, u32[]{:S(2)}, u32[]{:S(2)}) collective-permute-start(bf16[64,1024]{1,0:T(8,128)(2,1)S(1)} %get-tuple-element.42.refs_0_), channel_id=1, source_target_pairs={{0,6},{2,4},{4,2},{6,0},{1,7},{3,5},{5,3},{7,1},{8,14},{10,12},{12... | collective-permute-start | bytes 393224 | tf_op jit(solution)/shard_map/ppermute | solution.py:534
  63.1 20.1 %collective-permute-start.5 = (bf16[64,1024]{1,0:T(8,128)(2,1)S(1)}, bf16[64,1024]{1,0:T(8,128)(2,1)S(1)}, u32[]{:S(2)}, u32[]{:S(2)}) collective-permute-start(bf16[64,1024]{1,0:T(8,128)(2,1)S(1)} %get-tuple-element.42.refs_0_), channel_id=1, source_target_pairs={{0,8},{8,0},{1,9},{9,1},{2,10},{10,2},{3,11},{11,3},{4,12},{12,4},... | collective-permute-start | bytes 393224 | tf_op jit(solution)/shard_map/ppermute | solution.py:539
  63.1 20.6 %collective-permute-start.9 = (bf16[64,1024]{1,0:T(8,128)(2,1)S(1)}, bf16[64,1024]{1,0:T(8,128)(2,1)S(1)}, u32[]{:S(2)}, u32[]{:S(2)}) collective-permute-start(bf16[64,1024]{1,0:T(8,128)(2,1)S(1)} %get-tuple-element.34.activated_ref.refs_8_), channel_id=1, source_target_pairs={{0,2},{2,0},{4,6},{6,4},{1,3},{3,1},{5,7},{7,5},{8,10},{10,8},{12,... | collective-permute-start | bytes 393224 | tf_op jit(solution)/shard_map/ppermute | solution.py:534
  70.7 22.8 %collective-permute-start.10 = (bf16[64,1024]{1,0:T(8,128)(2,1)S(1)}, bf16[64,1024]{1,0:T(8,128)(2,1)S(1)}, u32[]{:S(2)}, u32[]{:S(2)}) collective-permute-start(bf16[64,1024]{1,0:T(8,128)(2,1)S(1)} %get-tuple-element.34.activated_ref.refs_8_), channel_id=1, source_target_pairs={{0,4},{2,6},{4,0},{6,2},{1,5},{3,7},{5,1},{7,3},{8,12},{10,14},{12... | collective-permute-start | bytes 393224 | tf_op jit(solution)/shard_map/ppermute | solution.py:534
  82.2 11.2 %collective-permute-start.11 = (bf16[64,1024]{1,0:T(8,128)(2,1)S(1)}, bf16[64,1024]{1,0:T(8,128)(2,1)S(1)}, u32[]{:S(2)}, u32[]{:S(2)}) collective-permute-start(bf16[64,1024]{1,0:T(8,128)(2,1)S(1)} %get-tuple-element.34.activated_ref.refs_8_), channel_id=1, source_target_pairs={{0,6},{2,4},{4,2},{6,0},{1,7},{3,5},{5,3},{7,1},{8,14},{10,12},{12... | collective-permute-start | bytes 393224 | tf_op jit(solution)/shard_map/ppermute | solution.py:534
  83.1 10.8 %collective-permute-start.12 = (bf16[64,1024]{1,0:T(8,128)(2,1)S(1)}, bf16[64,1024]{1,0:T(8,128)(2,1)S(1)}, u32[]{:S(2)}, u32[]{:S(2)}) collective-permute-start(bf16[64,1024]{1,0:T(8,128)(2,1)S(1)} %get-tuple-element.34.activated_ref.refs_8_), channel_id=1, source_target_pairs={{0,8},{8,0},{1,9},{9,1},{2,10},{10,2},{3,11},{11,3},{4,12},{12,4},... | collective-permute-start | bytes 393224 | tf_op jit(solution)/shard_map/ppermute | solution.py:539
  83.2 10.9 %collective-permute-start.6 = (bf16[64,1024]{1,0:T(8,128)(2,1)S(1)}, bf16[64,1024]{1,0:T(8,128)(2,1)S(1)}, u32[]{:S(2)}, u32[]{:S(2)}) collective-permute-start(bf16[64,1024]{1,0:T(8,128)(2,1)S(1)} %collective-permute-done.2.refs_1_), channel_id=1, source_target_pairs={{0,8},{8,0},{1,9},{9,1},{2,10},{10,2},{3,11},{11,3},{4,12},{12,4},... | collective-permute-start | bytes 393224 | tf_op jit(solution)/shard_map/ppermute | solution.py:539
  83.7 10.8 %collective-permute-start.7 = (bf16[64,1024]{1,0:T(8,128)(2,1)S(1)}, bf16[64,1024]{1,0:T(8,128)(2,1)S(1)}, u32[]{:S(2)}, u32[]{:S(2)}) collective-permute-start(bf16[64,1024]{1,0:T(8,128)(2,1)S(1)} %collective-permute-done.3.refs_2_), channel_id=1, source_target_pairs={{0,8},{8,0},{1,9},{9,1},{2,10},{10,2},{3,11},{11,3},{4,12},{12,4},... | collective-permute-start | bytes 393224 | tf_op jit(solution)/shard_map/ppermute | solution.py:539
  93.5 1.3 %collective-permute-start.8 = (bf16[64,1024]{1,0:T(8,128)(2,1)S(1)}, bf16[64,1024]{1,0:T(8,128)(2,1)S(1)}, u32[]{:S(2)}, u32[]{:S(2)}) collective-permute-start(bf16[64,1024]{1,0:T(8,128)(2,1)S(1)} %collective-permute-done.4.refs_3_), channel_id=1, source_target_pairs={{0,8},{8,0},{1,9},{9,1},{2,10},{10,2},{3,11},{11,3},{4,12},{12,4},... | collective-permute-start | bytes 393224 | tf_op jit(solution)/shard_map/ppermute | solution.py:539
  93.5 1.5 %collective-permute-start.13 = (bf16[64,1024]{1,0:T(8,128)(2,1)S(1)}, bf16[64,1024]{1,0:T(8,128)(2,1)S(1)}, u32[]{:S(2)}, u32[]{:S(2)}) collective-permute-start(bf16[64,1024]{1,0:T(8,128)(2,1)S(1)} %collective-permute-done.9.refs_9_), channel_id=1, source_target_pairs={{0,8},{8,0},{1,9},{9,1},{2,10},{10,2},{3,11},{11,3},{4,12},{12,4},... | collective-permute-start | bytes 393224 | tf_op jit(solution)/shard_map/ppermute | solution.py:539
  94.0 1.3 %collective-permute-start.14 = (bf16[64,1024]{1,0:T(8,128)(2,1)S(1)}, bf16[64,1024]{1,0:T(8,128)(2,1)S(1)}, u32[]{:S(2)}, u32[]{:S(2)}) collective-permute-start(bf16[64,1024]{1,0:T(8,128)(2,1)S(1)} %collective-permute-done.10.refs_10_), channel_id=1, source_target_pairs={{0,8},{8,0},{1,9},{9,1},{2,10},{10,2},{3,11},{11,3},{4,12},{12,4},... | collective-permute-start | bytes 393224 | tf_op jit(solution)/shard_map/ppermute | solution.py:539
  94.0 1.5 %collective-permute-start.15 = (bf16[64,1024]{1,0:T(8,128)(2,1)S(1)}, bf16[64,1024]{1,0:T(8,128)(2,1)S(1)}, u32[]{:S(2)}, u32[]{:S(2)}) collective-permute-start(bf16[64,1024]{1,0:T(8,128)(2,1)S(1)} %collective-permute-done.11.refs_11_), channel_id=1, source_target_pairs={{0,8},{8,0},{1,9},{9,1},{2,10},{10,2},{3,11},{11,3},{4,12},{12,4},... | collective-permute-start | bytes 393224 | tf_op jit(solution)/shard_map/ppermute | solution.py:539

commit v3 on v2

--- a/solution.py
+++ b/solution.py
@@ -20,6 +20,7 @@
 
 SMEM = pl.BlockSpec(memory_space=pltpu.SMEM)
 VMEM = pl.BlockSpec(memory_space=pltpu.VMEM)
+HBM = pl.BlockSpec(memory_space=pltpu.HBM)
 
 
 def normalize(values):
@@ -65,73 +66,88 @@
     return jnp.concatenate([jnp.where(first, line, other), jnp.where(first, other, line)], axis=0)
 
 
-def params():
-    return pltpu.CompilerParams(vmem_limit_bytes=40 * 1024 * 1024)
+def params(mebi=8):
+    return pltpu.CompilerParams(vmem_limit_bytes=mebi * 1024 * 1024)
 
 
 def struct(shape, dtype):
     return jax.ShapeDtypeStruct(shape, dtype)
 
 
-def split_kernel(proj_ref, out_ref, sems):
+def in_hbm(array):
+    return pltpu.with_memory_space_constraint(array, pltpu.HBM)
+
+
+def fetches(source, target, sems, parts):
+    copies = []
+    for i, part in enumerate(parts):
+        copies.append(pltpu.make_async_copy(source.at[part], target.at[part], sems.at[i]))
+        copies[-1].start()
+    return copies
+
+
+def split_kernel(proj_ref, out_ref, held_ref, sems):
     count, _, span = out_ref.shape
-    copies = [
-        pltpu.make_async_copy(proj_ref.at[:, pl.ds(i * span, span)], out_ref.at[i], sems.at[i])
-        for i in range(count)
-    ]
-    for copy in copies:
-        copy.start()
+    copies = []
+    for i in range(count):
+        copies.append(
+            pltpu.make_async_copy(
+                proj_ref.at[:, pl.ds(i * span, span)], held_ref.at[i], sems.at[0, i]
+            )
+        )
+        copies[-1].start()
+    sends = []
+    for i, copy in enumerate(copies):
+        copy.wait()
+        sends.append(pltpu.make_async_copy(held_ref.at[i], out_ref.at[i], sems.at[1, i]))
+        sends[-1].start()
+    for send in sends:
+        send.wait()
+
+
+def split_heads(proj, count):
+    rows, cols = proj.shape
+    shape = (count, rows, cols // count)
+    return pl.pallas_call(
+        split_kernel,
+        out_shape=struct(shape, proj.dtype),
+        in_specs=[HBM],
+        out_specs=HBM,
+        scratch_shapes=[pltpu.VMEM(shape, proj.dtype), pltpu.SemaphoreType.DMA((2, count))],
+        compiler_params=params(),
+        name="split_heads",
+    )(in_hbm(proj))
+
+
+def edge_kernel(res_ref, grad_ref, low_ref, high_ref, sems):
+    rows = res_ref.shape[0]
+    copies = []
+    for i, (source, at, count) in enumerate(
+        ((res_ref, 0, MARGIN), (grad_ref, MARGIN, MARGIN // 2))
+    ):
+        for j, (target, start) in enumerate(((high_ref, rows - count), (low_ref, 0))):
+            copies.append(
+                pltpu.make_async_copy(
+                    source.at[pl.ds(start, count)], target.at[pl.ds(at, count)], sems.at[i, j]
+                )
+            )
+            copies[-1].start()
     for copy in copies:
         copy.wait()
 
 
-def split_heads(proj, count):
-    rows, cols = proj.shape
-    return pl.pallas_call(
-        split_kernel,
-        out_shape=struct((count, rows, cols // count), proj.dtype),
-        in_specs=[pl.BlockSpec(memory_space=pl.ANY)],
-        out_specs=pl.BlockSpec(memory_space=pl.ANY),
-        scratch_shapes=[pltpu.SemaphoreType.DMA((count,))],
-        compiler_params=params(),
-        name="split_heads",
-    )(proj)
-
-
-def edge_kernel(res_ref, grad_ref, low_ref, high_ref, sems):
-    rows, width = res_ref.shape
-    copies = []
-    for i, (source, lanes) in enumerate(((res_ref, 0), (grad_ref, width))):
-        copies.append(
-            pltpu.make_async_copy(
-                source.at[pl.ds(0, MARGIN)], low_ref.at[:, pl.ds(lanes, width)], sems.at[2 * i]
-            )
-        )
-        copies.append(
-            pltpu.make_async_copy(
-                source.at[pl.ds(rows - MARGIN, MARGIN)],
-                high_ref.at[:, pl.ds(lanes, width)],
-                sems.at[2 * i + 1],
-            )
-        )
-    for copy in copies:
-        copy.start()
-    for copy in copies:
-        copy.wait()
-
-
 def edges(res, grad):
-    shape = struct((MARGIN, 2 * res.shape[1]), res.dtype)
+    shape = struct((MARGIN + MARGIN // 2, res.shape[1]), res.dtype)
     spec = pl.BlockSpec(memory_space=pl.ANY)
     return pl.pallas_call(
         edge_kernel,
         out_shape=(shape, shape),
-        in_specs=[spec, spec],
+        in_specs=[HBM, HBM],
         out_specs=(spec, spec),
-        scratch_shapes=[pltpu.SemaphoreType.DMA((4,))],
+        scratch_shapes=[pltpu.SemaphoreType.DMA((2, 2))],
         compiler_params=params(),
         name="edges",
-    )(res, grad)
+    )(in_hbm(res), in_hbm(grad))
 
 
 def attend_kernel(head_size, frames, scalar_ref, qkv_ref, out_ref):
@@ -177,134 +193,144 @@
         out_shape=struct((ctx, wide, qkv.shape[1] // 3), jnp.bfloat16),
         in_specs=[SMEM, VMEM],
         out_specs=VMEM,
-        compiler_params=params(),
+        compiler_params=params(16),
         name="attend",
     )(scalars, qkv)
 
 
-def cot_kernel(scalar_ref, grad_ref, low_ref, high_ref, weight_ref, act_ref, cols_ref):
+def cot_kernel(scalar_ref, grad_ref, low_ref, high_ref, weight_ref, *refs):
+    cols_refs, (act_ref, held_ref, weight_held_ref, sems) = refs[:4], refs[4:]
     frames, width = grad_ref.shape
+    copies = fetches(
+        weight_ref, weight_held_ref, sems, [pl.ds(i * 256, 256) for i in range(width // 256)]
+    )
     edge = MARGIN // 2
-    whole = jnp.concatenate(
-        [low_ref[edge:, width:], grad_ref[...], high_ref[: MARGIN - edge, width:]], axis=0
-    )
+    whole = jnp.concatenate([low_ref[MARGIN:, :], grad_ref[...], high_ref[MARGIN:, :]], axis=0)
     near = whole.shape[0]
     place = scalar_ref[1] - edge + lax.broadcasted_iota(jnp.int32, (near, width), 0)
     valid = (place >= 0) & (place < scalar_ref[0])
     whole = jnp.where(valid, whole.astype(jnp.float32), 0.0).astype(jnp.bfloat16)
-    act_ref[...] = lax.dot_general(
-        whole, weight_ref[...], (((1,), (1,)), ((), ())), preferred_element_type=jnp.float32
-    )
-    own = whole[edge : edge + frames]
-    count, _, span = cols_ref.shape
-    half = width // 2
-    piece = span // 2
-    for i in range(count):
-        cols_ref[i, :, :] = jnp.concatenate(
-            [own[:, i * piece : (i + 1) * piece], own[:, half + i * piece : half + (i + 1) * piece]],
+    cot = whole[edge : edge + frames]
+    count, _, span = held_ref.shape
+    piece = span // 4
+    for group in range(count):
+        high_bits, low_bit = group // 2, group % 2
+        held_ref[group, :, :] = jnp.concatenate(
+            [
+                cot[:, (8 * high_bits + 2 * z + low_bit) * piece :][:, :piece]
+                for z in range(4)
+            ],
             axis=1,
         )
-
-
-def cot_part(scalars, grad, low, high, weight, count):
+    dhi, dlo, clo = scalar_ref[5], scalar_ref[2], scalar_ref[6]
+    for k, cols_ref in enumerate(cols_refs):
+        for side in range(2):
+            group = ((dhi ^ (k // 2)) * 2 + (dlo ^ side)) * 2 + (clo ^ (k % 2))
+            cols_ref[:, side * span : (side + 1) * span] = held_ref[group]
+    for copy in copies:
+        copy.wait()
+    act_ref[...] = lax.dot_general(
+        whole, weight_held_ref[...], (((1,), (1,)), ((), ())), preferred_element_type=jnp.float32
+    )
+
+
+def cot_part(scalars, grad, low, high, weight):
     frames, width = grad.shape
+    cols = struct((frames, width // 4), grad.dtype)
     return pl.pallas_call(
         cot_kernel,
-        out_shape=(
-            struct((frames + MARGIN, width), jnp.float32),
-            struct((count, frames, width // count), jnp.bfloat16),
-        ),
-        in_specs=[SMEM, VMEM, VMEM, VMEM, VMEM],
-        out_specs=(VMEM, VMEM),
-        compiler_params=params(),
+        out_shape=(cols, cols, cols, cols, struct((frames + MARGIN, width), jnp.float32)),
+        in_specs=[SMEM, VMEM, VMEM, VMEM, HBM],
+        out_specs=(VMEM,) * 5,
+        scratch_shapes=[
+            pltpu.VMEM((8, frames, width // 8), grad.dtype),
+            pltpu.VMEM(weight.shape, weight.dtype),
+            pltpu.SemaphoreType.DMA((width // 256,)),
+        ],
+        compiler_params=params(12),
         name="cotangent",
-    )(scalars, grad, low, high, weight)
-
-
-def hidden_kernel(
-    context_ref, res_ref, low_ref, high_ref, weight_ref, gain_ref,
-    hidden_ref, normed_ref, scaled_ref, own_ref,
+    )(scalars, grad, low, high, in_hbm(weight))
+
+
+def forward_kernel(
+    scalar_ref, context_ref, res_ref, low_ref, high_ref, out_ref, gain_one_ref, weight_ref,
+    taps_ref, gain_ref, cols_own_ref, cols_y_ref, cols_x_ref, cols_xy_ref,
+    hidden_ref, one_ref, own_ref, act_ref, to_y_ref, to_x_ref, to_xy_ref, linear_ref, gate_ref, glu_ref,
+    normed_ref, inverse_ref, scaled_ref, conv_ref, out_held_ref, held_ref, res_held_ref, out_sems, sems, res_sems,
 ):
     frames, width = res_ref.shape
-    ctx, wide, _ = context_ref.shape
-    context = jnp.concatenate([context_ref[i] for i in range(ctx)], axis=1)
-    product = jnp.dot(context, weight_ref[...], preferred_element_type=jnp.float32)
+    ctx, wide, lanes = context_ref.shape
+    taps = taps_ref.shape[0]
+    half = (taps - 1) // 2
+    edge = MARGIN // 2
+    near = wide - 2 * edge
+    depth = 2 * lanes
+    res_copies = fetches(res_ref, res_held_ref, res_sems, [slice(None)])
+    out_copies = fetches(
+        out_ref, out_held_ref, out_sems, [pl.ds(i * depth, depth) for i in range(ctx // 2)]
+    )
+    span = 256
+    copies = fetches(
+        weight_ref, held_ref, sems, [pl.ds(i * span, span) for i in range(width // span)]
+    )
+    product = jnp.zeros((wide, width), jnp.float32)
+    for i, copy in enumerate(out_copies):
+        copy.wait()
+        product = product + jnp.dot(
+            jnp.concatenate([context_ref[2 * i], context_ref[2 * i + 1]], axis=1),
+            out_held_ref[i * depth : (i + 1) * depth, :],
+            preferred_element_type=jnp.float32,
+        )
+    res_copies[0].wait()
     step = 32
     for at in range(0, wide, step):
         if at < MARGIN:
-            res = low_ref[at : at + step, :width]
+            res = low_ref[at : at + step, :]
         elif at < MARGIN + frames:
-            res = res_ref[at - MARGIN : at - MARGIN + step, :]
+            res = res_held_ref[at - MARGIN : at - MARGIN + step, :]
         else:
-            res = high_ref[at - MARGIN - frames : at - MARGIN - frames + step, :width]
+            res = high_ref[at - MARGIN - frames : at - MARGIN - frames + step, :]
         hidden = res.astype(jnp.float32) + product[at : at + step]
         normed, _ = normalize(hidden)
-        scaled = (normed * gain_ref[...]).astype(jnp.bfloat16)
+        scaled = (normed * gain_one_ref[...]).astype(jnp.bfloat16)
         scaled_ref[at : at + step, :] = scaled
         if MARGIN <= at < MARGIN + frames:
             rows = slice(at - MARGIN, at - MARGIN + step)
             hidden_ref[rows, :] = hidden
-            normed_ref[rows, :] = normed
+            one_ref[rows, :] = normed
             own_ref[rows, :] = scaled
-
-
-def hidden_part(context, res, low, high, weight, gain):
-    frames, width = res.shape
-    wide = frames + 2 * MARGIN
-    return pl.pallas_call(
-        hidden_kernel,
-        out_shape=(
-            struct((frames, width), jnp.float32),
-            struct((frames, width), jnp.float32),
-            struct((wide, width), jnp.bfloat16),
-            struct((frames, width), jnp.bfloat16),
-        ),
-        in_specs=[VMEM] * 6,
-        out_specs=(VMEM,) * 4,
-        compiler_params=params(),
-        name="hidden",
-    )(context, res, low, high, weight, gain)
-
-
-def conv_kernel_body(
-    scalar_ref, scaled_ref, weight_ref, taps_ref, gain_ref,
-    act_ref, linear_ref, gate_ref, glu_ref, normed_ref, inverse_ref, conv_ref,
-):
-    frames, width = act_ref.shape
-    wide = scaled_ref.shape[0]
-    taps = taps_ref.shape[0]
-    half = (taps - 1) // 2
-    edge = MARGIN // 2
-    near = wide - 2 * edge
-    linear = jnp.dot(scaled_ref[...], weight_ref[:, :width], preferred_element_type=jnp.float32)
-    lifted = jnp.dot(scaled_ref[...], weight_ref[:, width:], preferred_element_type=jnp.float32)
-    step = 32
-    for at in range(0, wide, step):
-        place = scalar_ref[1] - MARGIN + at + lax.broadcasted_iota(jnp.int32, (step, width), 0)
-        valid = (place >= 0) & (place < scalar_ref[0])
-        gate = jax.nn.sigmoid(lifted[at : at + step])
-        value = linear[at : at + step]
-        glu = jnp.where(valid, value * gate, 0.0)
-        glu_ref[at : at + step, :] = glu.astype(jnp.bfloat16).astype(jnp.float32)
-        if MARGIN <= at < MARGIN + frames:
-            rows = slice(at - MARGIN, at - MARGIN + step)
-            linear_ref[rows, :] = value
-            gate_ref[rows, :] = gate
-
-    def lanes(i, carry):
-        cols = pl.ds(pl.multiple_of(i * 128, 128), 128)
-        block = glu_ref[:, cols]
-        total = jnp.zeros((near, 128), jnp.float32)
-        for shift in range(8):
-            moved = block if shift == 0 else pltpu.roll(block, wide - shift, 0)
-            for j in range(taps):
-                start = edge + j - half
-                if start % 8 == shift:
-                    total = total + taps_ref[j : j + 1, cols] * moved[start - shift : start - shift + near]
-        conv_ref[:, cols] = total
-        return carry
-
-    lax.fori_loop(0, width // 128, lanes, 0)
+    for copy in copies:
+        copy.wait()
+    place = scalar_ref[1] - MARGIN + lax.broadcasted_iota(jnp.int32, (wide, span), 0)
+    valid = (place >= 0) & (place < scalar_ref[0])
+    own = slice(MARGIN, MARGIN + frames)
+    for i in range(width // span):
+        cols = slice(i * span, (i + 1) * span)
+        linear = jnp.dot(scaled_ref[...], held_ref[:, cols], preferred_element_type=jnp.float32)
+        gate = jax.nn.sigmoid(
+            jnp.dot(
+                scaled_ref[...],
+                held_ref[:, width + i * span : width + (i + 1) * span],
+                preferred_element_type=jnp.float32,
+            )
+        )
+        glu = jnp.where(valid, linear * gate, 0.0).astype(jnp.bfloat16).astype(jnp.float32)
+        glu_ref[:, cols] = glu
+        linear_ref[:, cols] = linear[own]
+        gate_ref[:, cols] = gate[own]
+        for at in range(i * span, (i + 1) * span, 128):
+            lane = slice(at, at + 128)
+            block = glu[:, at - i * span : at - i * span + 128]
+            total = jnp.zeros((near, 128), jnp.float32)
+            for shift in range(8):
+                moved = block if shift == 0 else pltpu.roll(block, wide - shift, 0)
+                for j in range(taps):
+                    start = edge + j - half
+                    if start % 8 == shift:
+                        total = total + taps_ref[j : j + 1, lane] * moved[
+                            start - shift : start - shift + near
+                        ]
+            conv_ref[:, lane] = total
     step = 16
     for at in range(0, near, step):
         normed, inverse = normalize(conv_ref[at : at + step, :])
@@ -313,44 +339,69 @@
         if MARGIN - edge <= at < MARGIN - edge + frames:
             pre = normed * gain_ref[...]
             rows = slice(at - (MARGIN - edge), at - (MARGIN - edge) + step)
-            act_ref[rows, :] = (pre * jax.nn.sigmoid(pre)).astype(jnp.bfloat16)
-
-
-def conv_part(scalars, scaled, weight, taps, gain):
-    wide, width = scaled.shape
-    frames = wide - 2 * MARGIN
+            act = (pre * jax.nn.sigmoid(pre)).astype(jnp.bfloat16)
+            for ref in (act_ref, to_y_ref, to_x_ref, to_xy_ref):
+                ref[rows, :width] = act
+    act_ref[:, width:] = cols_own_ref[...]
+    to_y_ref[:, width:] = cols_y_ref[...]
+    to_x_ref[:, width:] = cols_x_ref[...]
+    to_xy_ref[:, width:] = cols_xy_ref[...]
+
+
+def forward_part(scalars, context, res, low, high, out_weight, gain_one, weight, taps, gain, cols):
+    frames, width = res.shape
+    ctx, wide, _ = context.shape
     near = wide - MARGIN
-    f32 = jnp.float32
+    f32, bf = jnp.float32, jnp.bfloat16
     return pl.pallas_call(
-        conv_kernel_body,
+        forward_kernel,
         out_shape=(
-            struct((frames, width), jnp.bfloat16),
+            struct((frames, width), f32),
+            struct((frames, width), f32),
+            struct((frames, width), bf),
+            struct((frames, width + width // 4), bf),
+            struct((frames, width + width // 4), bf),
+            struct((frames, width + width // 4), bf),
+            struct((frames, width + width // 4), bf),
             struct((frames, width), f32),
             struct((frames, width), f32),
             struct((wide, width), f32),
             struct((near, width), f32),
             struct((near, 128), f32),
         ),
-        in_specs=[SMEM] + [VMEM] * 4,
-        out_specs=(VMEM,) * 6,
-        scratch_shapes=[pltpu.VMEM((near, width), f32)],
-        compiler_params=params(),
-        name="conv",
-    )(scalars, scaled, weight, taps, gain)
+        in_specs=[SMEM, VMEM, HBM, VMEM, VMEM, HBM, VMEM, HBM] + [VMEM] * 6,
+        out_specs=(VMEM,) * 12,
+        scratch_shapes=[
+            pltpu.VMEM((wide, width), bf),
+            pltpu.VMEM((near, width), f32),
+            pltpu.VMEM(out_weight.shape, bf),
+            pltpu.VMEM(weight.shape, bf),
+            pltpu.VMEM(res.shape, bf),
+            pltpu.SemaphoreType.DMA((ctx // 2,)),
+            pltpu.SemaphoreType.DMA((width // 256,)),
+            pltpu.SemaphoreType.DMA((1,)),
+        ],
+        compiler_params=params(24),
+        name="forward",
+    )(
+        scalars, context, in_hbm(res), low, high, in_hbm(out_weight), gain_one, in_hbm(weight), taps, gain,
+        *cols,
+    )
 
 
 def back_kernel(
-    scalar_ref, act_grad_ref, cols_ref, hidden_ref, one_ref, activated_ref, linear_ref, gate_ref,
-    glu_ref, normed_ref, inverse_ref, taps_ref, gain_ref, down_ref, up_ref,
-    block_ref, message_ref, grad_ref, small_ref, lifted_ref,
+    scalar_ref, act_grad_ref, one_ref, linear_ref, gate_ref,
+    glu_ref, normed_ref, inverse_ref, taps_ref, gain_ref, up_ref,
+    message_ref, grad_ref, small_ref, lifted_ref, held_ref, sems,
 ):
-    frames, width = hidden_ref.shape
+    frames, width = one_ref.shape
     near = normed_ref.shape[0]
     wide = glu_ref.shape[0]
     taps = taps_ref.shape[0]
     half = (taps - 1) // 2
     edge = MARGIN // 2
     first = MARGIN - edge
+    copies = fetches(up_ref, held_ref, sems, [pl.ds(i * 256, 256) for i in range(width // 256)])
     gain = gain_ref[...]
     step = 16
     two = jnp.zeros((1, width), jnp.float32)
@@ -403,113 +454,180 @@
         lifted_ref[:, high] = gate_grad
         message_ref[i, :frames, :128] = linear_grad
         message_ref[i, :frames, 128:256] = gate_grad
-        message_ref[i, :frames, 256:384] = cols_ref[i]
         return carry
 
     lax.fori_loop(0, width // 128, lanes, 0)
+    for copy in copies:
+        copy.wait()
     input_grad = lax.dot_general(
-        lifted_ref[...], up_ref[...], (((1,), (1,)), ((), ())), preferred_element_type=jnp.float32
+        lifted_ref[...], held_ref[...], (((1,), (1,)), ((), ())), preferred_element_type=jnp.float32
     )
     small_ref[taps : taps + 1, :] = jnp.sum(input_grad * one_ref[...], axis=0, keepdims=True)
     for i in range(width // 128):
-        for part in range(3):
-            rows = small_ref[part * 16 : (part + 1) * 16, :]
+        for part in range(2):
+            rows = small_ref[part * 24 : (part + 1) * 24, :]
             message_ref[i, frames:, part * 128 : (part + 1) * 128] = jnp.concatenate(
                 [rows[:, i * 64 : (i + 1) * 64], rows[:, (i + 8) * 64 : (i + 9) * 64]], axis=1
             ).astype(jnp.bfloat16)
+
+
+def block_kernel(hidden_ref, activated_ref, down_ref, block_ref, held_ref, sems):
+    width = hidden_ref.shape[1]
+    copies = fetches(
+        down_ref, held_ref, sems, [pl.ds(i * 256, 256) for i in range(width // 256)]
+    )
+    for copy in copies:
+        copy.wait()
     block_ref[...] = (
         hidden_ref[...]
-        + jnp.dot(activated_ref[...], down_ref[...], preferred_element_type=jnp.float32)
+        + jnp.dot(
+            activated_ref[:, :width], held_ref[...], preferred_element_type=jnp.float32
+        )
     ).astype(jnp.bfloat16)
 
 
+def block_part(hidden, activated, down):
+    return pl.pallas_call(
+        block_kernel,
+        out_shape=struct(hidden.shape, jnp.bfloat16),
+        in_specs=[VMEM, VMEM, HBM],
+        out_specs=VMEM,
+        scratch_shapes=[
+            pltpu.VMEM(down.shape, down.dtype),
+            pltpu.SemaphoreType.DMA((down.shape[0] // 256,)),
+        ],
+        compiler_params=params(12),
+        name="block_out",
+    )(hidden, activated, in_hbm(down))
+
+
 def back_part(*operands):
-    frames, width = operands[3].shape
+    frames, width = operands[2].shape
     near = frames + MARGIN
     f32, bf = jnp.float32, jnp.bfloat16
     return pl.pallas_call(
         back_kernel,
-        out_shape=(
-            struct((frames, width), bf),
-            struct((width // 128, frames + 16, 384), bf),
-        ),
-        in_specs=[SMEM] + [VMEM] * 14,
-        out_specs=(VMEM,) * 2,
+        out_shape=struct((width // 128, frames + 24, 256), bf),
+        in_specs=[SMEM] + [VMEM] * 9 + [HBM],
+        out_specs=VMEM,
         scratch_shapes=[
             pltpu.VMEM((near, width), f32),
             pltpu.VMEM((48, width), f32),
             pltpu.VMEM((frames, 2 * width), bf),
+            pltpu.VMEM((width, 2 * width), bf),
+            pltpu.SemaphoreType.DMA((width // 256,)),
         ],
-        compiler_params=params(),
+        compiler_params=params(20),
         name="backward",
-    )(*operands)
-
-
-def product_kernel(count, scalar_ref, message_ref, *refs):
-    pieces = refs[: 4 * count]
-    parts_ref, cols_ref, one_ref, two_ref = refs[4 * count :]
-    frames, width = pieces[0].shape
+    )(*operands[:-1], in_hbm(operands[-1]))
+
+
+TURNED = (((0,), (0,)), ((), ()))
+
+
+def up_kernel(count, scalar_ref, message_ref, *refs):
+    parts_ref, cols_ref, one_ref = refs[2 * count :]
+    frames, width = refs[0].shape
     core, line = scalar_ref[2], scalar_ref[3]
-    small = jnp.zeros((16, 384), jnp.float32)
+    small = jnp.zeros((24, 256), jnp.float32)
     for side in range(2):
         for k in range(count):
             at = (side * count + k) * frames
             source = (core ^ side) * count + (line ^ k)
             cols_ref[at : at + frames, :] = message_ref[source, :frames, :]
+            one_ref[at : at + frames, :] = refs[side * count + k][...]
             small = small + message_ref[source, frames:, :].astype(jnp.float32)
-            one_ref[at : at + frames, :] = pieces[side * count + k][...]
-            two_ref[at : at + frames, :] = pieces[2 * count + side * count + k][...]
-    turned = (((0,), (0,)), ((), ()))
     up = lax.dot_general(
-        cols_ref[:, :256], one_ref[...], turned, preferred_element_type=jnp.float32
-    ).astype(jnp.bfloat16)
-    down = lax.dot_general(
-        cols_ref[:, 256:], two_ref[...], turned, preferred_element_type=jnp.float32
+        cols_ref[...], one_ref[...], TURNED, preferred_element_type=jnp.float32
     ).astype(jnp.bfloat16)
     small = small.astype(jnp.bfloat16)
     for s in range(4):
         parts_ref[s, :64, :] = up[s * 64 : (s + 1) * 64]
-        parts_ref[s, 64:96, :] = down[s * 32 : (s + 1) * 32]
-        parts_ref[s, 96:, :384] = small
-        parts_ref[s, 96:, 384:] = jnp.zeros((16, width - 384), jnp.bfloat16)
-
-
-def product_part(scalars, message, pieces):
-    count = len(pieces) // 4
+        for i in range(3):
+            parts_ref[s, 64:, i * 256 : (i + 1) * 256] = small[i * 8 : (i + 1) * 8]
+        parts_ref[s, 64:, 768:] = jnp.zeros((8, width - 768), jnp.bfloat16)
+
+
+def up_part(scalars, message, pieces):
+    count = len(pieces) // 2
     frames, width = pieces[0].shape
     bf = jnp.bfloat16
     rows = 2 * count * frames
     return pl.pallas_call(
-        functools.partial(product_kernel, count),
-        out_shape=struct((4, 112, width), bf),
-        in_specs=[SMEM] + [VMEM] * (1 + len(pieces)),
+        functools.partial(up_kernel, count),
+        out_shape=struct((4, 72, width), bf),
+        in_specs=[SMEM, VMEM] + [VMEM] * len(pieces),
         out_specs=VMEM,
+        scratch_shapes=[pltpu.VMEM((rows, 256), bf), pltpu.VMEM((rows, width), bf)],
+        compiler_params=params(12),
+        name="up_products",
+    )(scalars, message, *pieces)
+
+
+def down_kernel(scalar_ref, *refs):
+    count = (len(refs) - 3) // 3
+    pieces, outs = refs[: 2 * count], refs[2 * count : 3 * count]
+    cols_ref, rows_ref, total_ref = refs[3 * count :]
+    frames, width = pieces[0].shape[0], rows_ref.shape[1]
+    span = cols_ref.shape[1]
+    for i, piece in enumerate(pieces):
+        rows = slice(i * frames, (i + 1) * frames)
+        at = width + (i // count) * span
+        rows_ref[rows, :] = piece[:, :width]
+        cols_ref[rows, :] = piece[:, at : at + span]
+    total_ref[...] = lax.dot_general(
+        cols_ref[...], rows_ref[...], TURNED, preferred_element_type=jnp.float32
+    )
+    line = scalar_ref[3]
+    for k, out in enumerate(outs):
+        at = pl.multiple_of((line ^ k) * 32, 32)
+        out[...] = total_ref[pl.ds(at, 32), :].astype(jnp.bfloat16)
+
+
+def down_part(scalars, pieces, width):
+    count = len(pieces) // 2
+    frames = pieces[0].shape[0]
+    bf = jnp.bfloat16
+    rows = 2 * count * frames
+    return pl.pallas_call(
+        down_kernel,
+        out_shape=(struct((32, width), bf),) * count,
+        in_specs=[SMEM] + [VMEM] * (2 * count),
+        out_specs=(VMEM,) * count,
         scratch_shapes=[
-            pltpu.VMEM((rows, 384), bf),
+            pltpu.VMEM((rows, 128), bf),
             pltpu.VMEM((rows, width), bf),
-            pltpu.VMEM((rows, width), bf),
+            pltpu.VMEM((128, width), jnp.float32),
         ],
-        compiler_params=params(),
-        name="products",
-    )(scalars, message, *pieces)
-
-
-def sum_kernel(taps, scalar_ref, parts_ref, up_ref, down_ref, kernel_ref, one_ref, two_ref):
+        compiler_params=params(12),
+        name="down_products",
+    )(scalars, *pieces)
+
+
+def sum_kernel(taps, scalar_ref, parts_ref, *refs):
+    pieces, (up_ref, down_ref, kernel_ref, one_ref, two_ref) = refs[:4], refs[4:]
     total = parts_ref[0].astype(jnp.float32)
     for s in range(1, parts_ref.shape[0]):
         total = total + parts_ref[s].astype(jnp.float32)
     up_ref[...] = total[:64]
-    down_ref[...] = total[64:96]
-    small = jnp.concatenate([total[96:112, :128], total[96:112, 128:256]], axis=0)
-    back = (128 - 32 * scalar_ref[4]) % 128
-    small = pltpu.roll(small, back, 1)
-    last = pltpu.roll(total[96:104, 256:384], back, 1)
-    kernel_ref[...] = jnp.transpose(small)[:32, :taps]
+    down_ref[...] = (pieces[0][...].astype(jnp.float32) + pieces[1][...].astype(jnp.float32)) + (
+        pieces[2][...].astype(jnp.float32) + pieces[3][...].astype(jnp.float32)
+    )
+    small = jnp.concatenate(
+        [
+            total[64:72, i * 256 + part * 128 : i * 256 + part * 128 + 128]
+            for part in range(2)
+            for i in range(3)
+        ],
+        axis=0,
+    )
+    small = pltpu.roll(small, (128 - 32 * scalar_ref[4]) % 128, 1)
+    kernel_ref[...] = jnp.transpose(small[:32])[:32, :taps]
     one_ref[...] = small[taps : taps + 1, :32]
-    two_ref[...] = last[:1, :32]
-
-
-def sum_part(scalars, parts, taps):
+    two_ref[...] = small[taps + 1 : taps + 2, :32]
+
+
+def sum_part(scalars, parts, pieces, taps):
     width = parts.shape[2]
     f32 = jnp.float32
     return pl.pallas_call(
@@ -521,22 +639,20 @@
             struct((1, 32), f32),
             struct((1, 32), f32),
         ),
-        in_specs=[SMEM, VMEM],
+        in_specs=[SMEM] + [VMEM] * 5,
         out_specs=(VMEM,) * 5,
         compiler_params=params(),
         name="sums",
-    )(scalars, parts)
-
-
-def line_pieces(rows, chi):
-    pieces = [rows]
-    for k in range(1, chi):
-        pieces.append(lax.ppermute(rows, "chi", [(i, i ^ k) for i in range(chi)]))
-    return pieces
-
-
-def swapped(pieces):
-    return [lax.ppermute(piece, "dlo", [(0, 1), (1, 0)]) for piece in pieces]
+    )(scalars, parts, *pieces)
+
+
+def flipped(rows, axis, bit):
+    size = lax.axis_size(axis)
+    return lax.ppermute(rows, axis, [(i, i ^ bit) for i in range(size)])
+
+
+def with_swapped(pieces):
+    return list(pieces) + [flipped(piece, "dlo", 1) for piece in pieces]
 
 
 def small_device(
@@ -551,7 +667,10 @@
     me = lax.axis_index(CTX)
     second = lax.axis_index("dhi") * clo + lax.axis_index("clo")
     scalars = jnp.stack(
-        [lengths[0], me * frames, lax.axis_index("dlo"), lax.axis_index("chi"), second]
+        [
+            lengths[0], me * frames, lax.axis_index("dlo"), lax.axis_index("chi"), second,
+            lax.axis_index("dhi"), lax.axis_index("clo"),
+        ]
     ).astype(jnp.int32)
     res = residual.reshape(frames, width)
     grad = out_grad.reshape(frames, width)
@@ -565,28 +684,48 @@
     down = [(j, i) for i, j in up]
     before = lax.ppermute(high, CTX, up)
     after = lax.ppermute(low, CTX, down)
+    qkv, before, after = lax.optimization_barrier((qkv, before, after))
     windows = attend_windows(scalars, qkv.reshape(ctx * frames, -1), head_size, frames, ctx)
+    windows, before, after = lax.optimization_barrier((windows, before, after))
     windows = lax.all_to_all(windows, CTX, split_axis=0, concat_axis=0, tiled=True)
-    act_grad, cot_cols = cot_part(scalars, grad, before, after, down_weight, 2 * chi)
-
-    hidden, normed_one, scaled, scaled_own = hidden_part(
-        windows, res, before, after, out_weight, gain_one
-    )
-    ones = line_pieces(scaled_own, chi)
-    activated, linear, gate, glu, normed_two, inverse_two = conv_part(
-        scalars, scaled, up_weight, conv_kernel, gain_two
-    )
-    twos = line_pieces(activated, chi)
-    block_out, message = back_part(
-        scalars, act_grad, cot_cols, hidden, normed_one, activated, linear, gate,
-        glu, normed_two, inverse_two, conv_kernel, gain_two, down_weight, up_weight,
-    )
-    ones = ones + swapped(ones)
-    twos = twos + swapped(twos)
+    *cols, act_grad = cot_part(scalars, grad, before, after, down_weight)
+    windows, act_grad, cols = lax.optimization_barrier((windows, act_grad, cols))
+
+    (
+        hidden, normed_one, scaled, activated, to_y, to_x, to_xy, linear, gate, glu,
+        normed_two, inverse_two,
+    ) = forward_part(
+        scalars, windows, res, before, after, out_weight, gain_one, up_weight, conv_kernel,
+        gain_two, cols,
+    )
+    pairs = [(i, i ^ 3) for i in range(4)]
+    received = (
+        flipped(scaled, "chi", 2),
+        flipped(scaled, "chi", 1),
+        flipped(to_x, "dhi", 1),
+        flipped(to_y, "clo", 1),
+        lax.ppermute(to_xy, SECOND, pairs),
+    )
+    message = back_part(
+        scalars, act_grad, normed_one, linear, gate,
+        glu, normed_two, inverse_two, conv_kernel, gain_two, up_weight,
+    )
+    message, received = lax.optimization_barrier((message, received))
+    one_far, one_near, from_x, from_y, from_xy = received
     message = lax.all_to_all(message, FIRST, split_axis=0, concat_axis=0, tiled=True)
-    parts = product_part(scalars, message, ones + twos)
+    one_last = flipped(one_far, "chi", 1)
+    downs = down_part(scalars, with_swapped([activated, from_y, from_x, from_xy]), width)
+    block_out = block_part(hidden, activated, down_weight)
+    early = with_swapped([scaled, one_near, one_far])
+    one_last, downs, block_out, early = lax.optimization_barrier(
+        (one_last, downs, block_out, early)
+    )
+    last = with_swapped([one_last])
+    ones = early[:3] + last[:1] + early[3:] + last[1:]
+    parts = up_part(scalars, message, ones)
     parts = lax.all_to_all(parts, SECOND, split_axis=0, concat_axis=0, tiled=True)
-    up_grad, down_grad, kernel_grad, one, two = sum_part(scalars, parts, taps)
+    downs = [downs[0]] + [flipped(downs[k], "chi", k) for k in range(1, chi)]
+    up_grad, down_grad, kernel_grad, one, two = sum_part(scalars, parts, downs, taps)
     return (
         block_out.reshape(frames, 1, width), up_grad, down_grad, kernel_grad,
         one.reshape(-1), two.reshape(-1),

time: 115 us -> 88.7 us (0.77)
  waiting for transfers between devices: 40.6 us -> 21.7 us
  blocking collectives: 15.9 us -> 0 us
  Pallas kernels: 16.3 us -> 26.2 us
  local copies, waits for them, and re-layouts: 5.03 us -> 0.11 us
  starting transfers between devices: 34.7 us -> 38.6 us
    all_to_all x1 -> x0, blocking collectives: 15.9 us -> none  [small_device(): lax.all_to_all(parts, SECOND, split_axis=0, concat_axis=0, tiled=True)]
    ppermute x14 -> x17, waiting for transfers between devices: 24.1 us -> 10.3 us  [the longest x16 10.3 us: flipped(): return lax.ppermute(rows, axis, [(i, i ^ bit) for i in range(size)])]
    all_to_all x1, waiting for transfers between devices: 10.9 us -> 0.84 us  [small_device(): qkv = lax.all_to_all(qkv, CTX, split_axis=0, concat_axis=0, tiled=True)]
    pallas_call x7 -> x8, Pallas kernels: 12 us -> 21.9 us  [the longest x1 5.87 us: forward_part(): pl.pallas_call(forward_kernel, out_shape=(struct((frames, width), f32), s...]
    all_to_all x1, waiting for transfers between devices: 0.01 us -> 5.29 us  [small_device(): lax.all_to_all(windows, CTX, split_axis=0, concat_axis=0, tiled=True)]
    unnamed x20 -> x8, local copies, waits for them, and re-layouts: 4.94 us -> 0.02 us
    all_to_all x0 -> x1, starting transfers between devices: none -> 3.48 us  [small_device(): lax.all_to_all(parts, SECOND, split_axis=0, concat_axis=0, tiled=True)]
    all_to_all x1, starting transfers between devices: 5.63 us -> 3.45 us  [small_device(): lax.all_to_all(message, FIRST, split_axis=0, concat_axis=0, tiled=True)]
  transfers between devices with their start and end apart: 19 -> 23, of which waited for: 10 -> 10; matrix products, arithmetic and copies ran while one was open for 0% -> 0% of each run, Pallas kernels for 1% -> 14%
where the time goes in v3:
time: 88.7 us; the launch traced here: 88.1 us
  starting transfers between devices  38.6 us (44%)
  Pallas kernels  26.2 us (30%)
  waiting for transfers between devices  21.7 us (24%)
  between operations  1.47 us (2%)
    ppermute x16, starting transfers between devices, flipped(): return lax.ppermute(rows, axis, [(i, i ^ bit) for i in range(size)])  14.1 us
    ppermute x16, waiting for transfers between devices, flipped(): return lax.ppermute(rows, axis, [(i, i ^ bit) for i in range(size)])  10.3 us
    all_to_all x1, starting transfers between devices, small_device(): qkv = lax.all_to_all(qkv, CTX, split_axis=0, concat_axis=0, tiled=True)  7.29 us
    pallas_call x1, Pallas kernels, forward_part(): pl.pallas_call(forward_kernel, out_shape=(struct((frames, width), f32), s...  5.87 us
    all_to_all x1, waiting for transfers between devices, small_device(): lax.all_to_all(windows, CTX, split_axis=0, concat_axis=0, tiled=True)  5.29 us
    pallas_call x1, Pallas kernels, back_part(): pl.pallas_call(back_kernel, out_shape=struct((width // 128, frames + 24,...  5 us
    all_to_all x1, starting transfers between devices, small_device(): lax.all_to_all(windows, CTX, split_axis=0, concat_axis=0, tiled=True)  4.49 us
    ppermute x1, waiting for transfers between devices, small_device(): after = lax.ppermute(low, CTX, down)  4.46 us
  transfers between devices with their start and end apart: 23, of which 10 were waited for; matrix products, arithmetic and copies ran while one was open for 0% of the time, Pallas kernels for 14%

profile of v3, /device:TPU:0, one launch (start us, length us, event | category | flops | bytes accessed | tf_op | source)
XLA Modules:
  0.0 88.1 jit_solution(9238380192919766013)
XLA Ops:
  0.6 0.0 copy-start.1
  0.6 1.8 %split_heads.1 = bf16[8,64,384]{2,1,0:T(8,128)(2,1)} custom-call(bf16[64,3072]{1,0:T(8,128)(2,1)} %bitcast.23), custom_call_target="tpu_custom_call" | custom-call | tf_op jit(solution)/shard_map/split_heads/pallas_call | solution.py:111
  2.4 7.3 %all-to-all-start = ((bf16[8,64,384]{2,1,0:T(8,128)(2,1)}), bf16[8,64,384]{2,1,0:T(8,128)(2,1)S(1)}, u32[]{:S(2)}, u32[]{:S(2)}) async-start(bf16[8,64,384]{2,1,0:T(8,128)(2,1)} %split_heads.1), calls=%async_computation | async-start | bytes 786432 | tf_op jit(solution)/shard_map/all_to_all | solution.py:681
  9.7 0.0 copy-start.2
  9.7 0.0 copy-start.3
  9.7 1.0 %edges.1 = (bf16[48,1024]{1,0:T(8,128)(2,1)S(1)}, bf16[48,1024]{1,0:T(8,128)(2,1)S(1)}) custom-call(bf16[64,1024]{1,0:T(8,128)(2,1)} %bitcast.21, bf16[64,1024]{1,0:T(8,128)(2,1)} %bitcast.16), custom_call_target="tpu_custom_call" | custom-call | tf_op jit(solution)/shard_map/edges/pallas_call | solution.py:142
  10.7 3.9 %collective-permute-start = (bf16[48,1024]{1,0:T(8,128)(2,1)S(1)}, bf16[48,1024]{1,0:T(8,128)(2,1)S(1)}, u32[]{:S(2)}, u32[]{:S(2)}) collective-permute-start(bf16[48,1024]{1,0:T(8,128)(2,1)S(1)} %get-tuple-element.64), channel_id=1, source_target_pairs={{0,1},{1,2},{2,3},{3,4},{4,5},{5,6},{6,7},{8,9},{9,10},{10,11},{11... | collective-permute-start | bytes 294920 | tf_op jit(solution)/shard_map/ppermute | solution.py:685
  14.6 1.3 %collective-permute-start.1 = (bf16[48,1024]{1,0:T(8,128)(2,1)S(1)}, bf16[48,1024]{1,0:T(8,128)(2,1)S(1)}, u32[]{:S(2)}, u32[]{:S(2)}) collective-permute-start(bf16[48,1024]{1,0:T(8,128)(2,1)S(1)} %get-tuple-element.65), channel_id=1, source_target_pairs={{1,0},{2,1},{3,2},{4,3},{5,4},{6,5},{7,6},{9,8},{10,9},{11,10},{12... | collective-permute-start | bytes 294920 | tf_op jit(solution)/shard_map/ppermute | solution.py:686
  16.6 0.1 stack.27.scalar_ref
  16.7 0.5 collective-permute-done.low_ref
  17.1 4.5 %collective-permute-done.1.high_ref = bf16[48,1024]{1,0:T(8,128)(2,1)S(1)} collective-permute-done((bf16[48,1024]{1,0:T(8,128)(2,1)S(1)}, bf16[48,1024]{1,0:T(8,128)(2,1)S(1)}, u32[]{:S(2)}, u32[]{:S(2)}) %collective-permute-start.1) | collective-permute-done | bytes 98336 | tf_op jit(solution)/shard_map/ppermute | solution.py:686
  21.6 0.8 all-to-all-done
  22.5 2.9 %attend.1 = bf16[8,128,128]{2,1,0:T(8,128)(2,1)} custom-call(s32[7]{0:T(128)S(1)} %stack.27.scalar_ref, bf16[512,384]{1,0:T(8,128)(2,1)S(1)} %bitcast.15), custom_call_target="tpu_custom_call" | custom-call | tf_op jit(solution)/shard_map/attend/pallas_call | solution.py:191
  25.3 4.5 %all-to-all-start.1 = ((bf16[8,128,128]{2,1,0:T(8,128)(2,1)}), bf16[8,128,128]{2,1,0:T(8,128)(2,1)S(1)}, u32[]{:S(2)}, u32[]{:S(2)}) async-start(bf16[8,128,128]{2,1,0:T(8,128)(2,1)} %attend.1), calls=%async_computation.1 | async-start | bytes 524288 | tf_op jit(solution)/shard_map/all_to_all | solution.py:690
  29.8 0.0 copy-done.1
  29.8 2.9 %cotangent.1 = (bf16[64,256]{1,0:T(8,128)(2,1)S(1)}, bf16[64,256]{1,0:T(8,128)(2,1)S(1)}, bf16[64,256]{1,0:T(8,128)(2,1)S(1)}, bf16[64,256]{1,0:T(8,128)(2,1)S(1)}, f32[96,1024]{1,0:T(8,128)S(1)}) custom-call(s32[7]{0:T(128)S(1)} %stack.27.scalar_ref, bf16[64,1024]{1,0:T(8,128)(2,1)S(1)} %bitcast.17, bf16[48,1024]{1,0:T(8,128)(2,1)S(1)} %collective-permute-done.low_ref, ...), custom_call_target="tpu_custom_call" | custom-call | tf_op jit(solution)/shard_map/cotangent/pallas_call | solution.py:240
  32.7 5.3 %all-to-all-done.1.context_ref = bf16[8,128,128]{2,1,0:T(8,128)(2,1)S(1)} async-done(((bf16[8,128,128]{2,1,0:T(8,128)(2,1)}), bf16[8,128,128]{2,1,0:T(8,128)(2,1)S(1)}, u32[]{:S(2)}, u32[]{:S(2)}) %all-to-all-start.1) | async-done | bytes 262176 | tf_op jit(solution)/shard_map/all_to_all | solution.py:690
  38.0 0.0 copy-done
  38.0 0.0 copy-done.2
  38.0 0.0 copy-done.3
  38.0 5.9 %forward.1 = (f32[64,1024]{1,0:T(8,128)S(1)}, f32[64,1024]{1,0:T(8,128)S(1)}, bf16[64,1024]{1,0:T(8,128)(2,1)S(1)}, bf16[64,1280]{1,0:T(8,128)(2,1)S(1)}, bf16[6...) custom-call(s32[7]{0:T(128)S(1)} %stack.27.scalar_ref, ...), custom_call_target="tpu_custom_call" | custom-call | tf_op jit(solution)/shard_map/forward/pallas_call | solution.py:356
  43.9 1.6 %collective-permute-start.4 = (bf16[64,1280]{1,0:T(8,128)(2,1)S(1)}, bf16[64,1280]{1,0:T(8,128)(2,1)S(1)}, u32[]{:S(2)}, u32[]{:S(2)}) collective-permute-start(bf16[64,1280]{1,0:T(8,128)(2,1)S(1)} %get-tuple-element.90), channel_id=1, source_target_pairs={{0,16},{16,0},{1,17},{17,1},{2,18},{18,2},{3,19},{19,3},{4,20},{20... | collective-permute-start | bytes 491528 | tf_op jit(solution)/shard_map/ppermute | solution.py:651
  45.5 1.4 %collective-permute-start.5 = (bf16[64,1280]{1,0:T(8,128)(2,1)S(1)}, bf16[64,1280]{1,0:T(8,128)(2,1)S(1)}, u32[]{:S(2)}, u32[]{:S(2)}) collective-permute-start(bf16[64,1280]{1,0:T(8,128)(2,1)S(1)} %get-tuple-element.91), channel_id=1, source_target_pairs={{0,1},{1,0},{2,3},{3,2},{4,5},{5,4},{6,7},{7,6},{8,9},{9,8},{10,11... | collective-permute-start | bytes 491528 | tf_op jit(solution)/shard_map/ppermute | solution.py:651
  46.9 0.6 collective-permute-start.6
  47.5 1.1 %collective-permute-start.3 = (bf16[64,1024]{1,0:T(8,128)(2,1)S(1)}, bf16[64,1024]{1,0:T(8,128)(2,1)S(1)}, u32[]{:S(2)}, u32[]{:S(2)}) collective-permute-start(bf16[64,1024]{1,0:T(8,128)(2,1)S(1)} %get-tuple-element.106.refs_0_), channel_id=1, source_target_pairs={{0,2},{2,0},{4,6},{6,4},{1,3},{3,1},{5,7},{7,5},{8,10},{10,8},{12,... | collective-permute-start | bytes 393224 | tf_op jit(solution)/shard_map/ppermute | solution.py:651
  48.5 0.5 collective-permute-start.2
  49.0 5.0 %backward.1 = bf16[8,88,256]{2,1,0:T(8,128)(2,1)} custom-call(s32[7]{0:T(128)S(1)} %stack.27.scalar_ref, f32[96,1024]{1,0:T(8,128)S(1)} %get-tuple-element.77.act_grad_ref, f32[64,1024]{1,0:T(8,128)S(1)} %get-tuple-element.83.one_ref, f32[64,1024]{1,0:T(8,128)S(1)} %get-tuple-element.84.linear_ref, f32[64,1024]{1,0:T(8,128)S(1)} %get-tuple-element.85.gate_ref, ...), custom_call_target="tpu_custom_call" | custom-call | tf_op jit(solution)/shard_map/backward/pallas_call | solution.py:508
  54.0 0.0 collective-permute-done.3.refs_1_
  54.0 1.8 %collective-permute-done.2.refs_2_ = bf16[64,1024]{1,0:T(8,128)(2,1)S(1)} collective-permute-done((bf16[64,1024]{1,0:T(8,128)(2,1)S(1)}, bf16[64,1024]{1,0:T(8,128)(2,1)S(1)}, u32[]{:S(2)}, u32[]{:S(2)}) %collective-permute-start.2) | collective-permute-done | bytes 131104 | tf_op jit(solution)/shard_map/ppermute | solution.py:651
  55.8 0.0 collective-permute-done.4.refs_2_
  55.8 0.0 collective-permute-done.5.refs_1_
  55.8 0.0 collective-permute-done.6.refs_3_
  55.8 3.5 %all-to-all-start.2 = ((bf16[8,88,256]{2,1,0:T(8,128)(2,1)}), bf16[8,88,256]{2,1,0:T(8,128)(2,1)S(1)}, u32[]{:S(2)}, u32[]{:S(2)}) async-start(bf16[8,88,256]{2,1,0:T(8,128)(2,1)} %backward.1), calls=%async_computation.2 | async-start | bytes 720896 | tf_op jit(solution)/shard_map/all_to_all | solution.py:715
  59.3 0.4 collective-permute-start.8
  59.7 0.2 collective-permute-start.9
  59.9 0.4 collective-permute-start.10
  60.2 0.2 collective-permute-start.11
  60.4 0.4 collective-permute-start.12
  60.7 0.0 collective-permute-done.8.refs_4_
  60.8 0.4 collective-permute-start.13
  61.1 0.0 collective-permute-done.9.refs_5_
  61.1 0.2 collective-permute-start.14
  61.3 0.0 collective-permute-done.10.refs_6_
  61.4 1.8 %collective-permute-start.7 = (bf16[64,1024]{1,0:T(8,128)(2,1)S(1)}, bf16[64,1024]{1,0:T(8,128)(2,1)S(1)}, u32[]{:S(2)}, u32[]{:S(2)}) collective-permute-start(bf16[64,1024]{1,0:T(8,128)(2,1)S(1)} %collective-permute-done.2.refs_2_), channel_id=1, source_target_pairs={{0,2},{2,0},{4,6},{6,4},{1,3},{3,1},{5,7},{7,5},{8,10},{10,8},{12,... | collective-permute-start | bytes 393224 | tf_op jit(solution)/shard_map/ppermute | solution.py:651
  63.1 2.7 %block_out.1 = bf16[64,1024]{1,0:T(8,128)(2,1)} custom-call(f32[64,1024]{1,0:T(8,128)S(1)} %get-tuple-element.102.hidden_ref, bf16[64,1280]{1,0:T(8,128)(2,1)S(1)} %get-tuple-element.94.refs_0_.activated_ref, bf16[1024,1024]{1,0:T(8,128)(2,1)} %down_ref.1), custom_call_target="tpu_custom_call" | custom-call | tf_op jit(solution)/shard_map/block_out/pallas_call | solution.py:490
  65.8 0.0 collective-permute-done.11.refs_7_
  65.8 0.9 %down_products.1 = (bf16[32,1024]{1,0:T(8,128)(2,1)S(1)}, bf16[32,1024]{1,0:T(8,128)(2,1)S(1)}, bf16[32,1024]{1,0:T(8,128)(2,1)S(1)}, bf16[32,1024]{1,0:T(8,128)(2,1)S(1)}) custom-call(s32[7]{0:T(128)S(1)} %stack.27.scalar_ref, bf16[64,1280]{1,0:T(8,128)(2,1)S(1)} %get-tuple-element.94.refs_0_.activated_ref, ...), custom_call_target="tpu_custom_call" | custom-call | tf_op jit(solution)/shard_map/down_products/pallas_call | solution.py:592
  66.7 0.0 collective-permute-done.12.refs_4_
  66.8 0.0 collective-permute-done.13.refs_5_
  66.8 0.0 collective-permute-done.14.refs_6_
  66.8 2.2 %collective-permute-done.7.refs_3_ = bf16[64,1024]{1,0:T(8,128)(2,1)S(1)} collective-permute-done((bf16[64,1024]{1,0:T(8,128)(2,1)S(1)}, bf16[64,1024]{1,0:T(8,128)(2,1)S(1)}, u32[]{:S(2)}, u32[]{:S(2)}) %collective-permute-start.7) | collective-permute-done | bytes 131104 | tf_op jit(solution)/shard_map/ppermute | solution.py:651
  69.0 0.0 collective-permute-start.15
  69.0 1.3 %collective-permute-done.15.refs_7_ = bf16[64,1024]{1,0:T(8,128)(2,1)S(1)} collective-permute-done((bf16[64,1024]{1,0:T(8,128)(2,1)S(1)}, bf16[64,1024]{1,0:T(8,128)(2,1)S(1)}, u32[]{:S(2)}, u32[]{:S(2)}) %collective-permute-start.15) | collective-permute-done | bytes 131104 | tf_op jit(solution)/shard_map/ppermute | solution.py:651
  70.3 0.3 all-to-all-done.2.message_ref
  70.6 1.8 %up_products.1 = bf16[4,72,1024]{2,1,0:T(8,128)(2,1)} custom-call(s32[7]{0:T(128)S(1)} %stack.27.scalar_ref, bf16[8,88,256]{2,1,0:T(8,128)(2,1)S(1)} %all-to-all-done.2.message_ref, bf16[64,1024]{1,0:T(8,128)(2,1)S(1)} %get-tuple-element.106.refs_0_, bf16[64,1024]{1,0:T(8,128)(2,1)S(1)} %collective-permute-done.3.refs_1_, ...), custom_call_target="tpu_custom_call" | custom-call | tf_op jit(solution)/shard_map/up_products/pallas_call | solution.py:556
  72.4 3.5 %all-to-all-start.3 = ((bf16[4,72,1024]{2,1,0:T(8,128)(2,1)}), bf16[4,72,1024]{2,1,0:T(8,128)(2,1)S(1)}, u32[]{:S(2)}, u32[]{:S(2)}) async-start(bf16[4,72,1024]{2,1,0:T(8,128)(2,1)} %up_products.1), calls=%async_computation.3 | async-start | bytes 1179648 | tf_op jit(solution)/shard_map/all_to_all | solution.py:726
  75.9 2.3 %collective-permute-start.16 = (bf16[32,1024]{1,0:T(8,128)(2,1)S(1)}, bf16[32,1024]{1,0:T(8,128)(2,1)S(1)}, u32[]{:S(2)}, u32[]{:S(2)}) collective-permute-start(bf16[32,1024]{1,0:T(8,128)(2,1)S(1)} %get-tuple-element.114), channel_id=1, source_target_pairs={{0,2},{2,0},{4,6},{6,4},{1,3},{3,1},{5,7},{7,5},{8,10},{10,8},{12,... | collective-permute-start | bytes 196616 | tf_op jit(solution)/shard_map/ppermute | solution.py:651
  78.2 2.3 %collective-permute-start.17 = (bf16[32,1024]{1,0:T(8,128)(2,1)S(1)}, bf16[32,1024]{1,0:T(8,128)(2,1)S(1)}, u32[]{:S(2)}, u32[]{:S(2)}) collective-permute-start(bf16[32,1024]{1,0:T(8,128)(2,1)S(1)} %get-tuple-element.115), channel_id=1, source_target_pairs={{0,4},{2,6},{4,0},{6,2},{1,5},{3,7},{5,1},{7,3},{8,12},{10,14},{12... | collective-permute-start | bytes 196616 | tf_op jit(solution)/shard_map/ppermute | solution.py:651
  80.5 1.2 %collective-permute-start.18 = (bf16[32,1024]{1,0:T(8,128)(2,1)S(1)}, bf16[32,1024]{1,0:T(8,128)(2,1)S(1)}, u32[]{:S(2)}, u32[]{:S(2)}) collective-permute-start(bf16[32,1024]{1,0:T(8,128)(2,1)S(1)} %get-tuple-element.116), channel_id=1, source_target_pairs={{0,6},{2,4},{4,2},{6,0},{1,7},{3,5},{5,3},{7,1},{8,14},{10,12},{12... | collective-permute-start | bytes 196616 | tf_op jit(solution)/shard_map/ppermute | solution.py:651
  81.6 0.0 collective-permute-done.16.refs_1_
  81.7 2.1 %collective-permute-done.17.refs_2_ = bf16[32,1024]{1,0:T(8,128)(2,1)S(1)} collective-permute-done((bf16[32,1024]{1,0:T(8,128)(2,1)S(1)}, bf16[32,1024]{1,0:T(8,128)(2,1)S(1)}, u32[]{:S(2)}, u32[]{:S(2)}) %collective-permute-start.17) | collective-permute-done | bytes 65568 | tf_op jit(solution)/shard_map/ppermute | solution.py:651
  83.7 2.9 %collective-permute-done.18.refs_3_ = bf16[32,1024]{1,0:T(8,128)(2,1)S(1)} collective-permute-done((bf16[32,1024]{1,0:T(8,128)(2,1)S(1)}, bf16[32,1024]{1,0:T(8,128)(2,1)S(1)}, u32[]{:S(2)}, u32[]{:S(2)}) %collective-permute-start.18) | collective-permute-done | bytes 65568 | tf_op jit(solution)/shard_map/ppermute | solution.py:651
  86.6 0.0 all-to-all-done.3.parts_ref
  86.6 1.4 %sums.1 = (f32[64,1024]{1,0:T(8,128)}, f32[32,1024]{1,0:T(8,128)}, f32[32,31]{1,0:T(8,128)}, f32[1,32]{1,0:T(1,128)}, f32[1,32]{1,0:T(1,128)}) custom-call(s32[7]{0:T(128)S(1)} %stack.27.scalar_ref, bf16[4,72,1024]{2,1,0:T(8,128)(2,1)S(1)} %all-to-all-done.3.parts_ref, bf16[32,1024]{1,0:T(8,128)(2,1)S(1)} %get-tuple-element.113.refs_0_, ...), custom_call_target="tpu_custom_call" | custom-call | tf_op jit(solution)/shard_map/sums/pallas_call | solution.py:633
  (1 shorter events, 0.0 us)
Async XLA Ops:
  0.6 29.2 %copy-start.1 = (bf16[64,1,1024]{2,0,1:T(8,128)(2,1)S(1)}, bf16[64,1,1024]{2,0,1:T(8,128)(2,1)}, u32[]{:S(2)}) copy-start(bf16[64,1,1024]{2,0,1:T(8,128)(2,1)} %param.19) | copy-start | bytes 393220
  2.4 20.0 %all-to-all-start = ((bf16[8,64,384]{2,1,0:T(8,128)(2,1)}), bf16[8,64,384]{2,1,0:T(8,128)(2,1)S(1)}, u32[]{:S(2)}, u32[]{:S(2)}) async-start(bf16[8,64,384]{2,1,0:T(8,128)(2,1)} %split_heads.1), calls=%async_computation | async-start | bytes 786432 | tf_op jit(solution)/shard_map/all_to_all | solution.py:681
  9.7 28.3 %copy-start = (f32[31,1024]{1,0:T(8,128)S(1)}, f32[31,1024]{1,0:T(8,128)}, u32[]{:S(2)}) copy-start(f32[31,1024]{1,0:T(8,128)} %taps_ref.3) | copy-start | bytes 380932
  9.7 28.3 %copy-start.2 = (f32[1024]{0:T(1024)S(1)}, f32[1024]{0:T(1024)}, u32[]{:S(2)}) copy-start(f32[1024]{0:T(1024)} %param.16) | copy-start | bytes 12292
  9.7 28.3 %copy-start.3 = (f32[1024]{0:T(1024)S(1)}, f32[1024]{0:T(1024)}, u32[]{:S(2)}) copy-start(f32[1024]{0:T(1024)} %param.13) | copy-start | bytes 12292
  10.7 6.4 %collective-permute-start = (bf16[48,1024]{1,0:T(8,128)(2,1)S(1)}, bf16[48,1024]{1,0:T(8,128)(2,1)S(1)}, u32[]{:S(2)}, u32[]{:S(2)}) collective-permute-start(bf16[48,1024]{1,0:T(8,128)(2,1)S(1)} %get-tuple-element.64), channel_id=1, source_target_pairs={{0,1},{1,2},{2,3},{3,4},{4,5},{5,6},{6,7},{8,9},{9,10},{10,11},{11... | collective-permute-start | bytes 294920 | tf_op jit(solution)/shard_map/ppermute | solution.py:685
  14.6 7.0 %collective-permute-start.1 = (bf16[48,1024]{1,0:T(8,128)(2,1)S(1)}, bf16[48,1024]{1,0:T(8,128)(2,1)S(1)}, u32[]{:S(2)}, u32[]{:S(2)}) collective-permute-start(bf16[48,1024]{1,0:T(8,128)(2,1)S(1)} %get-tuple-element.65), channel_id=1, source_target_pairs={{1,0},{2,1},{3,2},{4,3},{5,4},{6,5},{7,6},{9,8},{10,9},{11,10},{12... | collective-permute-start | bytes 294920 | tf_op jit(solution)/shard_map/ppermute | solution.py:686
  25.3 12.7 %all-to-all-start.1 = ((bf16[8,128,128]{2,1,0:T(8,128)(2,1)}), bf16[8,128,128]{2,1,0:T(8,128)(2,1)S(1)}, u32[]{:S(2)}, u32[]{:S(2)}) async-start(bf16[8,128,128]{2,1,0:T(8,128)(2,1)} %attend.1), calls=%async_computation.1 | async-start | bytes 524288 | tf_op jit(solution)/shard_map/all_to_all | solution.py:690
  43.9 11.9 %collective-permute-start.4 = (bf16[64,1280]{1,0:T(8,128)(2,1)S(1)}, bf16[64,1280]{1,0:T(8,128)(2,1)S(1)}, u32[]{:S(2)}, u32[]{:S(2)}) collective-permute-start(bf16[64,1280]{1,0:T(8,128)(2,1)S(1)} %get-tuple-element.90), channel_id=1, source_target_pairs={{0,16},{16,0},{1,17},{17,1},{2,18},{18,2},{3,19},{19,3},{4,20},{20... | collective-permute-start | bytes 491528 | tf_op jit(solution)/shard_map/ppermute | solution.py:651
  45.5 10.3 %collective-permute-start.5 = (bf16[64,1280]{1,0:T(8,128)(2,1)S(1)}, bf16[64,1280]{1,0:T(8,128)(2,1)S(1)}, u32[]{:S(2)}, u32[]{:S(2)}) collective-permute-start(bf16[64,1280]{1,0:T(8,128)(2,1)S(1)} %get-tuple-element.91), channel_id=1, source_target_pairs={{0,1},{1,0},{2,3},{3,2},{4,5},{5,4},{6,7},{7,6},{8,9},{9,8},{10,11... | collective-permute-start | bytes 491528 | tf_op jit(solution)/shard_map/ppermute | solution.py:651
  46.9 8.9 %collective-permute-start.6 = (bf16[64,1280]{1,0:T(8,128)(2,1)S(1)}, bf16[64,1280]{1,0:T(8,128)(2,1)S(1)}, u32[]{:S(2)}, u32[]{:S(2)}) collective-permute-start(bf16[64,1280]{1,0:T(8,128)(2,1)S(1)} %get-tuple-element.92), channel_id=1, source_target_pairs={{0,17},{1,16},{16,1},{17,0},{2,19},{3,18},{18,3},{19,2},{4,21},{5,... | collective-permute-start | bytes 491528 | tf_op jit(solution)/shard_map/ppermute | solution.py:707
  47.5 6.5 %collective-permute-start.3 = (bf16[64,1024]{1,0:T(8,128)(2,1)S(1)}, bf16[64,1024]{1,0:T(8,128)(2,1)S(1)}, u32[]{:S(2)}, u32[]{:S(2)}) collective-permute-start(bf16[64,1024]{1,0:T(8,128)(2,1)S(1)} %get-tuple-element.106.refs_0_), channel_id=1, source_target_pairs={{0,2},{2,0},{4,6},{6,4},{1,3},{3,1},{5,7},{7,5},{8,10},{10,8},{12,... | collective-permute-start | bytes 393224 | tf_op jit(solution)/shard_map/ppermute | solution.py:651
  48.5 7.3 %collective-permute-start.2 = (bf16[64,1024]{1,0:T(8,128)(2,1)S(1)}, bf16[64,1024]{1,0:T(8,128)(2,1)S(1)}, u32[]{:S(2)}, u32[]{:S(2)}) collective-permute-start(bf16[64,1024]{1,0:T(8,128)(2,1)S(1)} %get-tuple-element.106.refs_0_), channel_id=1, source_target_pairs={{0,4},{2,6},{4,0},{6,2},{1,5},{3,7},{5,1},{7,3},{8,12},{10,14},{12... | collective-permute-start | bytes 393224 | tf_op jit(solution)/shard_map/ppermute | solution.py:651
  55.8 14.8 %all-to-all-start.2 = ((bf16[8,88,256]{2,1,0:T(8,128)(2,1)}), bf16[8,88,256]{2,1,0:T(8,128)(2,1)S(1)}, u32[]{:S(2)}, u32[]{:S(2)}) async-start(bf16[8,88,256]{2,1,0:T(8,128)(2,1)} %backward.1), calls=%async_computation.2 | async-start | bytes 720896 | tf_op jit(solution)/shard_map/all_to_all | solution.py:715
  59.3 1.5 %collective-permute-start.8 = (bf16[64,1280]{1,0:T(8,128)(2,1)S(1)}, bf16[64,1280]{1,0:T(8,128)(2,1)S(1)}, u32[]{:S(2)}, u32[]{:S(2)}) collective-permute-start(bf16[64,1280]{1,0:T(8,128)(2,1)S(1)} %get-tuple-element.94.refs_0_.activated_ref), channel_id=1, source_target_pairs={{0,8},{8,0},{1,9},{9,1},{2,10},{10,2},{3,11},{11,3},{4,12},{12,4},... | collective-permute-start | bytes 491528 | tf_op jit(solution)/shard_map/ppermute | solution.py:651
  59.7 1.4 %collective-permute-start.9 = (bf16[64,1280]{1,0:T(8,128)(2,1)S(1)}, bf16[64,1280]{1,0:T(8,128)(2,1)S(1)}, u32[]{:S(2)}, u32[]{:S(2)}) collective-permute-start(bf16[64,1280]{1,0:T(8,128)(2,1)S(1)} %collective-permute-done.5.refs_1_), channel_id=1, source_target_pairs={{0,8},{8,0},{1,9},{9,1},{2,10},{10,2},{3,11},{11,3},{4,12},{12,4},... | collective-permute-start | bytes 491528 | tf_op jit(solution)/shard_map/ppermute | solution.py:651
  59.9 1.5 %collective-permute-start.10 = (bf16[64,1280]{1,0:T(8,128)(2,1)S(1)}, bf16[64,1280]{1,0:T(8,128)(2,1)S(1)}, u32[]{:S(2)}, u32[]{:S(2)}) collective-permute-start(bf16[64,1280]{1,0:T(8,128)(2,1)S(1)} %collective-permute-done.4.refs_2_), channel_id=1, source_target_pairs={{0,8},{8,0},{1,9},{9,1},{2,10},{10,2},{3,11},{11,3},{4,12},{12,4},... | collective-permute-start | bytes 491528 | tf_op jit(solution)/shard_map/ppermute | solution.py:651
  60.2 5.6 %collective-permute-start.11 = (bf16[64,1280]{1,0:T(8,128)(2,1)S(1)}, bf16[64,1280]{1,0:T(8,128)(2,1)S(1)}, u32[]{:S(2)}, u32[]{:S(2)}) collective-permute-start(bf16[64,1280]{1,0:T(8,128)(2,1)S(1)} %collective-permute-done.6.refs_3_), channel_id=1, source_target_pairs={{0,8},{8,0},{1,9},{9,1},{2,10},{10,2},{3,11},{11,3},{4,12},{12,4},... | collective-permute-start | bytes 491528 | tf_op jit(solution)/shard_map/ppermute | solution.py:651
  60.4 6.4 %collective-permute-start.12 = (bf16[64,1024]{1,0:T(8,128)(2,1)S(1)}, bf16[64,1024]{1,0:T(8,128)(2,1)S(1)}, u32[]{:S(2)}, u32[]{:S(2)}) collective-permute-start(bf16[64,1024]{1,0:T(8,128)(2,1)S(1)} %get-tuple-element.106.refs_0_), channel_id=1, source_target_pairs={{0,8},{8,0},{1,9},{9,1},{2,10},{10,2},{3,11},{11,3},{4,12},{12,4},... | collective-permute-start | bytes 393224 | tf_op jit(solution)/shard_map/ppermute | solution.py:651
  60.8 6.0 %collective-permute-start.13 = (bf16[64,1024]{1,0:T(8,128)(2,1)S(1)}, bf16[64,1024]{1,0:T(8,128)(2,1)S(1)}, u32[]{:S(2)}, u32[]{:S(2)}) collective-permute-start(bf16[64,1024]{1,0:T(8,128)(2,1)S(1)} %collective-permute-done.3.refs_1_), channel_id=1, source_target_pairs={{0,8},{8,0},{1,9},{9,1},{2,10},{10,2},{3,11},{11,3},{4,12},{12,4},... | collective-permute-start | bytes 393224 | tf_op jit(solution)/shard_map/ppermute | solution.py:651
  61.1 5.7 %collective-permute-start.14 = (bf16[64,1024]{1,0:T(8,128)(2,1)S(1)}, bf16[64,1024]{1,0:T(8,128)(2,1)S(1)}, u32[]{:S(2)}, u32[]{:S(2)}) collective-permute-start(bf16[64,1024]{1,0:T(8,128)(2,1)S(1)} %collective-permute-done.2.refs_2_), channel_id=1, source_target_pairs={{0,8},{8,0},{1,9},{9,1},{2,10},{10,2},{3,11},{11,3},{4,12},{12,4},... | collective-permute-start | bytes 393224 | tf_op jit(solution)/shard_map/ppermute | solution.py:651
  61.4 7.6 %collective-permute-start.7 = (bf16[64,1024]{1,0:T(8,128)(2,1)S(1)}, bf16[64,1024]{1,0:T(8,128)(2,1)S(1)}, u32[]{:S(2)}, u32[]{:S(2)}) collective-permute-start(bf16[64,1024]{1,0:T(8,128)(2,1)S(1)} %collective-permute-done.2.refs_2_), channel_id=1, source_target_pairs={{0,2},{2,0},{4,6},{6,4},{1,3},{3,1},{5,7},{7,5},{8,10},{10,8},{12,... | collective-permute-start | bytes 393224 | tf_op jit(solution)/shard_map/ppermute | solution.py:651
  69.0 1.3 %collective-permute-start.15 = (bf16[64,1024]{1,0:T(8,128)(2,1)S(1)}, bf16[64,1024]{1,0:T(8,128)(2,1)S(1)}, u32[]{:S(2)}, u32[]{:S(2)}) collective-permute-start(bf16[64,1024]{1,0:T(8,128)(2,1)S(1)} %collective-permute-done.7.refs_3_), channel_id=1, source_target_pairs={{0,8},{8,0},{1,9},{9,1},{2,10},{10,2},{3,11},{11,3},{4,12},{12,4},... | collective-permute-start | bytes 393224 | tf_op jit(solution)/shard_map/ppermute | solution.py:651
  72.4 14.2 %all-to-all-start.3 = ((bf16[4,72,1024]{2,1,0:T(8,128)(2,1)}), bf16[4,72,1024]{2,1,0:T(8,128)(2,1)S(1)}, u32[]{:S(2)}, u32[]{:S(2)}) async-start(bf16[4,72,1024]{2,1,0:T(8,128)(2,1)} %up_products.1), calls=%async_computation.3 | async-start | bytes 1179648 | tf_op jit(solution)/shard_map/all_to_all | solution.py:726
  75.9 5.8 %collective-permute-start.16 = (bf16[32,1024]{1,0:T(8,128)(2,1)S(1)}, bf16[32,1024]{1,0:T(8,128)(2,1)S(1)}, u32[]{:S(2)}, u32[]{:S(2)}) collective-permute-start(bf16[32,1024]{1,0:T(8,128)(2,1)S(1)} %get-tuple-element.114), channel_id=1, source_target_pairs={{0,2},{2,0},{4,6},{6,4},{1,3},{3,1},{5,7},{7,5},{8,10},{10,8},{12,... | collective-permute-start | bytes 196616 | tf_op jit(solution)/shard_map/ppermute | solution.py:651
  78.2 5.5 %collective-permute-start.17 = (bf16[32,1024]{1,0:T(8,128)(2,1)S(1)}, bf16[32,1024]{1,0:T(8,128)(2,1)S(1)}, u32[]{:S(2)}, u32[]{:S(2)}) collective-permute-start(bf16[32,1024]{1,0:T(8,128)(2,1)S(1)} %get-tuple-element.115), channel_id=1, source_target_pairs={{0,4},{2,6},{4,0},{6,2},{1,5},{3,7},{5,1},{7,3},{8,12},{10,14},{12... | collective-permute-start | bytes 196616 | tf_op jit(solution)/shard_map/ppermute | solution.py:651
  80.5 6.1 %collective-permute-start.18 = (bf16[32,1024]{1,0:T(8,128)(2,1)S(1)}, bf16[32,1024]{1,0:T(8,128)(2,1)S(1)}, u32[]{:S(2)}, u32[]{:S(2)}) collective-permute-start(bf16[32,1024]{1,0:T(8,128)(2,1)S(1)} %get-tuple-element.116), channel_id=1, source_target_pairs={{0,6},{2,4},{4,2},{6,0},{1,7},{3,5},{5,3},{7,1},{8,14},{10,12},{12... | collective-permute-start | bytes 196616 | tf_op jit(solution)/shard_map/ppermute | solution.py:651

commit v4 on v3

--- a/solution.py
+++ b/solution.py
@@ -154,26 +154,28 @@
     length = qkv_ref.shape[0]
     count = qkv_ref.shape[1] // (3 * head_size)
     ctx, wide, _ = out_ref.shape
-    allowed = lax.broadcasted_iota(jnp.int32, (length, length), 1) < scalar_ref[0]
-    outs = []
+    places = lax.broadcasted_iota(jnp.int32, (1, length), 1)
+    bias = jnp.where(places < scalar_ref[0], 0.0, -jnp.inf)
+    scores = []
     for m in range(count):
         base = 3 * head_size * m
-        query = qkv_ref[:, base : base + head_size]
+        query = qkv_ref[:, base : base + head_size] * jnp.bfloat16(head_size ** (-0.5))
         key = qkv_ref[:, base + head_size : base + 2 * head_size]
+        scores.append(bias + lax.dot_general(
+                query, key, (((1,), (1,)), ((), ())), preferred_element_type=jnp.float32))
+    scores = jnp.concatenate(scores, axis=0)
+    raised = jnp.exp(scores - jnp.max(scores, axis=-1, keepdims=True))
+    share = 1.0 / jnp.sum(raised, axis=-1, keepdims=True)
+    weights = raised.astype(jnp.bfloat16)
+    heads = []
+    for m in range(count):
+        base = 3 * head_size * m
         value = qkv_ref[:, base + 2 * head_size : base + 3 * head_size]
-        scores = (
-            lax.dot_general(
-                query, key, (((1,), (1,)), ((), ())), preferred_element_type=jnp.float32
-            )
-            * head_size ** (-0.5)
+        rows = slice(m * length, (m + 1) * length)
+        heads.append(
+            jnp.dot(weights[rows], value, preferred_element_type=jnp.float32) * share[rows]
         )
-        scores = jnp.where(allowed, scores, -jnp.inf)
-        raised = jnp.exp(scores - jnp.max(scores, axis=-1, keepdims=True))
-        weights = raised * (1.0 / jnp.sum(raised, axis=-1, keepdims=True))
-        outs.append(
-            jnp.dot(weights.astype(jnp.bfloat16), value, preferred_element_type=jnp.float32)
-        )
-    context = jnp.concatenate(outs, axis=1).astype(jnp.bfloat16)
+    context = jnp.concatenate(heads, axis=1).astype(jnp.bfloat16)
     for i in range(ctx):
         low = max(i * frames - MARGIN, 0)
         high = min(i * frames - MARGIN + wide, length)
@@ -254,8 +256,8 @@
 
 def forward_kernel(
     scalar_ref, context_ref, res_ref, low_ref, high_ref, out_ref, gain_one_ref, weight_ref,
-    taps_ref, gain_ref, cols_own_ref, cols_y_ref, cols_x_ref, cols_xy_ref,
-    hidden_ref, one_ref, own_ref, act_ref, to_y_ref, to_x_ref, to_xy_ref, linear_ref, gate_ref, glu_ref,
+    taps_ref, gain_ref,
+    hidden_ref, one_ref, own_ref, act_ref, linear_ref, gate_ref, glu_ref,
     normed_ref, inverse_ref, scaled_ref, conv_ref, out_held_ref, held_ref, res_held_ref, out_sems, sems, res_sems,
 ):
     frames, width = res_ref.shape
@@ -339,16 +341,10 @@
         if MARGIN - edge <= at < MARGIN - edge + frames:
             pre = normed * gain_ref[...]
             rows = slice(at - (MARGIN - edge), at - (MARGIN - edge) + step)
-            act = (pre * jax.nn.sigmoid(pre)).astype(jnp.bfloat16)
-            for ref in (act_ref, to_y_ref, to_x_ref, to_xy_ref):
-                ref[rows, :width] = act
-    act_ref[:, width:] = cols_own_ref[...]
-    to_y_ref[:, width:] = cols_y_ref[...]
-    to_x_ref[:, width:] = cols_x_ref[...]
-    to_xy_ref[:, width:] = cols_xy_ref[...]
-
-
-def forward_part(scalars, context, res, low, high, out_weight, gain_one, weight, taps, gain, cols):
+            act_ref[rows, :] = (pre * jax.nn.sigmoid(pre)).astype(jnp.bfloat16)
+
+
+def forward_part(scalars, context, res, low, high, out_weight, gain_one, weight, taps, gain):
     frames, width = res.shape
     ctx, wide, _ = context.shape
     near = wide - MARGIN
@@ -359,18 +355,15 @@
             struct((frames, width), f32),
             struct((frames, width), f32),
             struct((frames, width), bf),
-            struct((frames, width + width // 4), bf),
-            struct((frames, width + width // 4), bf),
-            struct((frames, width + width // 4), bf),
-            struct((frames, width + width // 4), bf),
+            struct((frames, width), bf),
             struct((frames, width), f32),
             struct((frames, width), f32),
             struct((wide, width), f32),
             struct((near, width), f32),
             struct((near, 128), f32),
         ),
-        in_specs=[SMEM, VMEM, HBM, VMEM, VMEM, HBM, VMEM, HBM] + [VMEM] * 6,
-        out_specs=(VMEM,) * 12,
+        in_specs=[SMEM, VMEM, HBM, VMEM, VMEM, HBM, VMEM, HBM, VMEM, VMEM],
+        out_specs=(VMEM,) * 9,
         scratch_shapes=[
             pltpu.VMEM((wide, width), bf),
             pltpu.VMEM((near, width), f32),
@@ -384,8 +377,7 @@
         compiler_params=params(24),
         name="forward",
     )(
-        scalars, context, in_hbm(res), low, high, in_hbm(out_weight), gain_one, in_hbm(weight), taps, gain,
-        *cols,
+        scalars, context, in_hbm(res), low, high, in_hbm(out_weight), gain_one, in_hbm(weight), taps, gain
     )
 
 
@@ -425,9 +417,9 @@
     place = scalar_ref[1] + lax.broadcasted_iota(jnp.int32, (frames, 128), 0)
     valid = place < scalar_ref[0]
 
-    def lanes(i, carry):
-        cols = pl.ds(pl.multiple_of(i * 128, 128), 128)
-        high = pl.ds(pl.multiple_of(i * 128 + width, 128), 128)
+    def lanes(i):
+        cols = slice(i * 128, (i + 1) * 128)
+        high = slice(i * 128 + width, (i + 1) * 128 + width)
         block = grad_ref[:, cols]
         own = block[first : first + frames]
         total = jnp.zeros((frames, 128), jnp.float32)
@@ -454,9 +446,9 @@
         lifted_ref[:, high] = gate_grad
         message_ref[i, :frames, :128] = linear_grad
         message_ref[i, :frames, 128:256] = gate_grad
-        return carry
-
-    lax.fori_loop(0, width // 128, lanes, 0)
+
+    for i in range(width // 128):
+        lanes(i)
     for copy in copies:
         copy.wait()
     input_grad = lax.dot_general(
@@ -564,44 +556,75 @@
     )(scalars, message, *pieces)
 
 
-def down_kernel(scalar_ref, *refs):
-    count = (len(refs) - 3) // 3
-    pieces, outs = refs[: 2 * count], refs[2 * count : 3 * count]
-    cols_ref, rows_ref, total_ref = refs[3 * count :]
-    frames, width = pieces[0].shape[0], rows_ref.shape[1]
-    span = cols_ref.shape[1]
+def pack_kernel(act_ref, *refs):
+    count = len(refs) // 2
+    width = act_ref.shape[1]
+    for cols_ref, out_ref in zip(refs[:count], refs[count:]):
+        out_ref[:, :width] = act_ref[...]
+        out_ref[:, width:] = cols_ref[...]
+
+
+def pack_part(act, cols):
+    shape = struct((act.shape[0], act.shape[1] + cols[0].shape[1]), act.dtype)
+    count = len(cols)
+    return pl.pallas_call(
+        pack_kernel,
+        out_shape=(shape,) * count,
+        in_specs=[VMEM] * (1 + count),
+        out_specs=(VMEM,) * count,
+        compiler_params=params(),
+        name="pack",
+    )(act, *cols)
+
+
+def down_kernel(*refs):
+    pieces, (mine_ref, theirs_ref, rows_ref) = refs[:-3], refs[-3:]
+    width = mine_ref.shape[1]
+    frames = pieces[0].shape[0]
     for i, piece in enumerate(pieces):
-        rows = slice(i * frames, (i + 1) * frames)
-        at = width + (i // count) * span
-        rows_ref[rows, :] = piece[:, :width]
-        cols_ref[rows, :] = piece[:, at : at + span]
-    total_ref[...] = lax.dot_general(
-        cols_ref[...], rows_ref[...], TURNED, preferred_element_type=jnp.float32
-    )
-    line = scalar_ref[3]
-    for k, out in enumerate(outs):
-        at = pl.multiple_of((line ^ k) * 32, 32)
-        out[...] = total_ref[pl.ds(at, 32), :].astype(jnp.bfloat16)
-
-
-def down_part(scalars, pieces, width):
-    count = len(pieces) // 2
-    frames = pieces[0].shape[0]
-    bf = jnp.bfloat16
-    rows = 2 * count * frames
+        rows_ref[i * frames : (i + 1) * frames, :] = piece[...]
+    total = lax.dot_general(
+        rows_ref[:, width:], rows_ref[:, :width], TURNED, preferred_element_type=jnp.float32
+    ).astype(jnp.bfloat16)
+    half = total.shape[0] // 2
+    mine_ref[...] = total[:half]
+    theirs_ref[...] = total[half:]
+
+
+def down_part(pieces, width):
+    frames, wide = pieces[0].shape
+    shape = struct(((wide - width) // 2, width), jnp.bfloat16)
     return pl.pallas_call(
         down_kernel,
-        out_shape=(struct((32, width), bf),) * count,
-        in_specs=[SMEM] + [VMEM] * (2 * count),
-        out_specs=(VMEM,) * count,
-        scratch_shapes=[
-            pltpu.VMEM((rows, 128), bf),
-            pltpu.VMEM((rows, width), bf),
-            pltpu.VMEM((128, width), jnp.float32),
-        ],
+        out_shape=(shape, shape),
+        in_specs=[VMEM] * len(pieces),
+        out_specs=(VMEM, VMEM),
+        scratch_shapes=[pltpu.VMEM((len(pieces) * frames, wide), jnp.bfloat16)],
         compiler_params=params(12),
         name="down_products",
-    )(scalars, *pieces)
+    )(*pieces)
+
+
+def share_kernel(scalar_ref, mine_ref, other_ref, *refs):
+    outs, total_ref = refs[:-1], refs[-1]
+    total_ref[...] = mine_ref[...].astype(jnp.float32) + other_ref[...].astype(jnp.float32)
+    for k, out in enumerate(outs):
+        at = pl.multiple_of((scalar_ref[3] ^ k) * 32, 32)
+        out[...] = total_ref[pl.ds(at, 32), :].astype(jnp.bfloat16)
+
+
+def share_part(scalars, mine, other):
+    rows, width = mine.shape
+    count = rows // 32
+    return pl.pallas_call(
+        share_kernel,
+        out_shape=(struct((32, width), jnp.bfloat16),) * count,
+        in_specs=[SMEM, VMEM, VMEM],
+        out_specs=(VMEM,) * count,
+        scratch_shapes=[pltpu.VMEM((rows, width), jnp.float32)],
+        compiler_params=params(),
+        name="down_shares",
+    )(scalars, mine, other)
 
 
 def sum_kernel(taps, scalar_ref, parts_ref, *refs):
@@ -692,39 +715,35 @@
     windows, act_grad, cols = lax.optimization_barrier((windows, act_grad, cols))
 
     (
-        hidden, normed_one, scaled, activated, to_y, to_x, to_xy, linear, gate, glu,
-        normed_two, inverse_two,
+        hidden, normed_one, scaled, activated, linear, gate, glu, normed_two, inverse_two
     ) = forward_part(
-        scalars, windows, res, before, after, out_weight, gain_one, up_weight, conv_kernel,
-        gain_two, cols,
-    )
+        scalars, windows, res, before, after, out_weight, gain_one, up_weight, conv_kernel, gain_two
+    )
+    packed, to_y, to_x, to_xy = pack_part(activated, cols)
     pairs = [(i, i ^ 3) for i in range(4)]
-    received = (
-        flipped(scaled, "chi", 2),
-        flipped(scaled, "chi", 1),
-        flipped(to_x, "dhi", 1),
-        flipped(to_y, "clo", 1),
-        lax.ppermute(to_xy, SECOND, pairs),
-    )
+    received = [
+        flipped(to_y, "clo", 1), flipped(to_x, "dhi", 1), lax.ppermute(to_xy, SECOND, pairs)
+    ]
+    one_near, one_far = flipped(scaled, "chi", 1), flipped(scaled, "chi", 2)
     message = back_part(
         scalars, act_grad, normed_one, linear, gate,
         glu, normed_two, inverse_two, conv_kernel, gain_two, up_weight,
     )
-    message, received = lax.optimization_barrier((message, received))
-    one_far, one_near, from_x, from_y, from_xy = received
+    received, one_near, one_far, message = lax.optimization_barrier(
+        (received, one_near, one_far, message)
+    )
     message = lax.all_to_all(message, FIRST, split_axis=0, concat_axis=0, tiled=True)
     one_last = flipped(one_far, "chi", 1)
-    downs = down_part(scalars, with_swapped([activated, from_y, from_x, from_xy]), width)
-    block_out = block_part(hidden, activated, down_weight)
+    mine, theirs = down_part([packed, *received], width)
+    downs = share_part(scalars, mine, flipped(theirs, "dlo", 1))
     early = with_swapped([scaled, one_near, one_far])
-    one_last, downs, block_out, early = lax.optimization_barrier(
-        (one_last, downs, block_out, early)
-    )
+    one_last, early, downs = lax.optimization_barrier((one_last, early, downs))
     last = with_swapped([one_last])
     ones = early[:3] + last[:1] + early[3:] + last[1:]
+    downs = [downs[0]] + [flipped(downs[k], "chi", k) for k in range(1, chi)]
     parts = up_part(scalars, message, ones)
     parts = lax.all_to_all(parts, SECOND, split_axis=0, concat_axis=0, tiled=True)
-    downs = [downs[0]] + [flipped(downs[k], "chi", k) for k in range(1, chi)]
+    block_out = block_part(hidden, activated, down_weight)
     up_grad, down_grad, kernel_grad, one, two = sum_part(scalars, parts, downs, taps)
     return (
         block_out.reshape(frames, 1, width), up_grad, down_grad, kernel_grad,

time: 88.7 us -> 87.1 us (0.982)
    ppermute x16 -> x13, starting transfers between devices: 14.1 us -> 13.2 us  [flipped(): return lax.ppermute(rows, axis, [(i, i ^ bit) for i in range(size)])]
    ppermute x16 -> x13, waiting for transfers between devices: 10.3 us -> 10 us  [flipped(): return lax.ppermute(rows, axis, [(i, i ^ bit) for i in range(size)])]
  transfers between devices with their start and end apart: 23 -> 20, of which waited for: 10 -> 9; matrix products, arithmetic and copies ran while one was open for 0% -> 0% of each run, Pallas kernels for 14% -> 14%
where the time goes in v4:
time: 87.1 us; the launch traced here: 86.5 us
  starting transfers between devices  37.9 us (44%)
  Pallas kernels  25.7 us (30%)
  waiting for transfers between devices  21.4 us (25%)
  between operations  1.49 us (2%)
    ppermute x13, starting transfers between devices, flipped(): return lax.ppermute(rows, axis, [(i, i ^ bit) for i in range(size)])  13.2 us
    ppermute x13, waiting for transfers between devices, flipped(): return lax.ppermute(rows, axis, [(i, i ^ bit) for i in range(size)])  10 us
    all_to_all x1, starting transfers between devices, small_device(): qkv = lax.all_to_all(qkv, CTX, split_axis=0, concat_axis=0, tiled=True)  7.29 us
    pallas_call x1, Pallas kernels, forward_part(): pl.pallas_call(forward_kernel, out_shape=(struct((frames, width), f32), s...  5.83 us
    all_to_all x1, waiting for transfers between devices, small_device(): lax.all_to_all(windows, CTX, split_axis=0, concat_axis=0, tiled=True)  5.29 us
    pallas_call x1, Pallas kernels, back_part(): pl.pallas_call(back_kernel, out_shape=struct((width // 128, frames + 24,...  4.98 us
    all_to_all x1, starting transfers between devices, small_device(): lax.all_to_all(windows, CTX, split_axis=0, concat_axis=0, tiled=True)  4.5 us
    ppermute x1, waiting for transfers between devices, small_device(): after = lax.ppermute(low, CTX, down)  4.46 us
  transfers between devices with their start and end apart: 20, of which 9 were waited for; matrix products, arithmetic and copies ran while one was open for 0% of the time, Pallas kernels for 14%

profile of v4, /device:TPU:0, one launch (start us, length us, event | category | flops | bytes accessed | tf_op | source)
XLA Modules:
  0.0 86.5 jit_solution(4054343246035491536)
XLA Ops:
  0.6 0.0 copy-start.1
  0.6 1.8 %split_heads.1 = bf16[8,64,384]{2,1,0:T(8,128)(2,1)} custom-call(bf16[64,3072]{1,0:T(8,128)(2,1)} %bitcast.23), custom_call_target="tpu_custom_call" | custom-call | tf_op jit(solution)/shard_map/split_heads/pallas_call | solution.py:111
  2.4 7.3 %all-to-all-start = ((bf16[8,64,384]{2,1,0:T(8,128)(2,1)}), bf16[8,64,384]{2,1,0:T(8,128)(2,1)S(1)}, u32[]{:S(2)}, u32[]{:S(2)}) async-start(bf16[8,64,384]{2,1,0:T(8,128)(2,1)} %split_heads.1), calls=%async_computation | async-start | bytes 786432 | tf_op jit(solution)/shard_map/all_to_all | solution.py:704
  9.7 0.0 copy-start
  9.7 0.0 copy-start.2
  9.7 0.0 copy-start.3
  9.7 1.0 %edges.1 = (bf16[48,1024]{1,0:T(8,128)(2,1)S(1)}, bf16[48,1024]{1,0:T(8,128)(2,1)S(1)}) custom-call(bf16[64,1024]{1,0:T(8,128)(2,1)} %bitcast.21, bf16[64,1024]{1,0:T(8,128)(2,1)} %bitcast.16), custom_call_target="tpu_custom_call" | custom-call | tf_op jit(solution)/shard_map/edges/pallas_call | solution.py:142
  10.7 3.9 %collective-permute-start = (bf16[48,1024]{1,0:T(8,128)(2,1)S(1)}, bf16[48,1024]{1,0:T(8,128)(2,1)S(1)}, u32[]{:S(2)}, u32[]{:S(2)}) collective-permute-start(bf16[48,1024]{1,0:T(8,128)(2,1)S(1)} %get-tuple-element.66), channel_id=1, source_target_pairs={{0,1},{1,2},{2,3},{3,4},{4,5},{5,6},{6,7},{8,9},{9,10},{10,11},{11... | collective-permute-start | bytes 294920 | tf_op jit(solution)/shard_map/ppermute | solution.py:708
  14.6 1.3 %collective-permute-start.1 = (bf16[48,1024]{1,0:T(8,128)(2,1)S(1)}, bf16[48,1024]{1,0:T(8,128)(2,1)S(1)}, u32[]{:S(2)}, u32[]{:S(2)}) collective-permute-start(bf16[48,1024]{1,0:T(8,128)(2,1)S(1)} %get-tuple-element.67), channel_id=1, source_target_pairs={{1,0},{2,1},{3,2},{4,3},{5,4},{6,5},{7,6},{9,8},{10,9},{11,10},{12... | collective-permute-start | bytes 294920 | tf_op jit(solution)/shard_map/ppermute | solution.py:709
  16.6 0.1 stack.27.scalar_ref
  16.7 0.5 collective-permute-done.low_ref
  17.1 4.5 %collective-permute-done.1.high_ref = bf16[48,1024]{1,0:T(8,128)(2,1)S(1)} collective-permute-done((bf16[48,1024]{1,0:T(8,128)(2,1)S(1)}, bf16[48,1024]{1,0:T(8,128)(2,1)S(1)}, u32[]{:S(2)}, u32[]{:S(2)}) %collective-permute-start.1) | collective-permute-done | bytes 98336 | tf_op jit(solution)/shard_map/ppermute | solution.py:709
  21.6 0.8 all-to-all-done
  22.4 2.3 %attend.1 = bf16[8,128,128]{2,1,0:T(8,128)(2,1)} custom-call(s32[7]{0:T(128)S(1)} %stack.27.scalar_ref, bf16[512,384]{1,0:T(8,128)(2,1)S(1)} %bitcast.15), custom_call_target="tpu_custom_call" | custom-call | tf_op jit(solution)/shard_map/attend/pallas_call | solution.py:193
  24.7 4.5 %all-to-all-start.1 = ((bf16[8,128,128]{2,1,0:T(8,128)(2,1)}), bf16[8,128,128]{2,1,0:T(8,128)(2,1)S(1)}, u32[]{:S(2)}, u32[]{:S(2)}) async-start(bf16[8,128,128]{2,1,0:T(8,128)(2,1)} %attend.1), calls=%async_computation.1 | async-start | bytes 524288 | tf_op jit(solution)/shard_map/all_to_all | solution.py:713
  29.2 0.0 copy-done.1
  29.2 2.9 %cotangent.1 = (bf16[64,256]{1,0:T(8,128)(2,1)S(1)}, bf16[64,256]{1,0:T(8,128)(2,1)S(1)}, bf16[64,256]{1,0:T(8,128)(2,1)S(1)}, bf16[64,256]{1,0:T(8,128)(2,1)S(1)}, f32[96,1024]{1,0:T(8,128)S(1)}) custom-call(s32[7]{0:T(128)S(1)} %stack.27.scalar_ref, bf16[64,1024]{1,0:T(8,128)(2,1)S(1)} %bitcast.17, bf16[48,1024]{1,0:T(8,128)(2,1)S(1)} %collective-permute-done.low_ref, ...), custom_call_target="tpu_custom_call" | custom-call | tf_op jit(solution)/shard_map/cotangent/pallas_call | solution.py:242
  32.2 5.3 %all-to-all-done.1.context_ref = bf16[8,128,128]{2,1,0:T(8,128)(2,1)S(1)} async-done(((bf16[8,128,128]{2,1,0:T(8,128)(2,1)}), bf16[8,128,128]{2,1,0:T(8,128)(2,1)S(1)}, u32[]{:S(2)}, u32[]{:S(2)}) %all-to-all-start.1) | async-done | bytes 262176 | tf_op jit(solution)/shard_map/all_to_all | solution.py:713
  37.5 0.0 copy-done
  37.5 0.0 copy-done.2
  37.5 0.0 copy-done.3
  37.5 5.8 %forward.1 = (f32[64,1024]{1,0:T(8,128)S(1)}, f32[64,1024]{1,0:T(8,128)S(1)}, bf16[64,1024]{1,0:T(8,128)(2,1)S(1)}, bf16[64,1024]{1,0:T(8,128)(2,1)S(1)}, f32[64...) custom-call(s32[7]{0:T(128)S(1)} %stack.27.scalar_ref, ...), custom_call_target="tpu_custom_call" | custom-call | tf_op jit(solution)/shard_map/forward/pallas_call | solution.py:352
  43.4 1.5 %collective-permute-start.2 = (bf16[64,1280]{1,0:T(8,128)(2,1)S(1)}, bf16[64,1280]{1,0:T(8,128)(2,1)S(1)}, u32[]{:S(2)}, u32[]{:S(2)}) collective-permute-start(bf16[64,1280]{1,0:T(8,128)(2,1)S(1)} %get-tuple-element.86), channel_id=1, source_target_pairs={{0,1},{1,0},{2,3},{3,2},{4,5},{5,4},{6,7},{7,6},{8,9},{9,8},{10,11... | collective-permute-start | bytes 491528 | tf_op jit(solution)/shard_map/ppermute | solution.py:674
  44.8 1.5 %collective-permute-start.3 = (bf16[64,1280]{1,0:T(8,128)(2,1)S(1)}, bf16[64,1280]{1,0:T(8,128)(2,1)S(1)}, u32[]{:S(2)}, u32[]{:S(2)}) collective-permute-start(bf16[64,1280]{1,0:T(8,128)(2,1)S(1)} %get-tuple-element.87), channel_id=1, source_target_pairs={{0,16},{16,0},{1,17},{17,1},{2,18},{18,2},{3,19},{19,3},{4,20},{20... | collective-permute-start | bytes 491528 | tf_op jit(solution)/shard_map/ppermute | solution.py:674
  46.3 0.6 collective-permute-start.4
  46.9 0.9 %collective-permute-start.6 = (bf16[64,1024]{1,0:T(8,128)(2,1)S(1)}, bf16[64,1024]{1,0:T(8,128)(2,1)S(1)}, u32[]{:S(2)}, u32[]{:S(2)}) collective-permute-start(bf16[64,1024]{1,0:T(8,128)(2,1)S(1)} %get-tuple-element.110.refs_0_), channel_id=1, source_target_pairs={{0,4},{2,6},{4,0},{6,2},{1,5},{3,7},{5,1},{7,3},{8,12},{10,14},{12... | collective-permute-start | bytes 393224 | tf_op jit(solution)/shard_map/ppermute | solution.py:674
  47.8 0.6 collective-permute-start.5
  48.4 5.0 %backward.1 = bf16[8,88,256]{2,1,0:T(8,128)(2,1)} custom-call(s32[7]{0:T(128)S(1)} %stack.27.scalar_ref, f32[96,1024]{1,0:T(8,128)S(1)} %get-tuple-element.90.act_grad_ref, f32[64,1024]{1,0:T(8,128)S(1)} %get-tuple-element.91.one_ref, f32[64,1024]{1,0:T(8,128)S(1)} %get-tuple-element.92.linear_ref, f32[64,1024]{1,0:T(8,128)S(1)} %get-tuple-element.93.gate_ref, ...), custom_call_target="tpu_custom_call" | custom-call | tf_op jit(solution)/shard_map/backward/pallas_call | solution.py:500
  53.4 0.8 collective-permute-done.6.refs_2_
  54.2 0.0 collective-permute-done.5.refs_1_
  54.2 0.0 collective-permute-done.2.refs_1_
  54.2 0.0 collective-permute-done.3.refs_2_
  54.2 0.0 collective-permute-done.4.refs_3_
  54.2 3.5 %all-to-all-start.2 = ((bf16[8,88,256]{2,1,0:T(8,128)(2,1)}), bf16[8,88,256]{2,1,0:T(8,128)(2,1)S(1)}, u32[]{:S(2)}, u32[]{:S(2)}) async-start(bf16[8,88,256]{2,1,0:T(8,128)(2,1)} %backward.1), calls=%async_computation.2 | async-start | bytes 720896 | tf_op jit(solution)/shard_map/all_to_all | solution.py:735
  57.7 0.3 down_products.1
  58.0 0.5 collective-permute-start.11
  58.5 0.1 collective-permute-start.8
  58.6 0.4 collective-permute-start.9
  59.0 0.1 collective-permute-start.10
  59.1 1.9 %collective-permute-start.7 = (bf16[64,1024]{1,0:T(8,128)(2,1)S(1)}, bf16[64,1024]{1,0:T(8,128)(2,1)S(1)}, u32[]{:S(2)}, u32[]{:S(2)}) collective-permute-start(bf16[64,1024]{1,0:T(8,128)(2,1)S(1)} %collective-permute-done.6.refs_2_), channel_id=1, source_target_pairs={{0,2},{2,0},{4,6},{6,4},{1,3},{3,1},{5,7},{7,5},{8,10},{10,8},{12,... | collective-permute-start | bytes 393224 | tf_op jit(solution)/shard_map/ppermute | solution.py:674
  61.1 0.0 collective-permute-done.11.other_ref
  61.1 0.6 down_shares.1
  61.7 0.0 collective-permute-done.8.refs_4_
  61.7 0.0 collective-permute-done.9.refs_5_
  61.7 0.0 collective-permute-done.10.refs_6_
  61.7 5.6 %collective-permute-done.7.refs_3_ = bf16[64,1024]{1,0:T(8,128)(2,1)S(1)} collective-permute-done((bf16[64,1024]{1,0:T(8,128)(2,1)S(1)}, bf16[64,1024]{1,0:T(8,128)(2,1)S(1)}, u32[]{:S(2)}, u32[]{:S(2)}) %collective-permute-start.7) | collective-permute-done | bytes 131104 | tf_op jit(solution)/shard_map/ppermute | solution.py:674
  67.4 0.0 collective-permute-start.12
  67.4 1.3 %collective-permute-done.12.refs_7_ = bf16[64,1024]{1,0:T(8,128)(2,1)S(1)} collective-permute-done((bf16[64,1024]{1,0:T(8,128)(2,1)S(1)}, bf16[64,1024]{1,0:T(8,128)(2,1)S(1)}, u32[]{:S(2)}, u32[]{:S(2)}) %collective-permute-start.12) | collective-permute-done | bytes 131104 | tf_op jit(solution)/shard_map/ppermute | solution.py:674
  68.7 0.3 all-to-all-done.2.message_ref
  69.0 1.8 %up_products.1 = bf16[4,72,1024]{2,1,0:T(8,128)(2,1)} custom-call(s32[7]{0:T(128)S(1)} %stack.27.scalar_ref, bf16[8,88,256]{2,1,0:T(8,128)(2,1)S(1)} %all-to-all-done.2.message_ref, bf16[64,1024]{1,0:T(8,128)(2,1)S(1)} %get-tuple-element.110.refs_0_, bf16[64,1024]{1,0:T(8,128)(2,1)S(1)} %collective-permute-done.5.refs_1_, ...), custom_call_target="tpu_custom_call" | custom-call | tf_op jit(solution)/shard_map/up_products/pallas_call | solution.py:548
  70.8 3.6 %all-to-all-start.3 = ((bf16[4,72,1024]{2,1,0:T(8,128)(2,1)}), bf16[4,72,1024]{2,1,0:T(8,128)(2,1)S(1)}, u32[]{:S(2)}, u32[]{:S(2)}) async-start(bf16[4,72,1024]{2,1,0:T(8,128)(2,1)} %up_products.1), calls=%async_computation.3 | async-start | bytes 1179648 | tf_op jit(solution)/shard_map/all_to_all | solution.py:745
  74.4 2.2 %collective-permute-start.13 = (bf16[32,1024]{1,0:T(8,128)(2,1)S(1)}, bf16[32,1024]{1,0:T(8,128)(2,1)S(1)}, u32[]{:S(2)}, u32[]{:S(2)}) collective-permute-start(bf16[32,1024]{1,0:T(8,128)(2,1)S(1)} %get-tuple-element.118), channel_id=1, source_target_pairs={{0,2},{2,0},{4,6},{6,4},{1,3},{3,1},{5,7},{7,5},{8,10},{10,8},{12,... | collective-permute-start | bytes 196616 | tf_op jit(solution)/shard_map/ppermute | solution.py:674
  76.7 2.3 %collective-permute-start.14 = (bf16[32,1024]{1,0:T(8,128)(2,1)S(1)}, bf16[32,1024]{1,0:T(8,128)(2,1)S(1)}, u32[]{:S(2)}, u32[]{:S(2)}) collective-permute-start(bf16[32,1024]{1,0:T(8,128)(2,1)S(1)} %get-tuple-element.119), channel_id=1, source_target_pairs={{0,4},{2,6},{4,0},{6,2},{1,5},{3,7},{5,1},{7,3},{8,12},{10,14},{12... | collective-permute-start | bytes 196616 | tf_op jit(solution)/shard_map/ppermute | solution.py:674
  79.0 1.1 %collective-permute-start.15 = (bf16[32,1024]{1,0:T(8,128)(2,1)S(1)}, bf16[32,1024]{1,0:T(8,128)(2,1)S(1)}, u32[]{:S(2)}, u32[]{:S(2)}) collective-permute-start(bf16[32,1024]{1,0:T(8,128)(2,1)S(1)} %get-tuple-element.120), channel_id=1, source_target_pairs={{0,6},{2,4},{4,2},{6,0},{1,7},{3,5},{5,3},{7,1},{8,14},{10,12},{12... | collective-permute-start | bytes 196616 | tf_op jit(solution)/shard_map/ppermute | solution.py:674
  80.1 2.7 %block_out.1 = bf16[64,1024]{1,0:T(8,128)(2,1)} custom-call(f32[64,1024]{1,0:T(8,128)S(1)} %get-tuple-element.80.hidden_ref, bf16[64,1024]{1,0:T(8,128)(2,1)S(1)} %get-tuple-element.81.activated_ref.act_ref, bf16[1024,1024]{1,0:T(8,128)(2,1)} %down_ref.1), custom_call_target="tpu_custom_call" | custom-call | tf_op jit(solution)/shard_map/block_out/pallas_call | solution.py:482
  82.8 0.0 collective-permute-done.13.refs_1_
  82.8 0.0 collective-permute-done.14.refs_2_
  82.8 2.3 %collective-permute-done.15.refs_3_ = bf16[32,1024]{1,0:T(8,128)(2,1)S(1)} collective-permute-done((bf16[32,1024]{1,0:T(8,128)(2,1)S(1)}, bf16[32,1024]{1,0:T(8,128)(2,1)S(1)}, u32[]{:S(2)}, u32[]{:S(2)}) %collective-permute-start.15) | collective-permute-done | bytes 65568 | tf_op jit(solution)/shard_map/ppermute | solution.py:674
  85.1 0.0 all-to-all-done.3.parts_ref
  85.1 1.4 %sums.1 = (f32[64,1024]{1,0:T(8,128)}, f32[32,1024]{1,0:T(8,128)}, f32[32,31]{1,0:T(8,128)}, f32[1,32]{1,0:T(1,128)}, f32[1,32]{1,0:T(1,128)}) custom-call(s32[7]{0:T(128)S(1)} %stack.27.scalar_ref, bf16[4,72,1024]{2,1,0:T(8,128)(2,1)S(1)} %all-to-all-done.3.parts_ref, bf16[32,1024]{1,0:T(8,128)(2,1)S(1)} %get-tuple-element.117.refs_0_, ...), custom_call_target="tpu_custom_call" | custom-call | tf_op jit(solution)/shard_map/sums/pallas_call | solution.py:656
  (1 shorter events, 0.0 us)
Async XLA Ops:
  0.6 28.6 %copy-start.1 = (bf16[64,1,1024]{2,0,1:T(8,128)(2,1)S(1)}, bf16[64,1,1024]{2,0,1:T(8,128)(2,1)}, u32[]{:S(2)}) copy-start(bf16[64,1,1024]{2,0,1:T(8,128)(2,1)} %param.19) | copy-start | bytes 393220
  2.4 20.0 %all-to-all-start = ((bf16[8,64,384]{2,1,0:T(8,128)(2,1)}), bf16[8,64,384]{2,1,0:T(8,128)(2,1)S(1)}, u32[]{:S(2)}, u32[]{:S(2)}) async-start(bf16[8,64,384]{2,1,0:T(8,128)(2,1)} %split_heads.1), calls=%async_computation | async-start | bytes 786432 | tf_op jit(solution)/shard_map/all_to_all | solution.py:704
  9.7 27.8 %copy-start = (f32[31,1024]{1,0:T(8,128)S(1)}, f32[31,1024]{1,0:T(8,128)}, u32[]{:S(2)}) copy-start(f32[31,1024]{1,0:T(8,128)} %taps_ref.3) | copy-start | bytes 380932
  9.7 27.8 %copy-start.2 = (f32[1024]{0:T(1024)S(1)}, f32[1024]{0:T(1024)}, u32[]{:S(2)}) copy-start(f32[1024]{0:T(1024)} %param.16) | copy-start | bytes 12292
  9.7 27.7 %copy-start.3 = (f32[1024]{0:T(1024)S(1)}, f32[1024]{0:T(1024)}, u32[]{:S(2)}) copy-start(f32[1024]{0:T(1024)} %param.13) | copy-start | bytes 12292
  10.7 6.4 %collective-permute-start = (bf16[48,1024]{1,0:T(8,128)(2,1)S(1)}, bf16[48,1024]{1,0:T(8,128)(2,1)S(1)}, u32[]{:S(2)}, u32[]{:S(2)}) collective-permute-start(bf16[48,1024]{1,0:T(8,128)(2,1)S(1)} %get-tuple-element.66), channel_id=1, source_target_pairs={{0,1},{1,2},{2,3},{3,4},{4,5},{5,6},{6,7},{8,9},{9,10},{10,11},{11... | collective-permute-start | bytes 294920 | tf_op jit(solution)/shard_map/ppermute | solution.py:708
  14.6 7.0 %collective-permute-start.1 = (bf16[48,1024]{1,0:T(8,128)(2,1)S(1)}, bf16[48,1024]{1,0:T(8,128)(2,1)S(1)}, u32[]{:S(2)}, u32[]{:S(2)}) collective-permute-start(bf16[48,1024]{1,0:T(8,128)(2,1)S(1)} %get-tuple-element.67), channel_id=1, source_target_pairs={{1,0},{2,1},{3,2},{4,3},{5,4},{6,5},{7,6},{9,8},{10,9},{11,10},{12... | collective-permute-start | bytes 294920 | tf_op jit(solution)/shard_map/ppermute | solution.py:709
  24.7 12.7 %all-to-all-start.1 = ((bf16[8,128,128]{2,1,0:T(8,128)(2,1)}), bf16[8,128,128]{2,1,0:T(8,128)(2,1)S(1)}, u32[]{:S(2)}, u32[]{:S(2)}) async-start(bf16[8,128,128]{2,1,0:T(8,128)(2,1)} %attend.1), calls=%async_computation.1 | async-start | bytes 524288 | tf_op jit(solution)/shard_map/all_to_all | solution.py:713
  43.4 10.8 %collective-permute-start.2 = (bf16[64,1280]{1,0:T(8,128)(2,1)S(1)}, bf16[64,1280]{1,0:T(8,128)(2,1)S(1)}, u32[]{:S(2)}, u32[]{:S(2)}) collective-permute-start(bf16[64,1280]{1,0:T(8,128)(2,1)S(1)} %get-tuple-element.86), channel_id=1, source_target_pairs={{0,1},{1,0},{2,3},{3,2},{4,5},{5,4},{6,7},{7,6},{8,9},{9,8},{10,11... | collective-permute-start | bytes 491528 | tf_op jit(solution)/shard_map/ppermute | solution.py:674
  44.8 9.4 %collective-permute-start.3 = (bf16[64,1280]{1,0:T(8,128)(2,1)S(1)}, bf16[64,1280]{1,0:T(8,128)(2,1)S(1)}, u32[]{:S(2)}, u32[]{:S(2)}) collective-permute-start(bf16[64,1280]{1,0:T(8,128)(2,1)S(1)} %get-tuple-element.87), channel_id=1, source_target_pairs={{0,16},{16,0},{1,17},{17,1},{2,18},{18,2},{3,19},{19,3},{4,20},{20... | collective-permute-start | bytes 491528 | tf_op jit(solution)/shard_map/ppermute | solution.py:674
  46.3 7.9 %collective-permute-start.4 = (bf16[64,1280]{1,0:T(8,128)(2,1)S(1)}, bf16[64,1280]{1,0:T(8,128)(2,1)S(1)}, u32[]{:S(2)}, u32[]{:S(2)}) collective-permute-start(bf16[64,1280]{1,0:T(8,128)(2,1)S(1)} %get-tuple-element.88), channel_id=1, source_target_pairs={{0,17},{1,16},{16,1},{17,0},{2,19},{3,18},{18,3},{19,2},{4,21},{5,... | collective-permute-start | bytes 491528 | tf_op jit(solution)/shard_map/ppermute | solution.py:725
  46.9 7.3 %collective-permute-start.6 = (bf16[64,1024]{1,0:T(8,128)(2,1)S(1)}, bf16[64,1024]{1,0:T(8,128)(2,1)S(1)}, u32[]{:S(2)}, u32[]{:S(2)}) collective-permute-start(bf16[64,1024]{1,0:T(8,128)(2,1)S(1)} %get-tuple-element.110.refs_0_), channel_id=1, source_target_pairs={{0,4},{2,6},{4,0},{6,2},{1,5},{3,7},{5,1},{7,3},{8,12},{10,14},{12... | collective-permute-start | bytes 393224 | tf_op jit(solution)/shard_map/ppermute | solution.py:674
  47.8 6.4 %collective-permute-start.5 = (bf16[64,1024]{1,0:T(8,128)(2,1)S(1)}, bf16[64,1024]{1,0:T(8,128)(2,1)S(1)}, u32[]{:S(2)}, u32[]{:S(2)}) collective-permute-start(bf16[64,1024]{1,0:T(8,128)(2,1)S(1)} %get-tuple-element.110.refs_0_), channel_id=1, source_target_pairs={{0,2},{2,0},{4,6},{6,4},{1,3},{3,1},{5,7},{7,5},{8,10},{10,8},{12,... | collective-permute-start | bytes 393224 | tf_op jit(solution)/shard_map/ppermute | solution.py:674
  54.2 14.8 %all-to-all-start.2 = ((bf16[8,88,256]{2,1,0:T(8,128)(2,1)}), bf16[8,88,256]{2,1,0:T(8,128)(2,1)S(1)}, u32[]{:S(2)}, u32[]{:S(2)}) async-start(bf16[8,88,256]{2,1,0:T(8,128)(2,1)} %backward.1), calls=%async_computation.2 | async-start | bytes 720896 | tf_op jit(solution)/shard_map/all_to_all | solution.py:735
  58.0 3.1 %collective-permute-start.11 = (bf16[128,1024]{1,0:T(8,128)(2,1)S(1)}, bf16[128,1024]{1,0:T(8,128)(2,1)S(1)}, u32[]{:S(2)}, u32[]{:S(2)}) collective-permute-start(bf16[128,1024]{1,0:T(8,128)(2,1)S(1)} %get-tuple-element.105), channel_id=1, source_target_pairs={{0,8},{8,0},{1,9},{9,1},{2,10},{10,2},{3,11},{11,3},{4,12},{12,4},... | collective-permute-start | bytes 786440 | tf_op jit(solution)/shard_map/ppermute | solution.py:674
  58.5 3.2 %collective-permute-start.8 = (bf16[64,1024]{1,0:T(8,128)(2,1)S(1)}, bf16[64,1024]{1,0:T(8,128)(2,1)S(1)}, u32[]{:S(2)}, u32[]{:S(2)}) collective-permute-start(bf16[64,1024]{1,0:T(8,128)(2,1)S(1)} %get-tuple-element.110.refs_0_), channel_id=1, source_target_pairs={{0,8},{8,0},{1,9},{9,1},{2,10},{10,2},{3,11},{11,3},{4,12},{12,4},... | collective-permute-start | bytes 393224 | tf_op jit(solution)/shard_map/ppermute | solution.py:674
  58.6 3.1 %collective-permute-start.9 = (bf16[64,1024]{1,0:T(8,128)(2,1)S(1)}, bf16[64,1024]{1,0:T(8,128)(2,1)S(1)}, u32[]{:S(2)}, u32[]{:S(2)}) collective-permute-start(bf16[64,1024]{1,0:T(8,128)(2,1)S(1)} %collective-permute-done.5.refs_1_), channel_id=1, source_target_pairs={{0,8},{8,0},{1,9},{9,1},{2,10},{10,2},{3,11},{11,3},{4,12},{12,4},... | collective-permute-start | bytes 393224 | tf_op jit(solution)/shard_map/ppermute | solution.py:674
  59.0 2.7 %collective-permute-start.10 = (bf16[64,1024]{1,0:T(8,128)(2,1)S(1)}, bf16[64,1024]{1,0:T(8,128)(2,1)S(1)}, u32[]{:S(2)}, u32[]{:S(2)}) collective-permute-start(bf16[64,1024]{1,0:T(8,128)(2,1)S(1)} %collective-permute-done.6.refs_2_), channel_id=1, source_target_pairs={{0,8},{8,0},{1,9},{9,1},{2,10},{10,2},{3,11},{11,3},{4,12},{12,4},... | collective-permute-start | bytes 393224 | tf_op jit(solution)/shard_map/ppermute | solution.py:674
  59.1 8.3 %collective-permute-start.7 = (bf16[64,1024]{1,0:T(8,128)(2,1)S(1)}, bf16[64,1024]{1,0:T(8,128)(2,1)S(1)}, u32[]{:S(2)}, u32[]{:S(2)}) collective-permute-start(bf16[64,1024]{1,0:T(8,128)(2,1)S(1)} %collective-permute-done.6.refs_2_), channel_id=1, source_target_pairs={{0,2},{2,0},{4,6},{6,4},{1,3},{3,1},{5,7},{7,5},{8,10},{10,8},{12,... | collective-permute-start | bytes 393224 | tf_op jit(solution)/shard_map/ppermute | solution.py:674
  67.4 1.3 %collective-permute-start.12 = (bf16[64,1024]{1,0:T(8,128)(2,1)S(1)}, bf16[64,1024]{1,0:T(8,128)(2,1)S(1)}, u32[]{:S(2)}, u32[]{:S(2)}) collective-permute-start(bf16[64,1024]{1,0:T(8,128)(2,1)S(1)} %collective-permute-done.7.refs_3_), channel_id=1, source_target_pairs={{0,8},{8,0},{1,9},{9,1},{2,10},{10,2},{3,11},{11,3},{4,12},{12,4},... | collective-permute-start | bytes 393224 | tf_op jit(solution)/shard_map/ppermute | solution.py:674
  70.8 14.3 %all-to-all-start.3 = ((bf16[4,72,1024]{2,1,0:T(8,128)(2,1)}), bf16[4,72,1024]{2,1,0:T(8,128)(2,1)S(1)}, u32[]{:S(2)}, u32[]{:S(2)}) async-start(bf16[4,72,1024]{2,1,0:T(8,128)(2,1)} %up_products.1), calls=%async_computation.3 | async-start | bytes 1179648 | tf_op jit(solution)/shard_map/all_to_all | solution.py:745
  74.4 8.4 %collective-permute-start.13 = (bf16[32,1024]{1,0:T(8,128)(2,1)S(1)}, bf16[32,1024]{1,0:T(8,128)(2,1)S(1)}, u32[]{:S(2)}, u32[]{:S(2)}) collective-permute-start(bf16[32,1024]{1,0:T(8,128)(2,1)S(1)} %get-tuple-element.118), channel_id=1, source_target_pairs={{0,2},{2,0},{4,6},{6,4},{1,3},{3,1},{5,7},{7,5},{8,10},{10,8},{12,... | collective-permute-start | bytes 196616 | tf_op jit(solution)/shard_map/ppermute | solution.py:674
  76.7 6.2 %collective-permute-start.14 = (bf16[32,1024]{1,0:T(8,128)(2,1)S(1)}, bf16[32,1024]{1,0:T(8,128)(2,1)S(1)}, u32[]{:S(2)}, u32[]{:S(2)}) collective-permute-start(bf16[32,1024]{1,0:T(8,128)(2,1)S(1)} %get-tuple-element.119), channel_id=1, source_target_pairs={{0,4},{2,6},{4,0},{6,2},{1,5},{3,7},{5,1},{7,3},{8,12},{10,14},{12... | collective-permute-start | bytes 196616 | tf_op jit(solution)/shard_map/ppermute | solution.py:674
  79.0 6.1 %collective-permute-start.15 = (bf16[32,1024]{1,0:T(8,128)(2,1)S(1)}, bf16[32,1024]{1,0:T(8,128)(2,1)S(1)}, u32[]{:S(2)}, u32[]{:S(2)}) collective-permute-start(bf16[32,1024]{1,0:T(8,128)(2,1)S(1)} %get-tuple-element.120), channel_id=1, source_target_pairs={{0,6},{2,4},{4,2},{6,0},{1,7},{3,5},{5,3},{7,1},{8,14},{10,12},{12... | collective-permute-start | bytes 196616 | tf_op jit(solution)/shard_map/ppermute | solution.py:674

commit v5 on v4

--- a/solution.py
+++ b/solution.py
@@ -155,7 +155,7 @@
     count = qkv_ref.shape[1] // (3 * head_size)
     ctx, wide, _ = out_ref.shape
     places = lax.broadcasted_iota(jnp.int32, (1, length), 1)
-    bias = jnp.where(places < scalar_ref[0], 0.0, -jnp.inf)
+    bias = jnp.where(places < scalar_ref[:, 0:1], 0.0, -jnp.inf)
     scores = []
     for m in range(count):
         base = 3 * head_size * m
@@ -193,7 +193,7 @@
     return pl.pallas_call(
         functools.partial(attend_kernel, head_size, frames),
         out_shape=struct((ctx, wide, qkv.shape[1] // 3), jnp.bfloat16),
-        in_specs=[SMEM, VMEM],
+        in_specs=[VMEM, VMEM],
         out_specs=VMEM,
         compiler_params=params(16),
         name="attend",
@@ -209,8 +209,8 @@
     edge = MARGIN // 2
     whole = jnp.concatenate([low_ref[MARGIN:, :], grad_ref[...], high_ref[MARGIN:, :]], axis=0)
     near = whole.shape[0]
-    place = scalar_ref[1] - edge + lax.broadcasted_iota(jnp.int32, (near, width), 0)
-    valid = (place >= 0) & (place < scalar_ref[0])
+    place = scalar_ref[:, 1:2] - edge + lax.broadcasted_iota(jnp.int32, (near, width), 0)
+    valid = (place >= 0) & (place < scalar_ref[:, 0:1])
     whole = jnp.where(valid, whole.astype(jnp.float32), 0.0).astype(jnp.bfloat16)
     cot = whole[edge : edge + frames]
     count, _, span = held_ref.shape
@@ -224,7 +224,7 @@
             ],
             axis=1,
         )
-    dhi, dlo, clo = scalar_ref[5], scalar_ref[2], scalar_ref[6]
+    dhi, dlo, clo = lax.axis_index("dhi"), lax.axis_index("dlo"), lax.axis_index("clo")
     for k, cols_ref in enumerate(cols_refs):
         for side in range(2):
             group = ((dhi ^ (k // 2)) * 2 + (dlo ^ side)) * 2 + (clo ^ (k % 2))
@@ -242,7 +242,7 @@
     return pl.pallas_call(
         cot_kernel,
         out_shape=(cols, cols, cols, cols, struct((frames + MARGIN, width), jnp.float32)),
-        in_specs=[SMEM, VMEM, VMEM, VMEM, HBM],
+        in_specs=[VMEM, VMEM, VMEM, VMEM, HBM],
         out_specs=(VMEM,) * 5,
         scratch_shapes=[
             pltpu.VMEM((8, frames, width // 8), grad.dtype),
@@ -303,8 +303,8 @@
             own_ref[rows, :] = scaled
     for copy in copies:
         copy.wait()
-    place = scalar_ref[1] - MARGIN + lax.broadcasted_iota(jnp.int32, (wide, span), 0)
-    valid = (place >= 0) & (place < scalar_ref[0])
+    place = scalar_ref[:, 1:2] - MARGIN + lax.broadcasted_iota(jnp.int32, (wide, span), 0)
+    valid = (place >= 0) & (place < scalar_ref[:, 0:1])
     own = slice(MARGIN, MARGIN + frames)
     for i in range(width // span):
         cols = slice(i * span, (i + 1) * span)
@@ -362,7 +362,7 @@
             struct((near, width), f32),
             struct((near, 128), f32),
         ),
-        in_specs=[SMEM, VMEM, HBM, VMEM, VMEM, HBM, VMEM, HBM, VMEM, VMEM],
+        in_specs=[VMEM, VMEM, HBM, VMEM, VMEM, HBM, VMEM, HBM, VMEM, VMEM],
         out_specs=(VMEM,) * 9,
         scratch_shapes=[
             pltpu.VMEM((wide, width), bf),
@@ -414,8 +414,8 @@
     small_ref[32:, :] = jnp.zeros((16, width), jnp.float32)
     small_ref[taps + 1 : taps + 2, :] = two
 
-    place = scalar_ref[1] + lax.broadcasted_iota(jnp.int32, (frames, 128), 0)
-    valid = place < scalar_ref[0]
+    place = scalar_ref[:, 1:2] + lax.broadcasted_iota(jnp.int32, (frames, 128), 0)
+    valid = place < scalar_ref[:, 0:1]
 
     def lanes(i):
         cols = slice(i * 128, (i + 1) * 128)
@@ -500,7 +500,7 @@
     return pl.pallas_call(
         back_kernel,
         out_shape=struct((width // 128, frames + 24, 256), bf),
-        in_specs=[SMEM] + [VMEM] * 9 + [HBM],
+        in_specs=[VMEM] * 10 + [HBM],
         out_specs=VMEM,
         scratch_shapes=[
             pltpu.VMEM((near, width), f32),
@@ -517,10 +517,10 @@
 TURNED = (((0,), (0,)), ((), ()))
 
 
-def up_kernel(count, scalar_ref, message_ref, *refs):
+def up_kernel(count, message_ref, *refs):
     parts_ref, cols_ref, one_ref = refs[2 * count :]
     frames, width = refs[0].shape
-    core, line = scalar_ref[2], scalar_ref[3]
+    core, line = lax.axis_index("dlo"), lax.axis_index("chi")
     small = jnp.zeros((24, 256), jnp.float32)
     for side in range(2):
         for k in range(count):
@@ -535,12 +535,15 @@
     small = small.astype(jnp.bfloat16)
     for s in range(4):
         parts_ref[s, :64, :] = up[s * 64 : (s + 1) * 64]
-        for i in range(3):
-            parts_ref[s, 64:, i * 256 : (i + 1) * 256] = small[i * 8 : (i + 1) * 8]
+        for i in range(6):
+            at = (i // 3) * 128 + s * 32
+            parts_ref[s, 64:, i * 128 : (i + 1) * 128] = jnp.concatenate(
+                [small[(i % 3) * 8 : (i % 3 + 1) * 8, at : at + 32]] * 4, axis=1
+            )
         parts_ref[s, 64:, 768:] = jnp.zeros((8, width - 768), jnp.bfloat16)
 
 
-def up_part(scalars, message, pieces):
+def up_part(message, pieces):
     count = len(pieces) // 2
     frames, width = pieces[0].shape
     bf = jnp.bfloat16
@@ -548,12 +551,12 @@
     return pl.pallas_call(
         functools.partial(up_kernel, count),
         out_shape=struct((4, 72, width), bf),
-        in_specs=[SMEM, VMEM] + [VMEM] * len(pieces),
+        in_specs=[VMEM] * (1 + len(pieces)),
         out_specs=VMEM,
         scratch_shapes=[pltpu.VMEM((rows, 256), bf), pltpu.VMEM((rows, width), bf)],
         compiler_params=params(12),
         name="up_products",
-    )(scalars, message, *pieces)
+    )(message, *pieces)
 
 
 def pack_kernel(act_ref, *refs):
@@ -605,29 +608,29 @@
     )(*pieces)
 
 
-def share_kernel(scalar_ref, mine_ref, other_ref, *refs):
+def share_kernel(mine_ref, other_ref, *refs):
     outs, total_ref = refs[:-1], refs[-1]
     total_ref[...] = mine_ref[...].astype(jnp.float32) + other_ref[...].astype(jnp.float32)
     for k, out in enumerate(outs):
-        at = pl.multiple_of((scalar_ref[3] ^ k) * 32, 32)
+        at = pl.multiple_of((lax.axis_index("chi") ^ k) * 32, 32)
         out[...] = total_ref[pl.ds(at, 32), :].astype(jnp.bfloat16)
 
 
-def share_part(scalars, mine, other):
+def share_part(mine, other):
     rows, width = mine.shape
     count = rows // 32
     return pl.pallas_call(
         share_kernel,
         out_shape=(struct((32, width), jnp.bfloat16),) * count,
-        in_specs=[SMEM, VMEM, VMEM],
+        in_specs=[VMEM, VMEM],
         out_specs=(VMEM,) * count,
         scratch_shapes=[pltpu.VMEM((rows, width), jnp.float32)],
         compiler_params=params(),
         name="down_shares",
-    )(scalars, mine, other)
-
-
-def sum_kernel(taps, scalar_ref, parts_ref, *refs):
+    )(mine, other)
+
+
+def sum_kernel(taps, parts_ref, *refs):
     pieces, (up_ref, down_ref, kernel_ref, one_ref, two_ref) = refs[:4], refs[4:]
     total = parts_ref[0].astype(jnp.float32)
     for s in range(1, parts_ref.shape[0]):
@@ -637,20 +640,14 @@
         pieces[2][...].astype(jnp.float32) + pieces[3][...].astype(jnp.float32)
     )
     small = jnp.concatenate(
-        [
-            total[64:72, i * 256 + part * 128 : i * 256 + part * 128 + 128]
-            for part in range(2)
-            for i in range(3)
-        ],
-        axis=0,
-    )
-    small = pltpu.roll(small, (128 - 32 * scalar_ref[4]) % 128, 1)
+        [total[64:72, i * 128 : (i + 1) * 128] for i in range(6)], axis=0
+    )
     kernel_ref[...] = jnp.transpose(small[:32])[:32, :taps]
     one_ref[...] = small[taps : taps + 1, :32]
     two_ref[...] = small[taps + 1 : taps + 2, :32]
 
 
-def sum_part(scalars, parts, pieces, taps):
+def sum_part(parts, pieces, taps):
     width = parts.shape[2]
     f32 = jnp.float32
     return pl.pallas_call(
@@ -662,11 +659,11 @@
             struct((1, 32), f32),
             struct((1, 32), f32),
         ),
-        in_specs=[SMEM] + [VMEM] * 5,
+        in_specs=[VMEM] * 5,
         out_specs=(VMEM,) * 5,
         compiler_params=params(),
         name="sums",
-    )(scalars, parts, *pieces)
+    )(parts, *pieces)
 
 
 def flipped(rows, axis, bit):
@@ -688,13 +685,7 @@
     ctx = chi * clo
     head_size = width // HEADS
     me = lax.axis_index(CTX)
-    second = lax.axis_index("dhi") * clo + lax.axis_index("clo")
-    scalars = jnp.stack(
-        [
-            lengths[0], me * frames, lax.axis_index("dlo"), lax.axis_index("chi"), second,
-            lax.axis_index("dhi"), lax.axis_index("clo"),
-        ]
-    ).astype(jnp.int32)
+    scalars = jnp.stack([lengths[0], me * frames]).astype(jnp.int32).reshape(1, 2)
     res = residual.reshape(frames, width)
     grad = out_grad.reshape(frames, width)
     gain_one = gain_one.reshape(1, width)
@@ -735,16 +726,16 @@
     message = lax.all_to_all(message, FIRST, split_axis=0, concat_axis=0, tiled=True)
     one_last = flipped(one_far, "chi", 1)
     mine, theirs = down_part([packed, *received], width)
-    downs = share_part(scalars, mine, flipped(theirs, "dlo", 1))
+    downs = share_part(mine, flipped(theirs, "dlo", 1))
     early = with_swapped([scaled, one_near, one_far])
     one_last, early, downs = lax.optimization_barrier((one_last, early, downs))
     last = with_swapped([one_last])
     ones = early[:3] + last[:1] + early[3:] + last[1:]
     downs = [downs[0]] + [flipped(downs[k], "chi", k) for k in range(1, chi)]
-    parts = up_part(scalars, message, ones)
+    parts = up_part(message, ones)
     parts = lax.all_to_all(parts, SECOND, split_axis=0, concat_axis=0, tiled=True)
     block_out = block_part(hidden, activated, down_weight)
-    up_grad, down_grad, kernel_grad, one, two = sum_part(scalars, parts, downs, taps)
+    up_grad, down_grad, kernel_grad, one, two = sum_part(parts, downs, taps)
     return (
         block_out.reshape(frames, 1, width), up_grad, down_grad, kernel_grad,
         one.reshape(-1), two.reshape(-1),

time: 87.1 us -> 84.8 us (0.974)
  Pallas kernels: 25.7 us -> 22.1 us
  waiting for transfers between devices: 21.4 us -> 22.8 us
    ppermute x13, waiting for transfers between devices: 10 us -> 11 us  [flipped(): return lax.ppermute(rows, axis, [(i, i ^ bit) for i in range(size)])]
  transfers between devices with their start and end apart: 20 -> 20, of which waited for: 9 -> 9; matrix products, arithmetic and copies ran while one was open for 0% -> 0% of each run, Pallas kernels for 14% -> 13%
where the time goes in v5:
time: 84.8 us; the launch traced here: 84.1 us
  starting transfers between devices  37.7 us (44%)
  waiting for transfers between devices  22.8 us (27%)
  Pallas kernels  22.1 us (26%)
  between operations  1.49 us (2%)
    ppermute x13, starting transfers between devices, flipped(): return lax.ppermute(rows, axis, [(i, i ^ bit) for i in range(size)])  13.3 us
    ppermute x13, waiting for transfers between devices, flipped(): return lax.ppermute(rows, axis, [(i, i ^ bit) for i in range(size)])  11 us
    all_to_all x1, starting transfers between devices, small_device(): qkv = lax.all_to_all(qkv, CTX, split_axis=0, concat_axis=0, tiled=True)  7.29 us
    all_to_all x1, waiting for transfers between devices, small_device(): lax.all_to_all(windows, CTX, split_axis=0, concat_axis=0, tiled=True)  5.72 us
    pallas_call x1, Pallas kernels, forward_part(): pl.pallas_call(forward_kernel, out_shape=(struct((frames, width), f32), s...  5.2 us
    pallas_call x1, Pallas kernels, back_part(): pl.pallas_call(back_kernel, out_shape=struct((width // 128, frames + 24,...  4.62 us
    all_to_all x1, starting transfers between devices, small_device(): lax.all_to_all(windows, CTX, split_axis=0, concat_axis=0, tiled=True)  4.49 us
    ppermute x1, waiting for transfers between devices, small_device(): after = lax.ppermute(low, CTX, down)  4.46 us
  transfers between devices with their start and end apart: 20, of which 9 were waited for; matrix products, arithmetic and copies ran while one was open for 0% of the time, Pallas kernels for 13%

profile of v5, /device:TPU:0, one launch (start us, length us, event | category | flops | bytes accessed | tf_op | source)
XLA Modules:
  0.0 84.1 jit_solution(9334903159448670067)
XLA Ops:
  0.6 0.0 copy-start.1
  0.6 1.8 %split_heads.1 = bf16[8,64,384]{2,1,0:T(8,128)(2,1)} custom-call(bf16[64,3072]{1,0:T(8,128)(2,1)} %bitcast.20), custom_call_target="tpu_custom_call" | custom-call | tf_op jit(solution)/shard_map/split_heads/pallas_call | solution.py:111
  2.4 7.3 %all-to-all-start = ((bf16[8,64,384]{2,1,0:T(8,128)(2,1)}), bf16[8,64,384]{2,1,0:T(8,128)(2,1)S(1)}, u32[]{:S(2)}, u32[]{:S(2)}) async-start(bf16[8,64,384]{2,1,0:T(8,128)(2,1)} %split_heads.1), calls=%async_computation | async-start | bytes 786432 | tf_op jit(solution)/shard_map/all_to_all | solution.py:695
  9.7 0.0 copy-start
  9.7 0.0 copy-start.2
  9.7 0.0 copy-start.3
  9.7 1.0 %edges.1 = (bf16[48,1024]{1,0:T(8,128)(2,1)S(1)}, bf16[48,1024]{1,0:T(8,128)(2,1)S(1)}) custom-call(bf16[64,1024]{1,0:T(8,128)(2,1)} %bitcast.18, bf16[64,1024]{1,0:T(8,128)(2,1)} %bitcast.13), custom_call_target="tpu_custom_call" | custom-call | tf_op jit(solution)/shard_map/edges/pallas_call | solution.py:142
  10.7 3.9 %collective-permute-start = (bf16[48,1024]{1,0:T(8,128)(2,1)S(1)}, bf16[48,1024]{1,0:T(8,128)(2,1)S(1)}, u32[]{:S(2)}, u32[]{:S(2)}) collective-permute-start(bf16[48,1024]{1,0:T(8,128)(2,1)S(1)} %get-tuple-element.66), channel_id=1, source_target_pairs={{0,1},{1,2},{2,3},{3,4},{4,5},{5,6},{6,7},{8,9},{9,10},{10,11},{11... | collective-permute-start | bytes 294920 | tf_op jit(solution)/shard_map/ppermute | solution.py:699
  14.6 1.3 %collective-permute-start.1 = (bf16[48,1024]{1,0:T(8,128)(2,1)S(1)}, bf16[48,1024]{1,0:T(8,128)(2,1)S(1)}, u32[]{:S(2)}, u32[]{:S(2)}) collective-permute-start(bf16[48,1024]{1,0:T(8,128)(2,1)S(1)} %get-tuple-element.67), channel_id=1, source_target_pairs={{1,0},{2,1},{3,2},{4,3},{5,4},{6,5},{7,6},{9,8},{10,9},{11,10},{12... | collective-permute-start | bytes 294920 | tf_op jit(solution)/shard_map/ppermute | solution.py:700
  16.6 0.1 add_bitcast_fusion.scalar_ref
  16.6 0.5 collective-permute-done.low_ref
  17.1 4.5 %collective-permute-done.1.high_ref = bf16[48,1024]{1,0:T(8,128)(2,1)S(1)} collective-permute-done((bf16[48,1024]{1,0:T(8,128)(2,1)S(1)}, bf16[48,1024]{1,0:T(8,128)(2,1)S(1)}, u32[]{:S(2)}, u32[]{:S(2)}) %collective-permute-start.1) | collective-permute-done | bytes 98336 | tf_op jit(solution)/shard_map/ppermute | solution.py:700
  21.6 0.8 %all-to-all-done = bf16[8,64,384]{2,1,0:T(8,128)(2,1)S(1)} async-done(((bf16[8,64,384]{2,1,0:T(8,128)(2,1)}), bf16[8,64,384]{2,1,0:T(8,128)(2,1)S(1)}, u32[]{:S(2)}, u32[]{:S(2)}) %all-to-all-start) | async-done | bytes 393248 | tf_op jit(solution)/shard_map/all_to_all | solution.py:695
  22.4 1.7 %attend.1 = bf16[8,128,128]{2,1,0:T(8,128)(2,1)} custom-call(s32[1,2]{1,0:T(1,128)S(1)} %add_bitcast_fusion.scalar_ref, bf16[512,384]{1,0:T(8,128)(2,1)S(1)} %bitcast.12), custom_call_target="tpu_custom_call" | custom-call | tf_op jit(solution)/shard_map/attend/pallas_call | solution.py:193
  24.2 4.5 %all-to-all-start.1 = ((bf16[8,128,128]{2,1,0:T(8,128)(2,1)}), bf16[8,128,128]{2,1,0:T(8,128)(2,1)S(1)}, u32[]{:S(2)}, u32[]{:S(2)}) async-start(bf16[8,128,128]{2,1,0:T(8,128)(2,1)} %attend.1), calls=%async_computation.1 | async-start | bytes 524288 | tf_op jit(solution)/shard_map/all_to_all | solution.py:704
  28.7 0.0 copy-done.1
  28.7 2.5 %cotangent.1 = (bf16[64,256]{1,0:T(8,128)(2,1)S(1)}, bf16[64,256]{1,0:T(8,128)(2,1)S(1)}, bf16[64,256]{1,0:T(8,128)(2,1)S(1)}, bf16[64,256]{1,0:T(8,128)(2,1)S(1)}, f32[96,1024]{1,0:T(8,128)S(1)}) custom-call(s32[1,2]{1,0:T(1,128)S(1)} %add_bitcast_fusion.scalar_ref, bf16[64,1024]{1,0:T(8,128)(2,1)S(1)} %bitcast.14, ...), custom_call_target="tpu_custom_call" | custom-call | tf_op jit(solution)/shard_map/cotangent/pallas_call | solution.py:242
  31.2 5.7 %all-to-all-done.1.context_ref = bf16[8,128,128]{2,1,0:T(8,128)(2,1)S(1)} async-done(((bf16[8,128,128]{2,1,0:T(8,128)(2,1)}), bf16[8,128,128]{2,1,0:T(8,128)(2,1)S(1)}, u32[]{:S(2)}, u32[]{:S(2)}) %all-to-all-start.1) | async-done | bytes 262176 | tf_op jit(solution)/shard_map/all_to_all | solution.py:704
  36.9 0.0 copy-done
  36.9 0.0 copy-done.2
  36.9 0.0 copy-done.3
  36.9 5.2 %forward.1 = (f32[64,1024]{1,0:T(8,128)S(1)}, f32[64,1024]{1,0:T(8,128)S(1)}, bf16[64,1024]{1,0:T(8,128)(2,1)S(1)}, bf16[64,1024]{1,0:T(8,128)(2,1)S(1)}, f32[64...) custom-call(s32[1,2]{1,0:T(1,128)S(1)} %add_bitcast_fusion.scalar_re, ...), custom_call_target="tpu_custom_call" | custom-call | tf_op jit(solution)/shard_map/forward/pallas_call | solution.py:352
  42.2 1.5 %collective-permute-start.2 = (bf16[64,1280]{1,0:T(8,128)(2,1)S(1)}, bf16[64,1280]{1,0:T(8,128)(2,1)S(1)}, u32[]{:S(2)}, u32[]{:S(2)}) collective-permute-start(bf16[64,1280]{1,0:T(8,128)(2,1)S(1)} %get-tuple-element.86), channel_id=1, source_target_pairs={{0,1},{1,0},{2,3},{3,2},{4,5},{5,4},{6,7},{7,6},{8,9},{9,8},{10,11... | collective-permute-start | bytes 491528 | tf_op jit(solution)/shard_map/ppermute | solution.py:671
  43.7 1.5 %collective-permute-start.3 = (bf16[64,1280]{1,0:T(8,128)(2,1)S(1)}, bf16[64,1280]{1,0:T(8,128)(2,1)S(1)}, u32[]{:S(2)}, u32[]{:S(2)}) collective-permute-start(bf16[64,1280]{1,0:T(8,128)(2,1)S(1)} %get-tuple-element.87), channel_id=1, source_target_pairs={{0,16},{16,0},{1,17},{17,1},{2,18},{18,2},{3,19},{19,3},{4,20},{20... | collective-permute-start | bytes 491528 | tf_op jit(solution)/shard_map/ppermute | solution.py:671
  45.2 0.6 collective-permute-start.4
  45.7 0.9 %collective-permute-start.6 = (bf16[64,1024]{1,0:T(8,128)(2,1)S(1)}, bf16[64,1024]{1,0:T(8,128)(2,1)S(1)}, u32[]{:S(2)}, u32[]{:S(2)}) collective-permute-start(bf16[64,1024]{1,0:T(8,128)(2,1)S(1)} %get-tuple-element.110.refs_0_), channel_id=1, source_target_pairs={{0,4},{2,6},{4,0},{6,2},{1,5},{3,7},{5,1},{7,3},{8,12},{10,14},{12... | collective-permute-start | bytes 393224 | tf_op jit(solution)/shard_map/ppermute | solution.py:671
  46.6 0.6 collective-permute-start.5
  47.3 4.6 %backward.1 = bf16[8,88,256]{2,1,0:T(8,128)(2,1)} custom-call(s32[1,2]{1,0:T(1,128)S(1)} %add_bitcast_fusion.scalar_ref, f32[96,1024]{1,0:T(8,128)S(1)} %get-tuple-element.90.act_grad_ref, f32[64,1024]{1,0:T(8,128)S(1)} %get-tuple-element.91.one_ref, f32[64,1024]{1,0:T(8,128)S(1)} %get-tuple-element.92.linear_ref, ...), custom_call_target="tpu_custom_call" | custom-call | tf_op jit(solution)/shard_map/backward/pallas_call | solution.py:500
  51.9 1.1 %collective-permute-done.6.refs_2_ = bf16[64,1024]{1,0:T(8,128)(2,1)S(1)} collective-permute-done((bf16[64,1024]{1,0:T(8,128)(2,1)S(1)}, bf16[64,1024]{1,0:T(8,128)(2,1)S(1)}, u32[]{:S(2)}, u32[]{:S(2)}) %collective-permute-start.6) | collective-permute-done | bytes 131104 | tf_op jit(solution)/shard_map/ppermute | solution.py:671
  53.0 0.0 collective-permute-done.5.refs_1_
  53.0 0.0 collective-permute-done.2.refs_1_
  53.0 0.0 collective-permute-done.3.refs_2_
  53.0 0.0 collective-permute-done.4.refs_3_
  53.0 3.5 %all-to-all-start.2 = ((bf16[8,88,256]{2,1,0:T(8,128)(2,1)}), bf16[8,88,256]{2,1,0:T(8,128)(2,1)S(1)}, u32[]{:S(2)}, u32[]{:S(2)}) async-start(bf16[8,88,256]{2,1,0:T(8,128)(2,1)} %backward.1), calls=%async_computation.2 | async-start | bytes 720896 | tf_op jit(solution)/shard_map/all_to_all | solution.py:726
  56.5 0.3 down_products.1
  56.8 0.5 collective-permute-start.11
  57.3 0.1 collective-permute-start.8
  57.4 0.4 collective-permute-start.9
  57.8 0.1 collective-permute-start.10
  57.9 1.9 %collective-permute-start.7 = (bf16[64,1024]{1,0:T(8,128)(2,1)S(1)}, bf16[64,1024]{1,0:T(8,128)(2,1)S(1)}, u32[]{:S(2)}, u32[]{:S(2)}) collective-permute-start(bf16[64,1024]{1,0:T(8,128)(2,1)S(1)} %collective-permute-done.6.refs_2_), channel_id=1, source_target_pairs={{0,2},{2,0},{4,6},{6,4},{1,3},{3,1},{5,7},{7,5},{8,10},{10,8},{12,... | collective-permute-start | bytes 393224 | tf_op jit(solution)/shard_map/ppermute | solution.py:671
  59.8 0.0 collective-permute-done.11.other_ref
  59.8 0.1 down_shares.1
  59.9 0.0 collective-permute-done.8.refs_4_
  59.9 0.0 collective-permute-done.9.refs_5_
  60.0 0.0 collective-permute-done.10.refs_6_
  60.0 6.2 %collective-permute-done.7.refs_3_ = bf16[64,1024]{1,0:T(8,128)(2,1)S(1)} collective-permute-done((bf16[64,1024]{1,0:T(8,128)(2,1)S(1)}, bf16[64,1024]{1,0:T(8,128)(2,1)S(1)}, u32[]{:S(2)}, u32[]{:S(2)}) %collective-permute-start.7) | collective-permute-done | bytes 131104 | tf_op jit(solution)/shard_map/ppermute | solution.py:671
  66.2 0.0 collective-permute-start.12
  66.2 1.3 %collective-permute-done.12.refs_7_ = bf16[64,1024]{1,0:T(8,128)(2,1)S(1)} collective-permute-done((bf16[64,1024]{1,0:T(8,128)(2,1)S(1)}, bf16[64,1024]{1,0:T(8,128)(2,1)S(1)}, u32[]{:S(2)}, u32[]{:S(2)}) %collective-permute-start.12) | collective-permute-done | bytes 131104 | tf_op jit(solution)/shard_map/ppermute | solution.py:671
  67.5 0.3 all-to-all-done.2.message_ref
  67.8 1.3 %up_products.1 = bf16[4,72,1024]{2,1,0:T(8,128)(2,1)} custom-call(bf16[8,88,256]{2,1,0:T(8,128)(2,1)S(1)} %all-to-all-done.2.message_ref, bf16[64,1024]{1,0:T(8,128)(2,1)S(1)} %get-tuple-element.110.refs_0_, bf16[64,1024]{1,0:T(8,128)(2,1)S(1)} %collective-permute-done.5.refs_1_, bf16[64,1024]{1,0:T(8,128)(2,1)S(1)} %collective-permute-done.6.refs_2_, ...), custom_call_target="tpu_custom_call" | custom-call | tf_op jit(solution)/shard_map/up_products/pallas_call | solution.py:551
  69.1 3.5 %all-to-all-start.3 = ((bf16[4,72,1024]{2,1,0:T(8,128)(2,1)}), bf16[4,72,1024]{2,1,0:T(8,128)(2,1)S(1)}, u32[]{:S(2)}, u32[]{:S(2)}) async-start(bf16[4,72,1024]{2,1,0:T(8,128)(2,1)} %up_products.1), calls=%async_computation.3 | async-start | bytes 1179648 | tf_op jit(solution)/shard_map/all_to_all | solution.py:736
  72.6 2.3 %collective-permute-start.13 = (bf16[32,1024]{1,0:T(8,128)(2,1)S(1)}, bf16[32,1024]{1,0:T(8,128)(2,1)S(1)}, u32[]{:S(2)}, u32[]{:S(2)}) collective-permute-start(bf16[32,1024]{1,0:T(8,128)(2,1)S(1)} %get-tuple-element.118), channel_id=1, source_target_pairs={{0,2},{2,0},{4,6},{6,4},{1,3},{3,1},{5,7},{7,5},{8,10},{10,8},{12,... | collective-permute-start | bytes 196616 | tf_op jit(solution)/shard_map/ppermute | solution.py:671
  74.9 2.3 %collective-permute-start.14 = (bf16[32,1024]{1,0:T(8,128)(2,1)S(1)}, bf16[32,1024]{1,0:T(8,128)(2,1)S(1)}, u32[]{:S(2)}, u32[]{:S(2)}) collective-permute-start(bf16[32,1024]{1,0:T(8,128)(2,1)S(1)} %get-tuple-element.119), channel_id=1, source_target_pairs={{0,4},{2,6},{4,0},{6,2},{1,5},{3,7},{5,1},{7,3},{8,12},{10,14},{12... | collective-permute-start | bytes 196616 | tf_op jit(solution)/shard_map/ppermute | solution.py:671
  77.2 1.2 %collective-permute-start.15 = (bf16[32,1024]{1,0:T(8,128)(2,1)S(1)}, bf16[32,1024]{1,0:T(8,128)(2,1)S(1)}, u32[]{:S(2)}, u32[]{:S(2)}) collective-permute-start(bf16[32,1024]{1,0:T(8,128)(2,1)S(1)} %get-tuple-element.120), channel_id=1, source_target_pairs={{0,6},{2,4},{4,2},{6,0},{1,7},{3,5},{5,3},{7,1},{8,14},{10,12},{12... | collective-permute-start | bytes 196616 | tf_op jit(solution)/shard_map/ppermute | solution.py:671
  78.3 2.7 %block_out.1 = bf16[64,1024]{1,0:T(8,128)(2,1)} custom-call(f32[64,1024]{1,0:T(8,128)S(1)} %get-tuple-element.80.hidden_ref, bf16[64,1024]{1,0:T(8,128)(2,1)S(1)} %get-tuple-element.81.activated_ref.act_ref, bf16[1024,1024]{1,0:T(8,128)(2,1)} %down_ref.1), custom_call_target="tpu_custom_call" | custom-call | tf_op jit(solution)/shard_map/block_out/pallas_call | solution.py:482
  81.0 0.0 collective-permute-done.13.refs_1_
  81.0 0.0 collective-permute-done.14.refs_2_
  81.0 2.3 %collective-permute-done.15.refs_3_ = bf16[32,1024]{1,0:T(8,128)(2,1)S(1)} collective-permute-done((bf16[32,1024]{1,0:T(8,128)(2,1)S(1)}, bf16[32,1024]{1,0:T(8,128)(2,1)S(1)}, u32[]{:S(2)}, u32[]{:S(2)}) %collective-permute-start.15) | collective-permute-done | bytes 65568 | tf_op jit(solution)/shard_map/ppermute | solution.py:671
  83.3 0.0 all-to-all-done.3.parts_ref
  83.3 0.8 sums.1
  (1 shorter events, 0.0 us)
Async XLA Ops:
  0.6 28.1 %copy-start.1 = (bf16[64,1,1024]{2,0,1:T(8,128)(2,1)S(1)}, bf16[64,1,1024]{2,0,1:T(8,128)(2,1)}, u32[]{:S(2)}) copy-start(bf16[64,1,1024]{2,0,1:T(8,128)(2,1)} %param.19) | copy-start | bytes 393220
  2.4 20.0 %all-to-all-start = ((bf16[8,64,384]{2,1,0:T(8,128)(2,1)}), bf16[8,64,384]{2,1,0:T(8,128)(2,1)S(1)}, u32[]{:S(2)}, u32[]{:S(2)}) async-start(bf16[8,64,384]{2,1,0:T(8,128)(2,1)} %split_heads.1), calls=%async_computation | async-start | bytes 786432 | tf_op jit(solution)/shard_map/all_to_all | solution.py:695
  9.7 27.2 %copy-start = (f32[31,1024]{1,0:T(8,128)S(1)}, f32[31,1024]{1,0:T(8,128)}, u32[]{:S(2)}) copy-start(f32[31,1024]{1,0:T(8,128)} %taps_ref.3) | copy-start | bytes 380932
  9.7 27.2 %copy-start.2 = (f32[1024]{0:T(1024)S(1)}, f32[1024]{0:T(1024)}, u32[]{:S(2)}) copy-start(f32[1024]{0:T(1024)} %param.16) | copy-start | bytes 12292
  9.7 27.2 %copy-start.3 = (f32[1024]{0:T(1024)S(1)}, f32[1024]{0:T(1024)}, u32[]{:S(2)}) copy-start(f32[1024]{0:T(1024)} %param.13) | copy-start | bytes 12292
  10.7 6.4 %collective-permute-start = (bf16[48,1024]{1,0:T(8,128)(2,1)S(1)}, bf16[48,1024]{1,0:T(8,128)(2,1)S(1)}, u32[]{:S(2)}, u32[]{:S(2)}) collective-permute-start(bf16[48,1024]{1,0:T(8,128)(2,1)S(1)} %get-tuple-element.66), channel_id=1, source_target_pairs={{0,1},{1,2},{2,3},{3,4},{4,5},{5,6},{6,7},{8,9},{9,10},{10,11},{11... | collective-permute-start | bytes 294920 | tf_op jit(solution)/shard_map/ppermute | solution.py:699
  14.6 7.0 %collective-permute-start.1 = (bf16[48,1024]{1,0:T(8,128)(2,1)S(1)}, bf16[48,1024]{1,0:T(8,128)(2,1)S(1)}, u32[]{:S(2)}, u32[]{:S(2)}) collective-permute-start(bf16[48,1024]{1,0:T(8,128)(2,1)S(1)} %get-tuple-element.67), channel_id=1, source_target_pairs={{1,0},{2,1},{3,2},{4,3},{5,4},{6,5},{7,6},{9,8},{10,9},{11,10},{12... | collective-permute-start | bytes 294920 | tf_op jit(solution)/shard_map/ppermute | solution.py:700
  24.2 12.7 %all-to-all-start.1 = ((bf16[8,128,128]{2,1,0:T(8,128)(2,1)}), bf16[8,128,128]{2,1,0:T(8,128)(2,1)S(1)}, u32[]{:S(2)}, u32[]{:S(2)}) async-start(bf16[8,128,128]{2,1,0:T(8,128)(2,1)} %attend.1), calls=%async_computation.1 | async-start | bytes 524288 | tf_op jit(solution)/shard_map/all_to_all | solution.py:704
  42.2 10.8 %collective-permute-start.2 = (bf16[64,1280]{1,0:T(8,128)(2,1)S(1)}, bf16[64,1280]{1,0:T(8,128)(2,1)S(1)}, u32[]{:S(2)}, u32[]{:S(2)}) collective-permute-start(bf16[64,1280]{1,0:T(8,128)(2,1)S(1)} %get-tuple-element.86), channel_id=1, source_target_pairs={{0,1},{1,0},{2,3},{3,2},{4,5},{5,4},{6,7},{7,6},{8,9},{9,8},{10,11... | collective-permute-start | bytes 491528 | tf_op jit(solution)/shard_map/ppermute | solution.py:671
  43.7 9.4 %collective-permute-start.3 = (bf16[64,1280]{1,0:T(8,128)(2,1)S(1)}, bf16[64,1280]{1,0:T(8,128)(2,1)S(1)}, u32[]{:S(2)}, u32[]{:S(2)}) collective-permute-start(bf16[64,1280]{1,0:T(8,128)(2,1)S(1)} %get-tuple-element.87), channel_id=1, source_target_pairs={{0,16},{16,0},{1,17},{17,1},{2,18},{18,2},{3,19},{19,3},{4,20},{20... | collective-permute-start | bytes 491528 | tf_op jit(solution)/shard_map/ppermute | solution.py:671
  45.2 7.9 %collective-permute-start.4 = (bf16[64,1280]{1,0:T(8,128)(2,1)S(1)}, bf16[64,1280]{1,0:T(8,128)(2,1)S(1)}, u32[]{:S(2)}, u32[]{:S(2)}) collective-permute-start(bf16[64,1280]{1,0:T(8,128)(2,1)S(1)} %get-tuple-element.88), channel_id=1, source_target_pairs={{0,17},{1,16},{16,1},{17,0},{2,19},{3,18},{18,3},{19,2},{4,21},{5,... | collective-permute-start | bytes 491528 | tf_op jit(solution)/shard_map/ppermute | solution.py:716
  45.7 7.3 %collective-permute-start.6 = (bf16[64,1024]{1,0:T(8,128)(2,1)S(1)}, bf16[64,1024]{1,0:T(8,128)(2,1)S(1)}, u32[]{:S(2)}, u32[]{:S(2)}) collective-permute-start(bf16[64,1024]{1,0:T(8,128)(2,1)S(1)} %get-tuple-element.110.refs_0_), channel_id=1, source_target_pairs={{0,4},{2,6},{4,0},{6,2},{1,5},{3,7},{5,1},{7,3},{8,12},{10,14},{12... | collective-permute-start | bytes 393224 | tf_op jit(solution)/shard_map/ppermute | solution.py:671
  46.6 6.4 %collective-permute-start.5 = (bf16[64,1024]{1,0:T(8,128)(2,1)S(1)}, bf16[64,1024]{1,0:T(8,128)(2,1)S(1)}, u32[]{:S(2)}, u32[]{:S(2)}) collective-permute-start(bf16[64,1024]{1,0:T(8,128)(2,1)S(1)} %get-tuple-element.110.refs_0_), channel_id=1, source_target_pairs={{0,2},{2,0},{4,6},{6,4},{1,3},{3,1},{5,7},{7,5},{8,10},{10,8},{12,... | collective-permute-start | bytes 393224 | tf_op jit(solution)/shard_map/ppermute | solution.py:671
  53.0 14.8 %all-to-all-start.2 = ((bf16[8,88,256]{2,1,0:T(8,128)(2,1)}), bf16[8,88,256]{2,1,0:T(8,128)(2,1)S(1)}, u32[]{:S(2)}, u32[]{:S(2)}) async-start(bf16[8,88,256]{2,1,0:T(8,128)(2,1)} %backward.1), calls=%async_computation.2 | async-start | bytes 720896 | tf_op jit(solution)/shard_map/all_to_all | solution.py:726
  56.8 3.0 %collective-permute-start.11 = (bf16[128,1024]{1,0:T(8,128)(2,1)S(1)}, bf16[128,1024]{1,0:T(8,128)(2,1)S(1)}, u32[]{:S(2)}, u32[]{:S(2)}) collective-permute-start(bf16[128,1024]{1,0:T(8,128)(2,1)S(1)} %get-tuple-element.105), channel_id=1, source_target_pairs={{0,8},{8,0},{1,9},{9,1},{2,10},{10,2},{3,11},{11,3},{4,12},{12,4},... | collective-permute-start | bytes 786440 | tf_op jit(solution)/shard_map/ppermute | solution.py:671
  57.3 2.6 %collective-permute-start.8 = (bf16[64,1024]{1,0:T(8,128)(2,1)S(1)}, bf16[64,1024]{1,0:T(8,128)(2,1)S(1)}, u32[]{:S(2)}, u32[]{:S(2)}) collective-permute-start(bf16[64,1024]{1,0:T(8,128)(2,1)S(1)} %get-tuple-element.110.refs_0_), channel_id=1, source_target_pairs={{0,8},{8,0},{1,9},{9,1},{2,10},{10,2},{3,11},{11,3},{4,12},{12,4},... | collective-permute-start | bytes 393224 | tf_op jit(solution)/shard_map/ppermute | solution.py:671
  57.4 2.6 %collective-permute-start.9 = (bf16[64,1024]{1,0:T(8,128)(2,1)S(1)}, bf16[64,1024]{1,0:T(8,128)(2,1)S(1)}, u32[]{:S(2)}, u32[]{:S(2)}) collective-permute-start(bf16[64,1024]{1,0:T(8,128)(2,1)S(1)} %collective-permute-done.5.refs_1_), channel_id=1, source_target_pairs={{0,8},{8,0},{1,9},{9,1},{2,10},{10,2},{3,11},{11,3},{4,12},{12,4},... | collective-permute-start | bytes 393224 | tf_op jit(solution)/shard_map/ppermute | solution.py:671
  57.8 2.1 %collective-permute-start.10 = (bf16[64,1024]{1,0:T(8,128)(2,1)S(1)}, bf16[64,1024]{1,0:T(8,128)(2,1)S(1)}, u32[]{:S(2)}, u32[]{:S(2)}) collective-permute-start(bf16[64,1024]{1,0:T(8,128)(2,1)S(1)} %collective-permute-done.6.refs_2_), channel_id=1, source_target_pairs={{0,8},{8,0},{1,9},{9,1},{2,10},{10,2},{3,11},{11,3},{4,12},{12,4},... | collective-permute-start | bytes 393224 | tf_op jit(solution)/shard_map/ppermute | solution.py:671
  57.9 8.3 %collective-permute-start.7 = (bf16[64,1024]{1,0:T(8,128)(2,1)S(1)}, bf16[64,1024]{1,0:T(8,128)(2,1)S(1)}, u32[]{:S(2)}, u32[]{:S(2)}) collective-permute-start(bf16[64,1024]{1,0:T(8,128)(2,1)S(1)} %collective-permute-done.6.refs_2_), channel_id=1, source_target_pairs={{0,2},{2,0},{4,6},{6,4},{1,3},{3,1},{5,7},{7,5},{8,10},{10,8},{12,... | collective-permute-start | bytes 393224 | tf_op jit(solution)/shard_map/ppermute | solution.py:671
  66.2 1.3 %collective-permute-start.12 = (bf16[64,1024]{1,0:T(8,128)(2,1)S(1)}, bf16[64,1024]{1,0:T(8,128)(2,1)S(1)}, u32[]{:S(2)}, u32[]{:S(2)}) collective-permute-start(bf16[64,1024]{1,0:T(8,128)(2,1)S(1)} %collective-permute-done.7.refs_3_), channel_id=1, source_target_pairs={{0,8},{8,0},{1,9},{9,1},{2,10},{10,2},{3,11},{11,3},{4,12},{12,4},... | collective-permute-start | bytes 393224 | tf_op jit(solution)/shard_map/ppermute | solution.py:671
  69.1 14.2 %all-to-all-start.3 = ((bf16[4,72,1024]{2,1,0:T(8,128)(2,1)}), bf16[4,72,1024]{2,1,0:T(8,128)(2,1)S(1)}, u32[]{:S(2)}, u32[]{:S(2)}) async-start(bf16[4,72,1024]{2,1,0:T(8,128)(2,1)} %up_products.1), calls=%async_computation.3 | async-start | bytes 1179648 | tf_op jit(solution)/shard_map/all_to_all | solution.py:736
  72.6 8.4 %collective-permute-start.13 = (bf16[32,1024]{1,0:T(8,128)(2,1)S(1)}, bf16[32,1024]{1,0:T(8,128)(2,1)S(1)}, u32[]{:S(2)}, u32[]{:S(2)}) collective-permute-start(bf16[32,1024]{1,0:T(8,128)(2,1)S(1)} %get-tuple-element.118), channel_id=1, source_target_pairs={{0,2},{2,0},{4,6},{6,4},{1,3},{3,1},{5,7},{7,5},{8,10},{10,8},{12,... | collective-permute-start | bytes 196616 | tf_op jit(solution)/shard_map/ppermute | solution.py:671
  74.9 6.2 %collective-permute-start.14 = (bf16[32,1024]{1,0:T(8,128)(2,1)S(1)}, bf16[32,1024]{1,0:T(8,128)(2,1)S(1)}, u32[]{:S(2)}, u32[]{:S(2)}) collective-permute-start(bf16[32,1024]{1,0:T(8,128)(2,1)S(1)} %get-tuple-element.119), channel_id=1, source_target_pairs={{0,4},{2,6},{4,0},{6,2},{1,5},{3,7},{5,1},{7,3},{8,12},{10,14},{12... | collective-permute-start | bytes 196616 | tf_op jit(solution)/shard_map/ppermute | solution.py:671
  77.2 6.1 %collective-permute-start.15 = (bf16[32,1024]{1,0:T(8,128)(2,1)S(1)}, bf16[32,1024]{1,0:T(8,128)(2,1)S(1)}, u32[]{:S(2)}, u32[]{:S(2)}) collective-permute-start(bf16[32,1024]{1,0:T(8,128)(2,1)S(1)} %get-tuple-element.120), channel_id=1, source_target_pairs={{0,6},{2,4},{4,2},{6,0},{1,7},{3,5},{5,3},{7,1},{8,14},{10,12},{12... | collective-permute-start | bytes 196616 | tf_op jit(solution)/shard_map/ppermute | solution.py:671

commit v6 on v5

--- a/solution.py
+++ b/solution.py
@@ -201,7 +201,14 @@
 
 
 def cot_kernel(scalar_ref, grad_ref, low_ref, high_ref, weight_ref, *refs):
-    cols_refs, (act_ref, held_ref, weight_held_ref, sems) = refs[:4], refs[4:]
+    out_ref, cols_refs = refs[0], refs[1:5]
+    act_ref, ready_ref, held_ref, weight_held_ref, sems, ready_sems = refs[5:]
+    ready = fetches(
+        out_ref,
+        ready_ref,
+        ready_sems,
+        [pl.ds(i * 256, 256) for i in range(ready_ref.shape[0] // 256)],
+    )
     frames, width = grad_ref.shape
     copies = fetches(
         weight_ref, weight_held_ref, sems, [pl.ds(i * 256, 256) for i in range(width // 256)]
@@ -234,28 +241,35 @@
     act_ref[...] = lax.dot_general(
         whole, weight_held_ref[...], (((1,), (1,)), ((), ())), preferred_element_type=jnp.float32
     )
-
-
-def cot_part(scalars, grad, low, high, weight):
+    for copy in ready:
+        copy.wait()
+
+
+def cot_part(scalars, grad, low, high, weight, out_weight):
     frames, width = grad.shape
     cols = struct((frames, width // 4), grad.dtype)
     return pl.pallas_call(
         cot_kernel,
-        out_shape=(cols, cols, cols, cols, struct((frames + MARGIN, width), jnp.float32)),
-        in_specs=[VMEM, VMEM, VMEM, VMEM, HBM],
-        out_specs=(VMEM,) * 5,
+        out_shape=(
+            cols, cols, cols, cols,
+            struct((frames + MARGIN, width), jnp.float32),
+            struct((width * 3 // 4, width), weight.dtype),
+        ),
+        in_specs=[VMEM, VMEM, VMEM, VMEM, HBM, HBM],
+        out_specs=(VMEM,) * 6,
         scratch_shapes=[
             pltpu.VMEM((8, frames, width // 8), grad.dtype),
             pltpu.VMEM(weight.shape, weight.dtype),
             pltpu.SemaphoreType.DMA((width // 256,)),
+            pltpu.SemaphoreType.DMA((3,)),
         ],
         compiler_params=params(12),
         name="cotangent",
-    )(scalars, grad, low, high, in_hbm(weight))
+    )(scalars, grad, low, high, in_hbm(weight), in_hbm(out_weight))
 
 
 def forward_kernel(
-    scalar_ref, context_ref, res_ref, low_ref, high_ref, out_ref, gain_one_ref, weight_ref,
+    scalar_ref, context_ref, res_ref, low_ref, high_ref, out_ref, ready_ref, gain_one_ref, weight_ref,
     taps_ref, gain_ref,
     hidden_ref, one_ref, own_ref, act_ref, linear_ref, gate_ref, glu_ref,
     normed_ref, inverse_ref, scaled_ref, conv_ref, out_held_ref, held_ref, res_held_ref, out_sems, sems, res_sems,
@@ -268,21 +282,22 @@
     near = wide - 2 * edge
     depth = 2 * lanes
     res_copies = fetches(res_ref, res_held_ref, res_sems, [slice(None)])
+    held_rows = ready_ref.shape[0]
     out_copies = fetches(
-        out_ref, out_held_ref, out_sems, [pl.ds(i * depth, depth) for i in range(ctx // 2)]
+        out_ref, out_held_ref, out_sems, [pl.ds(held_rows, width - held_rows)]
     )
     span = 256
     copies = fetches(
         weight_ref, held_ref, sems, [pl.ds(i * span, span) for i in range(width // span)]
     )
-    product = jnp.zeros((wide, width), jnp.float32)
-    for i, copy in enumerate(out_copies):
-        copy.wait()
-        product = product + jnp.dot(
-            jnp.concatenate([context_ref[2 * i], context_ref[2 * i + 1]], axis=1),
-            out_held_ref[i * depth : (i + 1) * depth, :],
-            preferred_element_type=jnp.float32,
-        )
+    context = jnp.concatenate([context_ref[i] for i in range(ctx)], axis=1)
+    product = jnp.dot(
+        context[:, :held_rows], ready_ref[...], preferred_element_type=jnp.float32
+    )
+    out_copies[0].wait()
+    product = product + jnp.dot(
+        context[:, held_rows:], out_held_ref[held_rows:, :], preferred_element_type=jnp.float32
+    )
     res_copies[0].wait()
     step = 32
     for at in range(0, wide, step):
@@ -344,7 +359,9 @@
             act_ref[rows, :] = (pre * jax.nn.sigmoid(pre)).astype(jnp.bfloat16)
 
 
-def forward_part(scalars, context, res, low, high, out_weight, gain_one, weight, taps, gain):
+def forward_part(
+    scalars, context, res, low, high, out_weight, ready, gain_one, weight, taps, gain
+):
     frames, width = res.shape
     ctx, wide, _ = context.shape
     near = wide - MARGIN
@@ -362,7 +379,7 @@
             struct((near, width), f32),
             struct((near, 128), f32),
         ),
-        in_specs=[VMEM, VMEM, HBM, VMEM, VMEM, HBM, VMEM, HBM, VMEM, VMEM],
+        in_specs=[VMEM, VMEM, HBM, VMEM, VMEM, HBM, VMEM, VMEM, HBM, VMEM, VMEM],
         out_specs=(VMEM,) * 9,
         scratch_shapes=[
             pltpu.VMEM((wide, width), bf),
@@ -377,7 +394,8 @@
         compiler_params=params(24),
         name="forward",
     )(
-        scalars, context, in_hbm(res), low, high, in_hbm(out_weight), gain_one, in_hbm(weight), taps, gain
+        scalars, context, in_hbm(res), low, high, in_hbm(out_weight), ready, gain_one,
+        in_hbm(weight), taps, gain
     )
 
 
@@ -559,22 +577,26 @@
     )(message, *pieces)
 
 
-def pack_kernel(act_ref, *refs):
-    count = len(refs) // 2
-    width = act_ref.shape[1]
-    for cols_ref, out_ref in zip(refs[:count], refs[count:]):
+def pack_kernel(act_ref, own_ref, y_ref, x_ref, xy_ref, packed_ref, to_y_ref, to_x_ref):
+    width, span = act_ref.shape[1], own_ref.shape[1]
+    for cols_ref, out_ref in ((own_ref, packed_ref), (y_ref, to_y_ref), (x_ref, to_x_ref)):
         out_ref[:, :width] = act_ref[...]
-        out_ref[:, width:] = cols_ref[...]
+        out_ref[:, width : width + span] = cols_ref[...]
+    to_x_ref[:, width + span :] = xy_ref[...]
 
 
 def pack_part(act, cols):
-    shape = struct((act.shape[0], act.shape[1] + cols[0].shape[1]), act.dtype)
-    count = len(cols)
+    rows, width = act.shape
+    span = cols[0].shape[1]
     return pl.pallas_call(
         pack_kernel,
-        out_shape=(shape,) * count,
-        in_specs=[VMEM] * (1 + count),
-        out_specs=(VMEM,) * count,
+        out_shape=(
+            struct((rows, width + span), act.dtype),
+            struct((rows, width + span), act.dtype),
+            struct((rows, width + 2 * span), act.dtype),
+        ),
+        in_specs=[VMEM] * 5,
+        out_specs=(VMEM,) * 3,
         compiler_params=params(),
         name="pack",
     )(act, *cols)
@@ -585,7 +607,11 @@
     width = mine_ref.shape[1]
     frames = pieces[0].shape[0]
     for i, piece in enumerate(pieces):
-        rows_ref[i * frames : (i + 1) * frames, :] = piece[...]
+        rows = slice(i * frames, (i + 1) * frames)
+        span = rows_ref.shape[1] - width
+        at = width + (span if i == 3 else 0)
+        rows_ref[rows, :width] = piece[:, :width]
+        rows_ref[rows, width:] = piece[:, at : at + span]
     total = lax.dot_general(
         rows_ref[:, width:], rows_ref[:, :width], TURNED, preferred_element_type=jnp.float32
     ).astype(jnp.bfloat16)
@@ -702,19 +728,17 @@
     windows = attend_windows(scalars, qkv.reshape(ctx * frames, -1), head_size, frames, ctx)
     windows, before, after = lax.optimization_barrier((windows, before, after))
     windows = lax.all_to_all(windows, CTX, split_axis=0, concat_axis=0, tiled=True)
-    *cols, act_grad = cot_part(scalars, grad, before, after, down_weight)
-    windows, act_grad, cols = lax.optimization_barrier((windows, act_grad, cols))
+    *cols, act_grad, ready = cot_part(scalars, grad, before, after, down_weight, out_weight)
+    windows, act_grad, cols, ready = lax.optimization_barrier((windows, act_grad, cols, ready))
 
     (
         hidden, normed_one, scaled, activated, linear, gate, glu, normed_two, inverse_two
     ) = forward_part(
-        scalars, windows, res, before, after, out_weight, gain_one, up_weight, conv_kernel, gain_two
-    )
-    packed, to_y, to_x, to_xy = pack_part(activated, cols)
-    pairs = [(i, i ^ 3) for i in range(4)]
-    received = [
-        flipped(to_y, "clo", 1), flipped(to_x, "dhi", 1), lax.ppermute(to_xy, SECOND, pairs)
-    ]
+        scalars, windows, res, before, after, out_weight, ready, gain_one, up_weight, conv_kernel,
+        gain_two,
+    )
+    packed, to_y, to_x = pack_part(activated, cols)
+    received = [flipped(to_y, "clo", 1), flipped(to_x, "dhi", 1)]
     one_near, one_far = flipped(scaled, "chi", 1), flipped(scaled, "chi", 2)
     message = back_part(
         scalars, act_grad, normed_one, linear, gate,
@@ -725,15 +749,17 @@
     )
     message = lax.all_to_all(message, FIRST, split_axis=0, concat_axis=0, tiled=True)
     one_last = flipped(one_far, "chi", 1)
-    mine, theirs = down_part([packed, *received], width)
+    diagonal = flipped(received[1], "clo", 1)
+    early = with_swapped([scaled, one_near, one_far])
+    early, diagonal, one_last = lax.optimization_barrier((early, diagonal, one_last))
+    mine, theirs = down_part([packed, *received, diagonal], width)
     downs = share_part(mine, flipped(theirs, "dlo", 1))
-    early = with_swapped([scaled, one_near, one_far])
-    one_last, early, downs = lax.optimization_barrier((one_last, early, downs))
     last = with_swapped([one_last])
     ones = early[:3] + last[:1] + early[3:] + last[1:]
+    parts = up_part(message, ones)
+    parts, downs = lax.optimization_barrier((parts, downs))
+    parts = lax.all_to_all(parts, SECOND, split_axis=0, concat_axis=0, tiled=True)
     downs = [downs[0]] + [flipped(downs[k], "chi", k) for k in range(1, chi)]
-    parts = up_part(message, ones)
-    parts = lax.all_to_all(parts, SECOND, split_axis=0, concat_axis=0, tiled=True)
     block_out = block_part(hidden, activated, down_weight)
     up_grad, down_grad, kernel_grad, one, two = sum_part(parts, downs, taps)
     return (

time: 84.8 us -> 84.4 us (level)
  waiting for transfers between devices: 22.8 us -> 21.1 us
  starting transfers between devices: 37.7 us -> 38.9 us
    ppermute x13 -> x14, starting transfers between devices: 13.3 us -> 14.8 us  [flipped(): return lax.ppermute(rows, axis, [(i, i ^ bit) for i in range(size)])]
    ppermute x13 -> x14, waiting for transfers between devices: 11 us -> 9.98 us  [flipped(): return lax.ppermute(rows, axis, [(i, i ^ bit) for i in range(size)])]
  transfers between devices with their start and end apart: 20 -> 20, of which waited for: 9 -> 9; matrix products, arithmetic and copies ran while one was open for 0% -> 0% of each run, Pallas kernels for 13% -> 14%
where the time goes in v6:
time: 84.4 us; the launch traced here: 83.7 us
  starting transfers between devices  38.9 us (46%)
  Pallas kernels  22.2 us (26%)
  waiting for transfers between devices  21.1 us (25%)
  between operations  1.46 us (2%)
    ppermute x14, starting transfers between devices, flipped(): return lax.ppermute(rows, axis, [(i, i ^ bit) for i in range(size)])  14.8 us
    ppermute x14, waiting for transfers between devices, flipped(): return lax.ppermute(rows, axis, [(i, i ^ bit) for i in range(size)])  9.98 us
    all_to_all x1, starting transfers between devices, small_device(): qkv = lax.all_to_all(qkv, CTX, split_axis=0, concat_axis=0, tiled=True)  7.29 us
    all_to_all x1, waiting for transfers between devices, small_device(): lax.all_to_all(windows, CTX, split_axis=0, concat_axis=0, tiled=True)  5.26 us
    pallas_call x1, Pallas kernels, forward_part(): pl.pallas_call(forward_kernel, out_shape=(struct((frames, width), f32), s...  4.96 us
    pallas_call x1, Pallas kernels, back_part(): pl.pallas_call(back_kernel, out_shape=struct((width // 128, frames + 24,...  4.62 us
    all_to_all x1, starting transfers between devices, small_device(): lax.all_to_all(windows, CTX, split_axis=0, concat_axis=0, tiled=True)  4.49 us
    ppermute x1, waiting for transfers between devices, small_device(): after = lax.ppermute(low, CTX, down)  4.44 us
  transfers between devices with their start and end apart: 20, of which 9 were waited for; matrix products, arithmetic and copies ran while one was open for 0% of the time, Pallas kernels for 14%

profile of v6, /device:TPU:0, one launch (start us, length us, event | category | flops | bytes accessed | tf_op | source)
XLA Modules:
  0.0 83.7 jit_solution(7254253223800316195)
XLA Ops:
  0.6 0.0 copy-start.1
  0.6 1.8 %split_heads.1 = bf16[8,64,384]{2,1,0:T(8,128)(2,1)} custom-call(bf16[64,3072]{1,0:T(8,128)(2,1)} %bitcast.20), custom_call_target="tpu_custom_call" | custom-call | tf_op jit(solution)/shard_map/split_heads/pallas_call | solution.py:111
  2.4 7.3 %all-to-all-start = ((bf16[8,64,384]{2,1,0:T(8,128)(2,1)}), bf16[8,64,384]{2,1,0:T(8,128)(2,1)S(1)}, u32[]{:S(2)}, u32[]{:S(2)}) async-start(bf16[8,64,384]{2,1,0:T(8,128)(2,1)} %split_heads.1), calls=%async_computation | async-start | bytes 786432 | tf_op jit(solution)/shard_map/all_to_all | solution.py:721
  9.7 0.9 %edges.1 = (bf16[48,1024]{1,0:T(8,128)(2,1)S(1)}, bf16[48,1024]{1,0:T(8,128)(2,1)S(1)}) custom-call(bf16[64,1024]{1,0:T(8,128)(2,1)} %bitcast.18, bf16[64,1024]{1,0:T(8,128)(2,1)} %bitcast.13), custom_call_target="tpu_custom_call" | custom-call | tf_op jit(solution)/shard_map/edges/pallas_call | solution.py:142
  10.6 3.9 %collective-permute-start = (bf16[48,1024]{1,0:T(8,128)(2,1)S(1)}, bf16[48,1024]{1,0:T(8,128)(2,1)S(1)}, u32[]{:S(2)}, u32[]{:S(2)}) collective-permute-start(bf16[48,1024]{1,0:T(8,128)(2,1)S(1)} %get-tuple-element.68), channel_id=1, source_target_pairs={{0,1},{1,2},{2,3},{3,4},{4,5},{5,6},{6,7},{8,9},{9,10},{10,11},{11... | collective-permute-start | bytes 294920 | tf_op jit(solution)/shard_map/ppermute | solution.py:725
  14.6 1.3 %collective-permute-start.1 = (bf16[48,1024]{1,0:T(8,128)(2,1)S(1)}, bf16[48,1024]{1,0:T(8,128)(2,1)S(1)}, u32[]{:S(2)}, u32[]{:S(2)}) collective-permute-start(bf16[48,1024]{1,0:T(8,128)(2,1)S(1)} %get-tuple-element.69), channel_id=1, source_target_pairs={{1,0},{2,1},{3,2},{4,3},{5,4},{6,5},{7,6},{9,8},{10,9},{11,10},{12... | collective-permute-start | bytes 294920 | tf_op jit(solution)/shard_map/ppermute | solution.py:726
  16.5 0.1 add_bitcast_fusion.scalar_ref
  16.6 0.6 collective-permute-done.low_ref
  17.1 4.4 %collective-permute-done.1.high_ref = bf16[48,1024]{1,0:T(8,128)(2,1)S(1)} collective-permute-done((bf16[48,1024]{1,0:T(8,128)(2,1)S(1)}, bf16[48,1024]{1,0:T(8,128)(2,1)S(1)}, u32[]{:S(2)}, u32[]{:S(2)}) %collective-permute-start.1) | collective-permute-done | bytes 98336 | tf_op jit(solution)/shard_map/ppermute | solution.py:726
  21.6 0.9 %all-to-all-done = bf16[8,64,384]{2,1,0:T(8,128)(2,1)S(1)} async-done(((bf16[8,64,384]{2,1,0:T(8,128)(2,1)}), bf16[8,64,384]{2,1,0:T(8,128)(2,1)S(1)}, u32[]{:S(2)}, u32[]{:S(2)}) %all-to-all-start) | async-done | bytes 393248 | tf_op jit(solution)/shard_map/all_to_all | solution.py:721
  22.5 1.7 %attend.1 = bf16[8,128,128]{2,1,0:T(8,128)(2,1)} custom-call(s32[1,2]{1,0:T(1,128)S(1)} %add_bitcast_fusion.scalar_ref, bf16[512,384]{1,0:T(8,128)(2,1)S(1)} %bitcast.12), custom_call_target="tpu_custom_call" | custom-call | tf_op jit(solution)/shard_map/attend/pallas_call | solution.py:193
  24.2 4.5 %all-to-all-start.1 = ((bf16[8,128,128]{2,1,0:T(8,128)(2,1)}), bf16[8,128,128]{2,1,0:T(8,128)(2,1)S(1)}, u32[]{:S(2)}, u32[]{:S(2)}) async-start(bf16[8,128,128]{2,1,0:T(8,128)(2,1)} %attend.1), calls=%async_computation.1 | async-start | bytes 524288 | tf_op jit(solution)/shard_map/all_to_all | solution.py:730
  28.7 0.0 copy-done.1
  28.7 0.0 copy-start
  28.7 0.0 copy-start.2
  28.7 0.0 copy-start.3
  28.7 2.9 %cotangent.1 = (bf16[64,256]{1,0:T(8,128)(2,1)S(1)}, bf16[64,256]{1,0:T(8,128)(2,1)S(1)}, bf16[64,256]{1,0:T(8,128)(2,1)S(1)}, bf16[64,256]{1,0:T(8,128)(2,1)S(1...) custom-call(s32[1,2]{1,0:T(1,128)S(1)} %add_bitcast_fusion.scalar_ref, bf16[64,1024]{1,0:T(8,128)(2,1)S(1)} %bitcast.14, ...), custom_call_target="tpu_custom_call" | custom-call | tf_op jit(solution)/shard_map/cotangent/pallas_call | solution.py:251
  31.6 5.3 %all-to-all-done.1.context_ref = bf16[8,128,128]{2,1,0:T(8,128)(2,1)S(1)} async-done(((bf16[8,128,128]{2,1,0:T(8,128)(2,1)}), bf16[8,128,128]{2,1,0:T(8,128)(2,1)S(1)}, u32[]{:S(2)}, u32[]{:S(2)}) %all-to-all-start.1) | async-done | bytes 262176 | tf_op jit(solution)/shard_map/all_to_all | solution.py:730
  36.9 0.0 copy-done
  36.9 0.0 copy-done.2
  36.9 0.0 copy-done.3
  36.9 5.0 %forward.1 = (f32[64,1024]{1,0:T(8,128)S(1)}, f32[64,1024]{1,0:T(8,128)S(1)}, bf16[64,1024]{1,0:T(8,128)(2,1)S(1)}, bf16[64,1024]{1,0:T(8,128)(2,1)S(1)}, f32[64...) custom-call(s32[1,2]{1,0:T(1,128)S(1)} %add_bitcast_fusion.scalar_re, ...), custom_call_target="tpu_custom_call" | custom-call | tf_op jit(solution)/shard_map/forward/pallas_call | solution.py:369
  41.9 1.6 %collective-permute-start.3 = (bf16[64,1536]{1,0:T(8,128)(2,1)S(1)}, bf16[64,1536]{1,0:T(8,128)(2,1)S(1)}, u32[]{:S(2)}, u32[]{:S(2)}) collective-permute-start(bf16[64,1536]{1,0:T(8,128)(2,1)S(1)} %get-tuple-element.91), channel_id=1, source_target_pairs={{0,16},{16,0},{1,17},{17,1},{2,18},{18,2},{3,19},{19,3},{4,20},{20... | collective-permute-start | bytes 589832 | tf_op jit(solution)/shard_map/ppermute | solution.py:697
  43.5 1.4 %collective-permute-start.2 = (bf16[64,1280]{1,0:T(8,128)(2,1)S(1)}, bf16[64,1280]{1,0:T(8,128)(2,1)S(1)}, u32[]{:S(2)}, u32[]{:S(2)}) collective-permute-start(bf16[64,1280]{1,0:T(8,128)(2,1)S(1)} %get-tuple-element.90), channel_id=1, source_target_pairs={{0,1},{1,0},{2,3},{3,2},{4,5},{5,4},{6,7},{7,6},{8,9},{9,8},{10,11... | collective-permute-start | bytes 491528 | tf_op jit(solution)/shard_map/ppermute | solution.py:697
  44.9 0.0 collective-permute-start.5
  44.9 1.9 %collective-permute-start.4 = (bf16[64,1024]{1,0:T(8,128)(2,1)S(1)}, bf16[64,1024]{1,0:T(8,128)(2,1)S(1)}, u32[]{:S(2)}, u32[]{:S(2)}) collective-permute-start(bf16[64,1024]{1,0:T(8,128)(2,1)S(1)} %get-tuple-element.104.refs_0_), channel_id=1, source_target_pairs={{0,2},{2,0},{4,6},{6,4},{1,3},{3,1},{5,7},{7,5},{8,10},{10,8},{12,... | collective-permute-start | bytes 393224 | tf_op jit(solution)/shard_map/ppermute | solution.py:697
  46.8 4.6 %backward.1 = bf16[8,88,256]{2,1,0:T(8,128)(2,1)} custom-call(s32[1,2]{1,0:T(1,128)S(1)} %add_bitcast_fusion.scalar_ref, f32[96,1024]{1,0:T(8,128)S(1)} %get-tuple-element.93.act_grad_ref, f32[64,1024]{1,0:T(8,128)S(1)} %get-tuple-element.94.one_ref, f32[64,1024]{1,0:T(8,128)S(1)} %get-tuple-element.95.linear_ref, ...), custom_call_target="tpu_custom_call" | custom-call | tf_op jit(solution)/shard_map/backward/pallas_call | solution.py:518
  51.4 0.3 collective-permute-done.5.refs_2_
  51.7 0.0 collective-permute-done.4.refs_1_
  51.7 0.0 collective-permute-done.2.refs_1_
  51.7 0.0 collective-permute-done.3.refs_2_
  51.7 3.6 %all-to-all-start.2 = ((bf16[8,88,256]{2,1,0:T(8,128)(2,1)}), bf16[8,88,256]{2,1,0:T(8,128)(2,1)S(1)}, u32[]{:S(2)}, u32[]{:S(2)}) async-start(bf16[8,88,256]{2,1,0:T(8,128)(2,1)} %backward.1), calls=%async_computation.2 | async-start | bytes 720896 | tf_op jit(solution)/shard_map/all_to_all | solution.py:750
  55.3 1.1 %collective-permute-start.9 = (bf16[64,1536]{1,0:T(8,128)(2,1)S(1)}, bf16[64,1536]{1,0:T(8,128)(2,1)S(1)}, u32[]{:S(2)}, u32[]{:S(2)}) collective-permute-start(bf16[64,1536]{1,0:T(8,128)(2,1)S(1)} %collective-permute-done.3.refs_2_), channel_id=1, source_target_pairs={{0,1},{1,0},{2,3},{3,2},{4,5},{5,4},{6,7},{7,6},{8,9},{9,8},{10,11... | collective-permute-start | bytes 589832 | tf_op jit(solution)/shard_map/ppermute | solution.py:697
  56.3 0.1 collective-permute-start.6
  56.4 0.4 collective-permute-start.7
  56.9 1.8 %collective-permute-start.10 = (bf16[64,1024]{1,0:T(8,128)(2,1)S(1)}, bf16[64,1024]{1,0:T(8,128)(2,1)S(1)}, u32[]{:S(2)}, u32[]{:S(2)}) collective-permute-start(bf16[64,1024]{1,0:T(8,128)(2,1)S(1)} %collective-permute-done.5.refs_2_), channel_id=1, source_target_pairs={{0,2},{2,0},{4,6},{6,4},{1,3},{3,1},{5,7},{7,5},{8,10},{10,8},{12,... | collective-permute-start | bytes 393224 | tf_op jit(solution)/shard_map/ppermute | solution.py:697
  58.7 0.0 collective-permute-start.8
  58.7 0.0 collective-permute-done.6.refs_4_
  58.7 0.0 collective-permute-done.7.refs_5_
  58.7 6.3 %collective-permute-done.10.refs_3_ = bf16[64,1024]{1,0:T(8,128)(2,1)S(1)} collective-permute-done((bf16[64,1024]{1,0:T(8,128)(2,1)S(1)}, bf16[64,1024]{1,0:T(8,128)(2,1)S(1)}, u32[]{:S(2)}, u32[]{:S(2)}) %collective-permute-start.10) | collective-permute-done | bytes 131104 | tf_op jit(solution)/shard_map/ppermute | solution.py:697
  65.0 0.0 collective-permute-done.8.refs_6_
  65.0 0.0 collective-permute-done.9.refs_3_
  65.0 0.3 down_products.1
  65.4 0.1 collective-permute-start.12
  65.4 0.5 collective-permute-start.11
  65.9 1.0 %collective-permute-done.12.other_ref = bf16[128,1024]{1,0:T(8,128)(2,1)S(1)} collective-permute-done((bf16[128,1024]{1,0:T(8,128)(2,1)S(1)}, bf16[128,1024]{1,0:T(8,128)(2,1)S(1)}, u32[]{:S(2)}, u32[]{:S(2)}) %collective-permute-start.12) | collective-permute-done | bytes 262176 | tf_op jit(solution)/shard_map/ppermute | solution.py:697
  67.0 0.1 down_shares.1
  67.1 0.1 collective-permute-done.11.refs_7_
  67.1 0.0 all-to-all-done.2.message_ref
  67.1 1.3 %up_products.1 = bf16[4,72,1024]{2,1,0:T(8,128)(2,1)} custom-call(bf16[8,88,256]{2,1,0:T(8,128)(2,1)S(1)} %all-to-all-done.2.message_ref, bf16[64,1024]{1,0:T(8,128)(2,1)S(1)} %get-tuple-element.104.refs_0_, bf16[64,1024]{1,0:T(8,128)(2,1)S(1)} %collective-permute-done.4.refs_1_, bf16[64,1024]{1,0:T(8,128)(2,1)S(1)} %collective-permute-done.5.refs_2_, ...), custom_call_target="tpu_custom_call" | custom-call | tf_op jit(solution)/shard_map/up_products/pallas_call | solution.py:569
  68.4 3.5 %all-to-all-start.3 = ((bf16[4,72,1024]{2,1,0:T(8,128)(2,1)}), bf16[4,72,1024]{2,1,0:T(8,128)(2,1)S(1)}, u32[]{:S(2)}, u32[]{:S(2)}) async-start(bf16[4,72,1024]{2,1,0:T(8,128)(2,1)} %up_products.1), calls=%async_computation.3 | async-start | bytes 1179648 | tf_op jit(solution)/shard_map/all_to_all | solution.py:761
  71.9 2.5 %collective-permute-start.13 = (bf16[32,1024]{1,0:T(8,128)(2,1)S(1)}, bf16[32,1024]{1,0:T(8,128)(2,1)S(1)}, u32[]{:S(2)}, u32[]{:S(2)}) collective-permute-start(bf16[32,1024]{1,0:T(8,128)(2,1)S(1)} %get-tuple-element.122), channel_id=1, source_target_pairs={{0,2},{2,0},{4,6},{6,4},{1,3},{3,1},{5,7},{7,5},{8,10},{10,8},{12,... | collective-permute-start | bytes 196616 | tf_op jit(solution)/shard_map/ppermute | solution.py:697
  74.5 2.3 %collective-permute-start.14 = (bf16[32,1024]{1,0:T(8,128)(2,1)S(1)}, bf16[32,1024]{1,0:T(8,128)(2,1)S(1)}, u32[]{:S(2)}, u32[]{:S(2)}) collective-permute-start(bf16[32,1024]{1,0:T(8,128)(2,1)S(1)} %get-tuple-element.123), channel_id=1, source_target_pairs={{0,4},{2,6},{4,0},{6,2},{1,5},{3,7},{5,1},{7,3},{8,12},{10,14},{12... | collective-permute-start | bytes 196616 | tf_op jit(solution)/shard_map/ppermute | solution.py:697
  76.8 1.1 %collective-permute-start.15 = (bf16[32,1024]{1,0:T(8,128)(2,1)S(1)}, bf16[32,1024]{1,0:T(8,128)(2,1)S(1)}, u32[]{:S(2)}, u32[]{:S(2)}) collective-permute-start(bf16[32,1024]{1,0:T(8,128)(2,1)S(1)} %get-tuple-element.124), channel_id=1, source_target_pairs={{0,6},{2,4},{4,2},{6,0},{1,7},{3,5},{5,3},{7,1},{8,14},{10,12},{12... | collective-permute-start | bytes 196616 | tf_op jit(solution)/shard_map/ppermute | solution.py:697
  77.9 2.7 %block_out.1 = bf16[64,1024]{1,0:T(8,128)(2,1)} custom-call(f32[64,1024]{1,0:T(8,128)S(1)} %get-tuple-element.84.hidden_ref, bf16[64,1024]{1,0:T(8,128)(2,1)S(1)} %get-tuple-element.85.activated_ref.act_ref, bf16[1024,1024]{1,0:T(8,128)(2,1)} %down_ref.1), custom_call_target="tpu_custom_call" | custom-call | tf_op jit(solution)/shard_map/block_out/pallas_call | solution.py:500
  80.6 0.0 collective-permute-done.13.refs_1_
  80.6 0.0 collective-permute-done.14.refs_2_
  80.6 2.3 %collective-permute-done.15.refs_3_ = bf16[32,1024]{1,0:T(8,128)(2,1)S(1)} collective-permute-done((bf16[32,1024]{1,0:T(8,128)(2,1)S(1)}, bf16[32,1024]{1,0:T(8,128)(2,1)S(1)}, u32[]{:S(2)}, u32[]{:S(2)}) %collective-permute-start.15) | collective-permute-done | bytes 65568 | tf_op jit(solution)/shard_map/ppermute | solution.py:697
  82.9 0.0 all-to-all-done.3.parts_ref
  82.9 0.8 sums.1
  (1 shorter events, 0.0 us)
Async XLA Ops:
  0.6 28.1 %copy-start.1 = (bf16[64,1,1024]{2,0,1:T(8,128)(2,1)S(1)}, bf16[64,1,1024]{2,0,1:T(8,128)(2,1)}, u32[]{:S(2)}) copy-start(bf16[64,1,1024]{2,0,1:T(8,128)(2,1)} %param.19) | copy-start | bytes 393220
  2.4 20.0 %all-to-all-start = ((bf16[8,64,384]{2,1,0:T(8,128)(2,1)}), bf16[8,64,384]{2,1,0:T(8,128)(2,1)S(1)}, u32[]{:S(2)}, u32[]{:S(2)}) async-start(bf16[8,64,384]{2,1,0:T(8,128)(2,1)} %split_heads.1), calls=%async_computation | async-start | bytes 786432 | tf_op jit(solution)/shard_map/all_to_all | solution.py:721
  10.6 6.5 %collective-permute-start = (bf16[48,1024]{1,0:T(8,128)(2,1)S(1)}, bf16[48,1024]{1,0:T(8,128)(2,1)S(1)}, u32[]{:S(2)}, u32[]{:S(2)}) collective-permute-start(bf16[48,1024]{1,0:T(8,128)(2,1)S(1)} %get-tuple-element.68), channel_id=1, source_target_pairs={{0,1},{1,2},{2,3},{3,4},{4,5},{5,6},{6,7},{8,9},{9,10},{10,11},{11... | collective-permute-start | bytes 294920 | tf_op jit(solution)/shard_map/ppermute | solution.py:725
  14.6 7.0 %collective-permute-start.1 = (bf16[48,1024]{1,0:T(8,128)(2,1)S(1)}, bf16[48,1024]{1,0:T(8,128)(2,1)S(1)}, u32[]{:S(2)}, u32[]{:S(2)}) collective-permute-start(bf16[48,1024]{1,0:T(8,128)(2,1)S(1)} %get-tuple-element.69), channel_id=1, source_target_pairs={{1,0},{2,1},{3,2},{4,3},{5,4},{6,5},{7,6},{9,8},{10,9},{11,10},{12... | collective-permute-start | bytes 294920 | tf_op jit(solution)/shard_map/ppermute | solution.py:726
  24.2 12.7 %all-to-all-start.1 = ((bf16[8,128,128]{2,1,0:T(8,128)(2,1)}), bf16[8,128,128]{2,1,0:T(8,128)(2,1)S(1)}, u32[]{:S(2)}, u32[]{:S(2)}) async-start(bf16[8,128,128]{2,1,0:T(8,128)(2,1)} %attend.1), calls=%async_computation.1 | async-start | bytes 524288 | tf_op jit(solution)/shard_map/all_to_all | solution.py:730
  28.7 8.2 %copy-start = (f32[31,1024]{1,0:T(8,128)S(1)}, f32[31,1024]{1,0:T(8,128)}, u32[]{:S(2)}) copy-start(f32[31,1024]{1,0:T(8,128)} %taps_ref.3) | copy-start | bytes 380932
  28.7 8.2 %copy-start.2 = (f32[1024]{0:T(1024)S(1)}, f32[1024]{0:T(1024)}, u32[]{:S(2)}) copy-start(f32[1024]{0:T(1024)} %param.16) | copy-start | bytes 12292
  28.7 8.2 %copy-start.3 = (f32[1024]{0:T(1024)S(1)}, f32[1024]{0:T(1024)}, u32[]{:S(2)}) copy-start(f32[1024]{0:T(1024)} %param.13) | copy-start | bytes 12292
  41.9 9.8 %collective-permute-start.3 = (bf16[64,1536]{1,0:T(8,128)(2,1)S(1)}, bf16[64,1536]{1,0:T(8,128)(2,1)S(1)}, u32[]{:S(2)}, u32[]{:S(2)}) collective-permute-start(bf16[64,1536]{1,0:T(8,128)(2,1)S(1)} %get-tuple-element.91), channel_id=1, source_target_pairs={{0,16},{16,0},{1,17},{17,1},{2,18},{18,2},{3,19},{19,3},{4,20},{20... | collective-permute-start | bytes 589832 | tf_op jit(solution)/shard_map/ppermute | solution.py:697
  43.5 8.2 %collective-permute-start.2 = (bf16[64,1280]{1,0:T(8,128)(2,1)S(1)}, bf16[64,1280]{1,0:T(8,128)(2,1)S(1)}, u32[]{:S(2)}, u32[]{:S(2)}) collective-permute-start(bf16[64,1280]{1,0:T(8,128)(2,1)S(1)} %get-tuple-element.90), channel_id=1, source_target_pairs={{0,1},{1,0},{2,3},{3,2},{4,5},{5,4},{6,7},{7,6},{8,9},{9,8},{10,11... | collective-permute-start | bytes 491528 | tf_op jit(solution)/shard_map/ppermute | solution.py:697
  44.9 6.8 %collective-permute-start.5 = (bf16[64,1024]{1,0:T(8,128)(2,1)S(1)}, bf16[64,1024]{1,0:T(8,128)(2,1)S(1)}, u32[]{:S(2)}, u32[]{:S(2)}) collective-permute-start(bf16[64,1024]{1,0:T(8,128)(2,1)S(1)} %get-tuple-element.104.refs_0_), channel_id=1, source_target_pairs={{0,4},{2,6},{4,0},{6,2},{1,5},{3,7},{5,1},{7,3},{8,12},{10,14},{12... | collective-permute-start | bytes 393224 | tf_op jit(solution)/shard_map/ppermute | solution.py:697
  44.9 6.8 %collective-permute-start.4 = (bf16[64,1024]{1,0:T(8,128)(2,1)S(1)}, bf16[64,1024]{1,0:T(8,128)(2,1)S(1)}, u32[]{:S(2)}, u32[]{:S(2)}) collective-permute-start(bf16[64,1024]{1,0:T(8,128)(2,1)S(1)} %get-tuple-element.104.refs_0_), channel_id=1, source_target_pairs={{0,2},{2,0},{4,6},{6,4},{1,3},{3,1},{5,7},{7,5},{8,10},{10,8},{12,... | collective-permute-start | bytes 393224 | tf_op jit(solution)/shard_map/ppermute | solution.py:697
  51.7 15.5 %all-to-all-start.2 = ((bf16[8,88,256]{2,1,0:T(8,128)(2,1)}), bf16[8,88,256]{2,1,0:T(8,128)(2,1)S(1)}, u32[]{:S(2)}, u32[]{:S(2)}) async-start(bf16[8,88,256]{2,1,0:T(8,128)(2,1)} %backward.1), calls=%async_computation.2 | async-start | bytes 720896 | tf_op jit(solution)/shard_map/all_to_all | solution.py:750
  55.3 9.8 %collective-permute-start.9 = (bf16[64,1536]{1,0:T(8,128)(2,1)S(1)}, bf16[64,1536]{1,0:T(8,128)(2,1)S(1)}, u32[]{:S(2)}, u32[]{:S(2)}) collective-permute-start(bf16[64,1536]{1,0:T(8,128)(2,1)S(1)} %collective-permute-done.3.refs_2_), channel_id=1, source_target_pairs={{0,1},{1,0},{2,3},{3,2},{4,5},{5,4},{6,7},{7,6},{8,9},{9,8},{10,11... | collective-permute-start | bytes 589832 | tf_op jit(solution)/shard_map/ppermute | solution.py:697
  56.3 2.4 %collective-permute-start.6 = (bf16[64,1024]{1,0:T(8,128)(2,1)S(1)}, bf16[64,1024]{1,0:T(8,128)(2,1)S(1)}, u32[]{:S(2)}, u32[]{:S(2)}) collective-permute-start(bf16[64,1024]{1,0:T(8,128)(2,1)S(1)} %get-tuple-element.104.refs_0_), channel_id=1, source_target_pairs={{0,8},{8,0},{1,9},{9,1},{2,10},{10,2},{3,11},{11,3},{4,12},{12,4},... | collective-permute-start | bytes 393224 | tf_op jit(solution)/shard_map/ppermute | solution.py:697
  56.4 2.3 %collective-permute-start.7 = (bf16[64,1024]{1,0:T(8,128)(2,1)S(1)}, bf16[64,1024]{1,0:T(8,128)(2,1)S(1)}, u32[]{:S(2)}, u32[]{:S(2)}) collective-permute-start(bf16[64,1024]{1,0:T(8,128)(2,1)S(1)} %collective-permute-done.4.refs_1_), channel_id=1, source_target_pairs={{0,8},{8,0},{1,9},{9,1},{2,10},{10,2},{3,11},{11,3},{4,12},{12,4},... | collective-permute-start | bytes 393224 | tf_op jit(solution)/shard_map/ppermute | solution.py:697
  56.9 8.2 %collective-permute-start.10 = (bf16[64,1024]{1,0:T(8,128)(2,1)S(1)}, bf16[64,1024]{1,0:T(8,128)(2,1)S(1)}, u32[]{:S(2)}, u32[]{:S(2)}) collective-permute-start(bf16[64,1024]{1,0:T(8,128)(2,1)S(1)} %collective-permute-done.5.refs_2_), channel_id=1, source_target_pairs={{0,2},{2,0},{4,6},{6,4},{1,3},{3,1},{5,7},{7,5},{8,10},{10,8},{12,... | collective-permute-start | bytes 393224 | tf_op jit(solution)/shard_map/ppermute | solution.py:697
  58.7 6.3 %collective-permute-start.8 = (bf16[64,1024]{1,0:T(8,128)(2,1)S(1)}, bf16[64,1024]{1,0:T(8,128)(2,1)S(1)}, u32[]{:S(2)}, u32[]{:S(2)}) collective-permute-start(bf16[64,1024]{1,0:T(8,128)(2,1)S(1)} %collective-permute-done.5.refs_2_), channel_id=1, source_target_pairs={{0,8},{8,0},{1,9},{9,1},{2,10},{10,2},{3,11},{11,3},{4,12},{12,4},... | collective-permute-start | bytes 393224 | tf_op jit(solution)/shard_map/ppermute | solution.py:697
  65.4 1.6 %collective-permute-start.12 = (bf16[128,1024]{1,0:T(8,128)(2,1)S(1)}, bf16[128,1024]{1,0:T(8,128)(2,1)S(1)}, u32[]{:S(2)}, u32[]{:S(2)}) collective-permute-start(bf16[128,1024]{1,0:T(8,128)(2,1)S(1)} %get-tuple-element.115), channel_id=1, source_target_pairs={{0,8},{8,0},{1,9},{9,1},{2,10},{10,2},{3,11},{11,3},{4,12},{12,4},... | collective-permute-start | bytes 786440 | tf_op jit(solution)/shard_map/ppermute | solution.py:697
  65.4 1.7 %collective-permute-start.11 = (bf16[64,1024]{1,0:T(8,128)(2,1)S(1)}, bf16[64,1024]{1,0:T(8,128)(2,1)S(1)}, u32[]{:S(2)}, u32[]{:S(2)}) collective-permute-start(bf16[64,1024]{1,0:T(8,128)(2,1)S(1)} %collective-permute-done.10.refs_3_), channel_id=1, source_target_pairs={{0,8},{8,0},{1,9},{9,1},{2,10},{10,2},{3,11},{11,3},{4,12},{12,4},... | collective-permute-start | bytes 393224 | tf_op jit(solution)/shard_map/ppermute | solution.py:697
  68.4 14.5 %all-to-all-start.3 = ((bf16[4,72,1024]{2,1,0:T(8,128)(2,1)}), bf16[4,72,1024]{2,1,0:T(8,128)(2,1)S(1)}, u32[]{:S(2)}, u32[]{:S(2)}) async-start(bf16[4,72,1024]{2,1,0:T(8,128)(2,1)} %up_products.1), calls=%async_computation.3 | async-start | bytes 1179648 | tf_op jit(solution)/shard_map/all_to_all | solution.py:761
  71.9 8.7 %collective-permute-start.13 = (bf16[32,1024]{1,0:T(8,128)(2,1)S(1)}, bf16[32,1024]{1,0:T(8,128)(2,1)S(1)}, u32[]{:S(2)}, u32[]{:S(2)}) collective-permute-start(bf16[32,1024]{1,0:T(8,128)(2,1)S(1)} %get-tuple-element.122), channel_id=1, source_target_pairs={{0,2},{2,0},{4,6},{6,4},{1,3},{3,1},{5,7},{7,5},{8,10},{10,8},{12,... | collective-permute-start | bytes 196616 | tf_op jit(solution)/shard_map/ppermute | solution.py:697
  74.5 6.2 %collective-permute-start.14 = (bf16[32,1024]{1,0:T(8,128)(2,1)S(1)}, bf16[32,1024]{1,0:T(8,128)(2,1)S(1)}, u32[]{:S(2)}, u32[]{:S(2)}) collective-permute-start(bf16[32,1024]{1,0:T(8,128)(2,1)S(1)} %get-tuple-element.123), channel_id=1, source_target_pairs={{0,4},{2,6},{4,0},{6,2},{1,5},{3,7},{5,1},{7,3},{8,12},{10,14},{12... | collective-permute-start | bytes 196616 | tf_op jit(solution)/shard_map/ppermute | solution.py:697
  76.8 6.1 %collective-permute-start.15 = (bf16[32,1024]{1,0:T(8,128)(2,1)S(1)}, bf16[32,1024]{1,0:T(8,128)(2,1)S(1)}, u32[]{:S(2)}, u32[]{:S(2)}) collective-permute-start(bf16[32,1024]{1,0:T(8,128)(2,1)S(1)} %get-tuple-element.124), channel_id=1, source_target_pairs={{0,6},{2,4},{4,2},{6,0},{1,7},{3,5},{5,3},{7,1},{8,14},{10,12},{12... | collective-permute-start | bytes 196616 | tf_op jit(solution)/shard_map/ppermute | solution.py:697

commit v7 on v6

--- a/solution.py
+++ b/solution.py
@@ -469,8 +469,13 @@
         lanes(i)
     for copy in copies:
         copy.wait()
-    input_grad = lax.dot_general(
-        lifted_ref[...], held_ref[...], (((1,), (1,)), ((), ())), preferred_element_type=jnp.float32
+    input_grad = jnp.transpose(
+        lax.dot_general(
+            held_ref[...],
+            lifted_ref[...],
+            (((1,), (1,)), ((), ())),
+            preferred_element_type=jnp.float32,
+        )
     )
     small_ref[taps : taps + 1, :] = jnp.sum(input_grad * one_ref[...], axis=0, keepdims=True)
     for i in range(width // 128):

time: 84.4 us -> 84.3 us (level)
  no operation moved by 1% of the time
where the time goes in v7:
time: 84.3 us; the launch traced here: 83.6 us
  starting transfers between devices  38.9 us (46%)
  Pallas kernels  22.1 us (26%)
  waiting for transfers between devices  21.1 us (25%)
  between operations  1.46 us (2%)
    ppermute x14, starting transfers between devices, flipped(): return lax.ppermute(rows, axis, [(i, i ^ bit) for i in range(size)])  14.9 us
    ppermute x14, waiting for transfers between devices, flipped(): return lax.ppermute(rows, axis, [(i, i ^ bit) for i in range(size)])  9.98 us
    all_to_all x1, starting transfers between devices, small_device(): qkv = lax.all_to_all(qkv, CTX, split_axis=0, concat_axis=0, tiled=True)  7.29 us
    all_to_all x1, waiting for transfers between devices, small_device(): lax.all_to_all(windows, CTX, split_axis=0, concat_axis=0, tiled=True)  5.26 us
    pallas_call x1, Pallas kernels, forward_part(): pl.pallas_call(forward_kernel, out_shape=(struct((frames, width), f32), s...  4.96 us
    pallas_call x1, Pallas kernels, back_part(): pl.pallas_call(back_kernel, out_shape=struct((width // 128, frames + 24,...  4.52 us
    all_to_all x1, starting transfers between devices, small_device(): lax.all_to_all(windows, CTX, split_axis=0, concat_axis=0, tiled=True)  4.49 us
    ppermute x1, waiting for transfers between devices, small_device(): after = lax.ppermute(low, CTX, down)  4.44 us
  transfers between devices with their start and end apart: 20, of which 9 were waited for; matrix products, arithmetic and copies ran while one was open for 0% of the time, Pallas kernels for 14%

profile of v7, /device:TPU:0, one launch (start us, length us, event | category | flops | bytes accessed | tf_op | source)
XLA Modules:
  0.0 83.6 jit_solution(857512427671503308)
XLA Ops:
  0.6 0.0 copy-start.1
  0.6 1.8 %split_heads.1 = bf16[8,64,384]{2,1,0:T(8,128)(2,1)} custom-call(bf16[64,3072]{1,0:T(8,128)(2,1)} %bitcast.20), custom_call_target="tpu_custom_call" | custom-call | tf_op jit(solution)/shard_map/split_heads/pallas_call | solution.py:111
  2.4 7.3 %all-to-all-start = ((bf16[8,64,384]{2,1,0:T(8,128)(2,1)}), bf16[8,64,384]{2,1,0:T(8,128)(2,1)S(1)}, u32[]{:S(2)}, u32[]{:S(2)}) async-start(bf16[8,64,384]{2,1,0:T(8,128)(2,1)} %split_heads.1), calls=%async_computation | async-start | bytes 786432 | tf_op jit(solution)/shard_map/all_to_all | solution.py:726
  9.7 0.9 %edges.1 = (bf16[48,1024]{1,0:T(8,128)(2,1)S(1)}, bf16[48,1024]{1,0:T(8,128)(2,1)S(1)}) custom-call(bf16[64,1024]{1,0:T(8,128)(2,1)} %bitcast.18, bf16[64,1024]{1,0:T(8,128)(2,1)} %bitcast.13), custom_call_target="tpu_custom_call" | custom-call | tf_op jit(solution)/shard_map/edges/pallas_call | solution.py:142
  10.6 3.9 %collective-permute-start = (bf16[48,1024]{1,0:T(8,128)(2,1)S(1)}, bf16[48,1024]{1,0:T(8,128)(2,1)S(1)}, u32[]{:S(2)}, u32[]{:S(2)}) collective-permute-start(bf16[48,1024]{1,0:T(8,128)(2,1)S(1)} %get-tuple-element.68), channel_id=1, source_target_pairs={{0,1},{1,2},{2,3},{3,4},{4,5},{5,6},{6,7},{8,9},{9,10},{10,11},{11... | collective-permute-start | bytes 294920 | tf_op jit(solution)/shard_map/ppermute | solution.py:730
  14.6 1.3 %collective-permute-start.1 = (bf16[48,1024]{1,0:T(8,128)(2,1)S(1)}, bf16[48,1024]{1,0:T(8,128)(2,1)S(1)}, u32[]{:S(2)}, u32[]{:S(2)}) collective-permute-start(bf16[48,1024]{1,0:T(8,128)(2,1)S(1)} %get-tuple-element.69), channel_id=1, source_target_pairs={{1,0},{2,1},{3,2},{4,3},{5,4},{6,5},{7,6},{9,8},{10,9},{11,10},{12... | collective-permute-start | bytes 294920 | tf_op jit(solution)/shard_map/ppermute | solution.py:731
  16.5 0.1 add_bitcast_fusion.scalar_ref
  16.6 0.6 collective-permute-done.low_ref
  17.1 4.4 %collective-permute-done.1.high_ref = bf16[48,1024]{1,0:T(8,128)(2,1)S(1)} collective-permute-done((bf16[48,1024]{1,0:T(8,128)(2,1)S(1)}, bf16[48,1024]{1,0:T(8,128)(2,1)S(1)}, u32[]{:S(2)}, u32[]{:S(2)}) %collective-permute-start.1) | collective-permute-done | bytes 98336 | tf_op jit(solution)/shard_map/ppermute | solution.py:731
  21.6 0.9 %all-to-all-done = bf16[8,64,384]{2,1,0:T(8,128)(2,1)S(1)} async-done(((bf16[8,64,384]{2,1,0:T(8,128)(2,1)}), bf16[8,64,384]{2,1,0:T(8,128)(2,1)S(1)}, u32[]{:S(2)}, u32[]{:S(2)}) %all-to-all-start) | async-done | bytes 393248 | tf_op jit(solution)/shard_map/all_to_all | solution.py:726
  22.5 1.7 %attend.1 = bf16[8,128,128]{2,1,0:T(8,128)(2,1)} custom-call(s32[1,2]{1,0:T(1,128)S(1)} %add_bitcast_fusion.scalar_ref, bf16[512,384]{1,0:T(8,128)(2,1)S(1)} %bitcast.12), custom_call_target="tpu_custom_call" | custom-call | tf_op jit(solution)/shard_map/attend/pallas_call | solution.py:193
  24.2 4.5 %all-to-all-start.1 = ((bf16[8,128,128]{2,1,0:T(8,128)(2,1)}), bf16[8,128,128]{2,1,0:T(8,128)(2,1)S(1)}, u32[]{:S(2)}, u32[]{:S(2)}) async-start(bf16[8,128,128]{2,1,0:T(8,128)(2,1)} %attend.1), calls=%async_computation.1 | async-start | bytes 524288 | tf_op jit(solution)/shard_map/all_to_all | solution.py:735
  28.7 0.0 copy-done.1
  28.7 0.0 copy-start
  28.7 0.0 copy-start.2
  28.7 0.0 copy-start.3
  28.7 2.9 %cotangent.1 = (bf16[64,256]{1,0:T(8,128)(2,1)S(1)}, bf16[64,256]{1,0:T(8,128)(2,1)S(1)}, bf16[64,256]{1,0:T(8,128)(2,1)S(1)}, bf16[64,256]{1,0:T(8,128)(2,1)S(1...) custom-call(s32[1,2]{1,0:T(1,128)S(1)} %add_bitcast_fusion.scalar_ref, bf16[64,1024]{1,0:T(8,128)(2,1)S(1)} %bitcast.14, ...), custom_call_target="tpu_custom_call" | custom-call | tf_op jit(solution)/shard_map/cotangent/pallas_call | solution.py:251
  31.6 5.3 %all-to-all-done.1.context_ref = bf16[8,128,128]{2,1,0:T(8,128)(2,1)S(1)} async-done(((bf16[8,128,128]{2,1,0:T(8,128)(2,1)}), bf16[8,128,128]{2,1,0:T(8,128)(2,1)S(1)}, u32[]{:S(2)}, u32[]{:S(2)}) %all-to-all-start.1) | async-done | bytes 262176 | tf_op jit(solution)/shard_map/all_to_all | solution.py:735
  36.9 0.0 copy-done
  36.9 0.0 copy-done.2
  36.9 0.0 copy-done.3
  36.9 5.0 %forward.1 = (f32[64,1024]{1,0:T(8,128)S(1)}, f32[64,1024]{1,0:T(8,128)S(1)}, bf16[64,1024]{1,0:T(8,128)(2,1)S(1)}, bf16[64,1024]{1,0:T(8,128)(2,1)S(1)}, f32[64...) custom-call(s32[1,2]{1,0:T(1,128)S(1)} %add_bitcast_fusion.scalar_re, ...), custom_call_target="tpu_custom_call" | custom-call | tf_op jit(solution)/shard_map/forward/pallas_call | solution.py:369
  41.9 1.6 %collective-permute-start.3 = (bf16[64,1536]{1,0:T(8,128)(2,1)S(1)}, bf16[64,1536]{1,0:T(8,128)(2,1)S(1)}, u32[]{:S(2)}, u32[]{:S(2)}) collective-permute-start(bf16[64,1536]{1,0:T(8,128)(2,1)S(1)} %get-tuple-element.91), channel_id=1, source_target_pairs={{0,16},{16,0},{1,17},{17,1},{2,18},{18,2},{3,19},{19,3},{4,20},{20... | collective-permute-start | bytes 589832 | tf_op jit(solution)/shard_map/ppermute | solution.py:702
  43.5 1.4 %collective-permute-start.2 = (bf16[64,1280]{1,0:T(8,128)(2,1)S(1)}, bf16[64,1280]{1,0:T(8,128)(2,1)S(1)}, u32[]{:S(2)}, u32[]{:S(2)}) collective-permute-start(bf16[64,1280]{1,0:T(8,128)(2,1)S(1)} %get-tuple-element.90), channel_id=1, source_target_pairs={{0,1},{1,0},{2,3},{3,2},{4,5},{5,4},{6,7},{7,6},{8,9},{9,8},{10,11... | collective-permute-start | bytes 491528 | tf_op jit(solution)/shard_map/ppermute | solution.py:702
  44.9 0.0 collective-permute-start.5
  44.9 1.9 %collective-permute-start.4 = (bf16[64,1024]{1,0:T(8,128)(2,1)S(1)}, bf16[64,1024]{1,0:T(8,128)(2,1)S(1)}, u32[]{:S(2)}, u32[]{:S(2)}) collective-permute-start(bf16[64,1024]{1,0:T(8,128)(2,1)S(1)} %get-tuple-element.104.refs_0_), channel_id=1, source_target_pairs={{0,2},{2,0},{4,6},{6,4},{1,3},{3,1},{5,7},{7,5},{8,10},{10,8},{12,... | collective-permute-start | bytes 393224 | tf_op jit(solution)/shard_map/ppermute | solution.py:702
  46.8 4.5 %backward.1 = bf16[8,88,256]{2,1,0:T(8,128)(2,1)} custom-call(s32[1,2]{1,0:T(1,128)S(1)} %add_bitcast_fusion.scalar_ref, f32[96,1024]{1,0:T(8,128)S(1)} %get-tuple-element.93.act_grad_ref, f32[64,1024]{1,0:T(8,128)S(1)} %get-tuple-element.94.one_ref, f32[64,1024]{1,0:T(8,128)S(1)} %get-tuple-element.95.linear_ref, ...), custom_call_target="tpu_custom_call" | custom-call | tf_op jit(solution)/shard_map/backward/pallas_call | solution.py:523
  51.3 0.4 collective-permute-done.5.refs_2_
  51.7 0.0 collective-permute-done.4.refs_1_
  51.7 0.0 collective-permute-done.2.refs_1_
  51.7 0.0 collective-permute-done.3.refs_2_
  51.7 3.5 %all-to-all-start.2 = ((bf16[8,88,256]{2,1,0:T(8,128)(2,1)}), bf16[8,88,256]{2,1,0:T(8,128)(2,1)S(1)}, u32[]{:S(2)}, u32[]{:S(2)}) async-start(bf16[8,88,256]{2,1,0:T(8,128)(2,1)} %backward.1), calls=%async_computation.2 | async-start | bytes 720896 | tf_op jit(solution)/shard_map/all_to_all | solution.py:755
  55.2 1.2 %collective-permute-start.9 = (bf16[64,1536]{1,0:T(8,128)(2,1)S(1)}, bf16[64,1536]{1,0:T(8,128)(2,1)S(1)}, u32[]{:S(2)}, u32[]{:S(2)}) collective-permute-start(bf16[64,1536]{1,0:T(8,128)(2,1)S(1)} %collective-permute-done.3.refs_2_), channel_id=1, source_target_pairs={{0,1},{1,0},{2,3},{3,2},{4,5},{5,4},{6,7},{7,6},{8,9},{9,8},{10,11... | collective-permute-start | bytes 589832 | tf_op jit(solution)/shard_map/ppermute | solution.py:702
  56.3 0.1 collective-permute-start.6
  56.4 0.4 collective-permute-start.7
  56.9 1.8 %collective-permute-start.10 = (bf16[64,1024]{1,0:T(8,128)(2,1)S(1)}, bf16[64,1024]{1,0:T(8,128)(2,1)S(1)}, u32[]{:S(2)}, u32[]{:S(2)}) collective-permute-start(bf16[64,1024]{1,0:T(8,128)(2,1)S(1)} %collective-permute-done.5.refs_2_), channel_id=1, source_target_pairs={{0,2},{2,0},{4,6},{6,4},{1,3},{3,1},{5,7},{7,5},{8,10},{10,8},{12,... | collective-permute-start | bytes 393224 | tf_op jit(solution)/shard_map/ppermute | solution.py:702
  58.7 0.0 collective-permute-start.8
  58.7 0.0 collective-permute-done.6.refs_4_
  58.7 0.0 collective-permute-done.7.refs_5_
  58.7 6.2 %collective-permute-done.10.refs_3_ = bf16[64,1024]{1,0:T(8,128)(2,1)S(1)} collective-permute-done((bf16[64,1024]{1,0:T(8,128)(2,1)S(1)}, bf16[64,1024]{1,0:T(8,128)(2,1)S(1)}, u32[]{:S(2)}, u32[]{:S(2)}) %collective-permute-start.10) | collective-permute-done | bytes 131104 | tf_op jit(solution)/shard_map/ppermute | solution.py:702
  64.9 0.0 collective-permute-done.8.refs_6_
  64.9 0.0 collective-permute-done.9.refs_3_
  64.9 0.3 down_products.1
  65.3 0.1 collective-permute-start.12
  65.3 0.5 collective-permute-start.11
  65.8 1.0 %collective-permute-done.12.other_ref = bf16[128,1024]{1,0:T(8,128)(2,1)S(1)} collective-permute-done((bf16[128,1024]{1,0:T(8,128)(2,1)S(1)}, bf16[128,1024]{1,0:T(8,128)(2,1)S(1)}, u32[]{:S(2)}, u32[]{:S(2)}) %collective-permute-start.12) | collective-permute-done | bytes 262176 | tf_op jit(solution)/shard_map/ppermute | solution.py:702
  66.9 0.1 down_shares.1
  67.0 0.1 collective-permute-done.11.refs_7_
  67.0 0.0 all-to-all-done.2.message_ref
  67.0 1.3 %up_products.1 = bf16[4,72,1024]{2,1,0:T(8,128)(2,1)} custom-call(bf16[8,88,256]{2,1,0:T(8,128)(2,1)S(1)} %all-to-all-done.2.message_ref, bf16[64,1024]{1,0:T(8,128)(2,1)S(1)} %get-tuple-element.104.refs_0_, bf16[64,1024]{1,0:T(8,128)(2,1)S(1)} %collective-permute-done.4.refs_1_, bf16[64,1024]{1,0:T(8,128)(2,1)S(1)} %collective-permute-done.5.refs_2_, ...), custom_call_target="tpu_custom_call" | custom-call | tf_op jit(solution)/shard_map/up_products/pallas_call | solution.py:574
  68.3 3.5 %all-to-all-start.3 = ((bf16[4,72,1024]{2,1,0:T(8,128)(2,1)}), bf16[4,72,1024]{2,1,0:T(8,128)(2,1)S(1)}, u32[]{:S(2)}, u32[]{:S(2)}) async-start(bf16[4,72,1024]{2,1,0:T(8,128)(2,1)} %up_products.1), calls=%async_computation.3 | async-start | bytes 1179648 | tf_op jit(solution)/shard_map/all_to_all | solution.py:766
  71.8 2.5 %collective-permute-start.13 = (bf16[32,1024]{1,0:T(8,128)(2,1)S(1)}, bf16[32,1024]{1,0:T(8,128)(2,1)S(1)}, u32[]{:S(2)}, u32[]{:S(2)}) collective-permute-start(bf16[32,1024]{1,0:T(8,128)(2,1)S(1)} %get-tuple-element.122), channel_id=1, source_target_pairs={{0,2},{2,0},{4,6},{6,4},{1,3},{3,1},{5,7},{7,5},{8,10},{10,8},{12,... | collective-permute-start | bytes 196616 | tf_op jit(solution)/shard_map/ppermute | solution.py:702
  74.4 2.3 %collective-permute-start.14 = (bf16[32,1024]{1,0:T(8,128)(2,1)S(1)}, bf16[32,1024]{1,0:T(8,128)(2,1)S(1)}, u32[]{:S(2)}, u32[]{:S(2)}) collective-permute-start(bf16[32,1024]{1,0:T(8,128)(2,1)S(1)} %get-tuple-element.123), channel_id=1, source_target_pairs={{0,4},{2,6},{4,0},{6,2},{1,5},{3,7},{5,1},{7,3},{8,12},{10,14},{12... | collective-permute-start | bytes 196616 | tf_op jit(solution)/shard_map/ppermute | solution.py:702
  76.7 1.1 %collective-permute-start.15 = (bf16[32,1024]{1,0:T(8,128)(2,1)S(1)}, bf16[32,1024]{1,0:T(8,128)(2,1)S(1)}, u32[]{:S(2)}, u32[]{:S(2)}) collective-permute-start(bf16[32,1024]{1,0:T(8,128)(2,1)S(1)} %get-tuple-element.124), channel_id=1, source_target_pairs={{0,6},{2,4},{4,2},{6,0},{1,7},{3,5},{5,3},{7,1},{8,14},{10,12},{12... | collective-permute-start | bytes 196616 | tf_op jit(solution)/shard_map/ppermute | solution.py:702
  77.8 2.7 %block_out.1 = bf16[64,1024]{1,0:T(8,128)(2,1)} custom-call(f32[64,1024]{1,0:T(8,128)S(1)} %get-tuple-element.84.hidden_ref, bf16[64,1024]{1,0:T(8,128)(2,1)S(1)} %get-tuple-element.85.activated_ref.act_ref, bf16[1024,1024]{1,0:T(8,128)(2,1)} %down_ref.1), custom_call_target="tpu_custom_call" | custom-call | tf_op jit(solution)/shard_map/block_out/pallas_call | solution.py:505
  80.5 0.0 collective-permute-done.13.refs_1_
  80.5 0.0 collective-permute-done.14.refs_2_
  80.5 2.3 %collective-permute-done.15.refs_3_ = bf16[32,1024]{1,0:T(8,128)(2,1)S(1)} collective-permute-done((bf16[32,1024]{1,0:T(8,128)(2,1)S(1)}, bf16[32,1024]{1,0:T(8,128)(2,1)S(1)}, u32[]{:S(2)}, u32[]{:S(2)}) %collective-permute-start.15) | collective-permute-done | bytes 65568 | tf_op jit(solution)/shard_map/ppermute | solution.py:702
  82.8 0.0 all-to-all-done.3.parts_ref
  82.8 0.8 sums.1
  (1 shorter events, 0.0 us)
Async XLA Ops:
  0.6 28.1 %copy-start.1 = (bf16[64,1,1024]{2,0,1:T(8,128)(2,1)S(1)}, bf16[64,1,1024]{2,0,1:T(8,128)(2,1)}, u32[]{:S(2)}) copy-start(bf16[64,1,1024]{2,0,1:T(8,128)(2,1)} %param.19) | copy-start | bytes 393220
  2.4 20.0 %all-to-all-start = ((bf16[8,64,384]{2,1,0:T(8,128)(2,1)}), bf16[8,64,384]{2,1,0:T(8,128)(2,1)S(1)}, u32[]{:S(2)}, u32[]{:S(2)}) async-start(bf16[8,64,384]{2,1,0:T(8,128)(2,1)} %split_heads.1), calls=%async_computation | async-start | bytes 786432 | tf_op jit(solution)/shard_map/all_to_all | solution.py:726
  10.6 6.5 %collective-permute-start = (bf16[48,1024]{1,0:T(8,128)(2,1)S(1)}, bf16[48,1024]{1,0:T(8,128)(2,1)S(1)}, u32[]{:S(2)}, u32[]{:S(2)}) collective-permute-start(bf16[48,1024]{1,0:T(8,128)(2,1)S(1)} %get-tuple-element.68), channel_id=1, source_target_pairs={{0,1},{1,2},{2,3},{3,4},{4,5},{5,6},{6,7},{8,9},{9,10},{10,11},{11... | collective-permute-start | bytes 294920 | tf_op jit(solution)/shard_map/ppermute | solution.py:730
  14.6 7.0 %collective-permute-start.1 = (bf16[48,1024]{1,0:T(8,128)(2,1)S(1)}, bf16[48,1024]{1,0:T(8,128)(2,1)S(1)}, u32[]{:S(2)}, u32[]{:S(2)}) collective-permute-start(bf16[48,1024]{1,0:T(8,128)(2,1)S(1)} %get-tuple-element.69), channel_id=1, source_target_pairs={{1,0},{2,1},{3,2},{4,3},{5,4},{6,5},{7,6},{9,8},{10,9},{11,10},{12... | collective-permute-start | bytes 294920 | tf_op jit(solution)/shard_map/ppermute | solution.py:731
  24.2 12.7 %all-to-all-start.1 = ((bf16[8,128,128]{2,1,0:T(8,128)(2,1)}), bf16[8,128,128]{2,1,0:T(8,128)(2,1)S(1)}, u32[]{:S(2)}, u32[]{:S(2)}) async-start(bf16[8,128,128]{2,1,0:T(8,128)(2,1)} %attend.1), calls=%async_computation.1 | async-start | bytes 524288 | tf_op jit(solution)/shard_map/all_to_all | solution.py:735
  28.7 8.2 %copy-start = (f32[31,1024]{1,0:T(8,128)S(1)}, f32[31,1024]{1,0:T(8,128)}, u32[]{:S(2)}) copy-start(f32[31,1024]{1,0:T(8,128)} %taps_ref.3) | copy-start | bytes 380932
  28.7 8.2 %copy-start.2 = (f32[1024]{0:T(1024)S(1)}, f32[1024]{0:T(1024)}, u32[]{:S(2)}) copy-start(f32[1024]{0:T(1024)} %param.16) | copy-start | bytes 12292
  28.7 8.2 %copy-start.3 = (f32[1024]{0:T(1024)S(1)}, f32[1024]{0:T(1024)}, u32[]{:S(2)}) copy-start(f32[1024]{0:T(1024)} %param.13) | copy-start | bytes 12292
  41.9 9.8 %collective-permute-start.3 = (bf16[64,1536]{1,0:T(8,128)(2,1)S(1)}, bf16[64,1536]{1,0:T(8,128)(2,1)S(1)}, u32[]{:S(2)}, u32[]{:S(2)}) collective-permute-start(bf16[64,1536]{1,0:T(8,128)(2,1)S(1)} %get-tuple-element.91), channel_id=1, source_target_pairs={{0,16},{16,0},{1,17},{17,1},{2,18},{18,2},{3,19},{19,3},{4,20},{20... | collective-permute-start | bytes 589832 | tf_op jit(solution)/shard_map/ppermute | solution.py:702
  43.5 8.2 %collective-permute-start.2 = (bf16[64,1280]{1,0:T(8,128)(2,1)S(1)}, bf16[64,1280]{1,0:T(8,128)(2,1)S(1)}, u32[]{:S(2)}, u32[]{:S(2)}) collective-permute-start(bf16[64,1280]{1,0:T(8,128)(2,1)S(1)} %get-tuple-element.90), channel_id=1, source_target_pairs={{0,1},{1,0},{2,3},{3,2},{4,5},{5,4},{6,7},{7,6},{8,9},{9,8},{10,11... | collective-permute-start | bytes 491528 | tf_op jit(solution)/shard_map/ppermute | solution.py:702
  44.9 6.8 %collective-permute-start.5 = (bf16[64,1024]{1,0:T(8,128)(2,1)S(1)}, bf16[64,1024]{1,0:T(8,128)(2,1)S(1)}, u32[]{:S(2)}, u32[]{:S(2)}) collective-permute-start(bf16[64,1024]{1,0:T(8,128)(2,1)S(1)} %get-tuple-element.104.refs_0_), channel_id=1, source_target_pairs={{0,4},{2,6},{4,0},{6,2},{1,5},{3,7},{5,1},{7,3},{8,12},{10,14},{12... | collective-permute-start | bytes 393224 | tf_op jit(solution)/shard_map/ppermute | solution.py:702
  44.9 6.8 %collective-permute-start.4 = (bf16[64,1024]{1,0:T(8,128)(2,1)S(1)}, bf16[64,1024]{1,0:T(8,128)(2,1)S(1)}, u32[]{:S(2)}, u32[]{:S(2)}) collective-permute-start(bf16[64,1024]{1,0:T(8,128)(2,1)S(1)} %get-tuple-element.104.refs_0_), channel_id=1, source_target_pairs={{0,2},{2,0},{4,6},{6,4},{1,3},{3,1},{5,7},{7,5},{8,10},{10,8},{12,... | collective-permute-start | bytes 393224 | tf_op jit(solution)/shard_map/ppermute | solution.py:702
  51.7 15.4 %all-to-all-start.2 = ((bf16[8,88,256]{2,1,0:T(8,128)(2,1)}), bf16[8,88,256]{2,1,0:T(8,128)(2,1)S(1)}, u32[]{:S(2)}, u32[]{:S(2)}) async-start(bf16[8,88,256]{2,1,0:T(8,128)(2,1)} %backward.1), calls=%async_computation.2 | async-start | bytes 720896 | tf_op jit(solution)/shard_map/all_to_all | solution.py:755
  55.2 9.8 %collective-permute-start.9 = (bf16[64,1536]{1,0:T(8,128)(2,1)S(1)}, bf16[64,1536]{1,0:T(8,128)(2,1)S(1)}, u32[]{:S(2)}, u32[]{:S(2)}) collective-permute-start(bf16[64,1536]{1,0:T(8,128)(2,1)S(1)} %collective-permute-done.3.refs_2_), channel_id=1, source_target_pairs={{0,1},{1,0},{2,3},{3,2},{4,5},{5,4},{6,7},{7,6},{8,9},{9,8},{10,11... | collective-permute-start | bytes 589832 | tf_op jit(solution)/shard_map/ppermute | solution.py:702
  56.3 2.4 %collective-permute-start.6 = (bf16[64,1024]{1,0:T(8,128)(2,1)S(1)}, bf16[64,1024]{1,0:T(8,128)(2,1)S(1)}, u32[]{:S(2)}, u32[]{:S(2)}) collective-permute-start(bf16[64,1024]{1,0:T(8,128)(2,1)S(1)} %get-tuple-element.104.refs_0_), channel_id=1, source_target_pairs={{0,8},{8,0},{1,9},{9,1},{2,10},{10,2},{3,11},{11,3},{4,12},{12,4},... | collective-permute-start | bytes 393224 | tf_op jit(solution)/shard_map/ppermute | solution.py:702
  56.4 2.3 %collective-permute-start.7 = (bf16[64,1024]{1,0:T(8,128)(2,1)S(1)}, bf16[64,1024]{1,0:T(8,128)(2,1)S(1)}, u32[]{:S(2)}, u32[]{:S(2)}) collective-permute-start(bf16[64,1024]{1,0:T(8,128)(2,1)S(1)} %collective-permute-done.4.refs_1_), channel_id=1, source_target_pairs={{0,8},{8,0},{1,9},{9,1},{2,10},{10,2},{3,11},{11,3},{4,12},{12,4},... | collective-permute-start | bytes 393224 | tf_op jit(solution)/shard_map/ppermute | solution.py:702
  56.9 8.1 %collective-permute-start.10 = (bf16[64,1024]{1,0:T(8,128)(2,1)S(1)}, bf16[64,1024]{1,0:T(8,128)(2,1)S(1)}, u32[]{:S(2)}, u32[]{:S(2)}) collective-permute-start(bf16[64,1024]{1,0:T(8,128)(2,1)S(1)} %collective-permute-done.5.refs_2_), channel_id=1, source_target_pairs={{0,2},{2,0},{4,6},{6,4},{1,3},{3,1},{5,7},{7,5},{8,10},{10,8},{12,... | collective-permute-start | bytes 393224 | tf_op jit(solution)/shard_map/ppermute | solution.py:702
  58.7 6.2 %collective-permute-start.8 = (bf16[64,1024]{1,0:T(8,128)(2,1)S(1)}, bf16[64,1024]{1,0:T(8,128)(2,1)S(1)}, u32[]{:S(2)}, u32[]{:S(2)}) collective-permute-start(bf16[64,1024]{1,0:T(8,128)(2,1)S(1)} %collective-permute-done.5.refs_2_), channel_id=1, source_target_pairs={{0,8},{8,0},{1,9},{9,1},{2,10},{10,2},{3,11},{11,3},{4,12},{12,4},... | collective-permute-start | bytes 393224 | tf_op jit(solution)/shard_map/ppermute | solution.py:702
  65.3 1.6 %collective-permute-start.12 = (bf16[128,1024]{1,0:T(8,128)(2,1)S(1)}, bf16[128,1024]{1,0:T(8,128)(2,1)S(1)}, u32[]{:S(2)}, u32[]{:S(2)}) collective-permute-start(bf16[128,1024]{1,0:T(8,128)(2,1)S(1)} %get-tuple-element.115), channel_id=1, source_target_pairs={{0,8},{8,0},{1,9},{9,1},{2,10},{10,2},{3,11},{11,3},{4,12},{12,4},... | collective-permute-start | bytes 786440 | tf_op jit(solution)/shard_map/ppermute | solution.py:702
  65.3 1.7 %collective-permute-start.11 = (bf16[64,1024]{1,0:T(8,128)(2,1)S(1)}, bf16[64,1024]{1,0:T(8,128)(2,1)S(1)}, u32[]{:S(2)}, u32[]{:S(2)}) collective-permute-start(bf16[64,1024]{1,0:T(8,128)(2,1)S(1)} %collective-permute-done.10.refs_3_), channel_id=1, source_target_pairs={{0,8},{8,0},{1,9},{9,1},{2,10},{10,2},{3,11},{11,3},{4,12},{12,4},... | collective-permute-start | bytes 393224 | tf_op jit(solution)/shard_map/ppermute | solution.py:702
  68.3 14.5 %all-to-all-start.3 = ((bf16[4,72,1024]{2,1,0:T(8,128)(2,1)}), bf16[4,72,1024]{2,1,0:T(8,128)(2,1)S(1)}, u32[]{:S(2)}, u32[]{:S(2)}) async-start(bf16[4,72,1024]{2,1,0:T(8,128)(2,1)} %up_products.1), calls=%async_computation.3 | async-start | bytes 1179648 | tf_op jit(solution)/shard_map/all_to_all | solution.py:766
  71.8 8.7 %collective-permute-start.13 = (bf16[32,1024]{1,0:T(8,128)(2,1)S(1)}, bf16[32,1024]{1,0:T(8,128)(2,1)S(1)}, u32[]{:S(2)}, u32[]{:S(2)}) collective-permute-start(bf16[32,1024]{1,0:T(8,128)(2,1)S(1)} %get-tuple-element.122), channel_id=1, source_target_pairs={{0,2},{2,0},{4,6},{6,4},{1,3},{3,1},{5,7},{7,5},{8,10},{10,8},{12,... | collective-permute-start | bytes 196616 | tf_op jit(solution)/shard_map/ppermute | solution.py:702
  74.4 6.2 %collective-permute-start.14 = (bf16[32,1024]{1,0:T(8,128)(2,1)S(1)}, bf16[32,1024]{1,0:T(8,128)(2,1)S(1)}, u32[]{:S(2)}, u32[]{:S(2)}) collective-permute-start(bf16[32,1024]{1,0:T(8,128)(2,1)S(1)} %get-tuple-element.123), channel_id=1, source_target_pairs={{0,4},{2,6},{4,0},{6,2},{1,5},{3,7},{5,1},{7,3},{8,12},{10,14},{12... | collective-permute-start | bytes 196616 | tf_op jit(solution)/shard_map/ppermute | solution.py:702
  76.7 6.1 %collective-permute-start.15 = (bf16[32,1024]{1,0:T(8,128)(2,1)S(1)}, bf16[32,1024]{1,0:T(8,128)(2,1)S(1)}, u32[]{:S(2)}, u32[]{:S(2)}) collective-permute-start(bf16[32,1024]{1,0:T(8,128)(2,1)S(1)} %get-tuple-element.124), channel_id=1, source_target_pairs={{0,6},{2,4},{4,2},{6,0},{1,7},{3,5},{5,3},{7,1},{8,14},{10,12},{12... | collective-permute-start | bytes 196616 | tf_op jit(solution)/shard_map/ppermute | solution.py:702
